TPU v7x, 256 devices: a whole 4x4x8 slice. The times are simulated.
256 devices in a mesh: row: 16 (over z_lo, x, core), col: 16 (over y, z_hi).
Axes of the slice: x: 4, y: 4, z: 8 (z_hi: 4, z_lo: 2; z = z_hi * 2 + z_lo), core: 2. Of those that a mesh axis runs over, the one named last changes fastest.
Arguments:
- gradient: bfloat16 [6144, 24576], P('row', 'col'), may hold values from -60 to 60
Outputs:
- update: bfloat16 [6144, 24576], P('row', 'col')
All inputs are finite; a program needn't handle non-finite values.
Results may differ from a plain program's by a relative error of at most 0.001.
The roundings to bfloat16 on the way count: a program that leaves them out, or rounds other values in their place, can miss the bound.
Values may be sent and summed in bfloat16 or wider, within the bound.
No kernel may reach another device: no remote copies, remote signals or barrier semaphores. Data moves between devices by JAX's collectives and lax.ppermute only.
A program may use at most 128 MiB of HBM per device.

v0:
```python
import jax
import jax.numpy as jnp
from jax import lax
from jax.experimental import pallas as pl
from jax.experimental.pallas import tpu as pltpu
from jax.sharding import PartitionSpec as P

BLOCK = 1536
ROWS = 384
LANE = 128
BLOCKS = BLOCK // LANE
BAND = 7
HALF = BLOCK // 2
RIGHT = 192
LEFT = 96

damping = 0.001
F32 = jnp.float32
BF16 = jnp.bfloat16
MIB = 1 << 20

SMEM = pl.BlockSpec(memory_space=pltpu.SMEM)
VMEM = pl.BlockSpec(memory_space=pltpu.VMEM)
ANY = pl.BlockSpec(memory_space=pl.ANY)


def params(mib):
    return pltpu.CompilerParams(vmem_limit_bytes=mib * MIB)


def cost(flops, moved):
    return pl.CostEstimate(flops=flops, bytes_accessed=moved, transcendentals=0)


def sds(shape, dtype):
    return jax.ShapeDtypeStruct(shape, dtype)


def hop(value, axis, mask):
    return lax.ppermute(value, axis, [(i, i ^ mask) for i in range(16)])


def folded(wide):
    rows, cols = wide.shape
    tall = jnp.sum(wide.reshape(rows // 8, 8, cols), axis=0)
    total = tall[:, :LANE]
    for start in range(LANE, cols, LANE):
        total = total + tall[:, start : start + LANE]
    return total


def squares(ref):
    total = jnp.zeros((8, LANE), F32)
    for start in range(0, ref.shape[0], 48):
        part = ref[start : start + 48, :].astype(F32)
        total = total + folded(part * part)
    return total


def nt(a, b):
    return lax.dot_general(a, b, (((1,), (1,)), ((), ())), preferred_element_type=F32)


def dealt(whole, outs, rows, place, first):
    for slot in range(4):
        start = pl.multiple_of(place[first + slot] * rows, 16)
        at = slot % 2 * rows
        outs[slot // 2][at : at + rows, :] = whole[pl.ds(start, rows), :]


def right_kernel(place, mine, other, keep, send, wide, whole, sems):
    copies = []
    for at, source in enumerate((mine, other)):
        rows = pl.ds(at * ROWS, ROWS)
        copies.append(pltpu.make_async_copy(source, wide.at[rows, pl.ds(0, BLOCK)], sems.at[2 * at]))
        copies.append(
            pltpu.make_async_copy(
                source.at[:, pl.ds(0, HALF)], wide.at[rows, pl.ds(BLOCK, HALF)], sems.at[2 * at + 1]
            )
        )
    for copy in copies:
        copy.start()
    for copy in copies:
        copy.wait()
    for pair in range(3):
        start = pl.multiple_of(place[0] * HALF + pair * 256, LANE)
        strip = wide[:, pl.ds(start, 1024)]
        gram = lax.dot_general(
            strip[:, :256], strip, (((0,), (0,)), ((), ())), preferred_element_type=F32
        ).astype(BF16)
        for half in range(2):
            at = pair * 256 + half * LANE
            whole[at : at + LANE, :] = gram[
                half * LANE : half * LANE + LANE, half * LANE : half * LANE + BAND * LANE
            ]
    dealt(whole, (keep, send), RIGHT, place, 1)


def right_gram(place, mine, other):
    return pl.pallas_call(
        right_kernel,
        out_shape=[sds((2 * RIGHT, BAND * LANE), BF16)] * 2,
        in_specs=[SMEM, ANY, ANY],
        out_specs=[VMEM] * 2,
        scratch_shapes=[
            pltpu.VMEM((2 * ROWS, BLOCK + HALF), BF16),
            pltpu.VMEM((HALF, BAND * LANE), BF16),
            pltpu.SemaphoreType.DMA((4,)),
        ],
        compiler_params=params(32),
        cost_estimate=cost(10**6, 10**4),
        name="right_gram",
    )(place, mine, other)


def own_kernel(place, mine, other, keep, send, square_out, whole):
    for at, source in enumerate((mine, other)):
        whole[:, at * ROWS : (at + 1) * ROWS] = nt(mine[...], source[...]).astype(BF16)
    dealt(whole, (keep, send), LEFT, place, 5)
    square_out[...] = squares(mine)


def own_gram(place, mine, other):
    half = sds((2 * LEFT, 2 * ROWS), BF16)
    return pl.pallas_call(
        own_kernel,
        out_shape=[half, half, sds((8, LANE), F32)],
        in_specs=[SMEM, VMEM, VMEM],
        out_specs=[VMEM] * 3,
        scratch_shapes=[pltpu.VMEM((ROWS, 2 * ROWS), BF16)],
        compiler_params=params(24),
        cost_estimate=cost(10**6, 10**4),
        name="own_gram",
    )(place, mine, other)


def cross_kernel(place, mine, other, near, keep, send, whole):
    upper = place[9]
    half = pl.ds(pl.multiple_of(upper * HALF, LANE), HALF)
    for at, source in enumerate((mine, other)):
        span = slice(at * ROWS, (at + 1) * ROWS)

        @pl.when(upper == 0)
        def _():
            whole[:, span] = nt(source[:, half], near[...]).astype(BF16)

        @pl.when(upper == 1)
        def _():
            whole[:, span] = nt(near[...], source[:, half]).astype(BF16)

    dealt(whole, (keep, send), LEFT, place, 5)


def cross_gram(place, mine, other, near):
    return pl.pallas_call(
        cross_kernel,
        out_shape=[sds((2 * LEFT, 2 * ROWS), BF16)] * 2,
        in_specs=[SMEM] + [VMEM] * 3,
        out_specs=[VMEM] * 2,
        scratch_shapes=[pltpu.VMEM((ROWS, 2 * ROWS), BF16)],
        compiler_params=params(24),
        cost_estimate=cost(10**6, 10**4),
        name="cross_gram",
    )(place, mine, other, near)


def left_rows_kernel(place, low, high, rows_out, square_out, cross):
    for slot in range(4):
        rows = pl.ds(pl.multiple_of(place[5 + slot] * LEFT, 16), LEFT)
        span = slice(slot % 2 * LEFT, slot % 2 * LEFT + LEFT)
        rows_out[rows, : 2 * ROWS] = (low, high)[slot // 2][span, : 2 * ROWS]
        cross[rows, :] = (low, high)[slot // 2][span, 2 * ROWS :]

    @pl.when(place[9] == 0)
    def _():
        rows_out[:, 2 * ROWS :] = cross[...]

    @pl.when(place[9] == 1)
    def _():
        for at in range(2):
            part = cross[:, at * ROWS : (at + 1) * ROWS].astype(F32).T
            rows_out[:, (2 + at) * ROWS : (3 + at) * ROWS] = part.astype(BF16)

    own = rows_out[:, :ROWS].astype(F32)
    shape = (ROWS, ROWS)
    eye = lax.broadcasted_iota(jnp.int32, shape, 0) == lax.broadcasted_iota(jnp.int32, shape, 1)
    own = own + jnp.where(eye, damping, 0.0)
    square_out[...] = folded(own * own) + squares(rows_out.at[:, pl.ds(ROWS, BLOCK - ROWS)])


def left_rows(place, parts):
    return pl.pallas_call(
        left_rows_kernel,
        out_shape=[sds((ROWS, BLOCK), BF16), sds((8, LANE), F32)],
        in_specs=[SMEM] + [VMEM] * 2,
        out_specs=[VMEM] * 2,
        scratch_shapes=[pltpu.VMEM((ROWS, 2 * ROWS), BF16)],
        compiler_params=params(24),
        cost_estimate=cost(10**6, 2 * 10**6),
        name="left_rows",
    )(place, *parts)


def scale_of(total):
    total = jnp.sum(total, axis=1, keepdims=True)
    total = jnp.sum(total, axis=0, keepdims=True)
    return jnp.sqrt(jnp.broadcast_to(total, (1, LANE)))


def widened(row, width):
    return jnp.concatenate([row] * (width // LANE), axis=1)


def root_kernel(place, *refs):
    parts, (root, packed, sems) = refs[:4], refs[4:]
    core = place[0]
    copies = []
    for side in range(2):
        for slot in range(4):
            turned = slot if side == 0 or slot in (0, 3) else 3 - slot
            start = pl.multiple_of((core ^ side) * HALF + place[1 + turned] * RIGHT, 16)
            copies.append(
                pltpu.make_async_copy(
                    parts[2 * side + slot // 2].at[pl.ds(slot % 2 * RIGHT, RIGHT), :],
                    packed.at[pl.ds(start, RIGHT), :],
                    sems.at[4 * side + slot],
                )
            )
    for copy in copies:
        copy.start()
    for copy in copies:
        copy.wait()
    shape = (LANE, LANE)
    eye = lax.broadcasted_iota(jnp.int32, shape, 0) == lax.broadcasted_iota(jnp.int32, shape, 1)
    total = jnp.zeros((8, LANE), F32)
    for row in range(BLOCKS):
        strip = packed[row * LANE : (row + 1) * LANE, :].astype(F32)
        head = strip[:, :LANE] + jnp.where(eye, damping, 0.0)
        tail = strip[:, 6 * LANE :]
        middle = strip[:, LANE : 6 * LANE]
        total = total + folded(head * head) + folded(tail * tail) + 2.0 * folded(middle * middle)
    scale = scale_of(total)
    factor = 0.25 / jnp.sqrt(jnp.sqrt(scale))
    inverse = 1.0 / scale
    for row in range(BLOCKS):
        for apart in range(BAND):
            part = packed[row * LANE : (row + 1) * LANE, apart * LANE : (apart + 1) * LANE]
            part = part.astype(F32)
            if apart == 0:
                part = jnp.where(eye, 5.0 - (part + damping) * inverse, -part * inverse)
                part = part * factor
            else:
                part = (-part * inverse) * factor
            col = (row + apart) % BLOCKS
            root[row * LANE : (row + 1) * LANE, col * LANE : (col + 1) * LANE] = part.astype(BF16)
            if 0 < apart < 6:
                root[col * LANE : (col + 1) * LANE, row * LANE : (row + 1) * LANE] = part.T.astype(BF16)


def right_root(place, parts):
    return pl.pallas_call(
        root_kernel,
        out_shape=sds((BLOCK, BLOCK), BF16),
        in_specs=[SMEM] + [ANY] * 4,
        out_specs=VMEM,
        scratch_shapes=[pltpu.VMEM((BLOCK, BAND * LANE), BF16), pltpu.SemaphoreType.DMA((8,))],
        compiler_params=params(24),
        cost_estimate=cost(10**7, 8 * 10**6),
        name="right_root",
    )(place, *parts)


def product_kernel(tile, root, out):
    for start in range(0, BLOCK, 512):
        out[:, start : start + 512] = jnp.dot(
            tile[...], root[:, start : start + 512], preferred_element_type=F32
        ).astype(BF16)


def near_product_kernel(place, first, second, root, out):
    upper = place[9]
    top = pl.ds(pl.multiple_of(upper * HALF, 16), HALF)
    rest = pl.ds(pl.multiple_of((1 - upper) * HALF, 16), HALF)
    for start in range(0, BLOCK, 512):
        span = slice(start, start + 512)
        part = jnp.dot(first[...], root[top, span], preferred_element_type=F32)
        part = part + jnp.dot(second[...], root[rest, span], preferred_element_type=F32)
        out[:, span] = part.astype(BF16)


def product(root, tile, *more):
    near = [tile, *more]
    return pl.pallas_call(
        near_product_kernel if more else product_kernel,
        out_shape=sds((ROWS, BLOCK), BF16),
        in_specs=([SMEM] if more else []) + [VMEM] * (len(near) - 1 if more else len(near)) + [VMEM],
        out_specs=VMEM,
        compiler_params=params(24),
        cost_estimate=cost(18 * 10**8, 7 * 10**6),
        name="product",
    )(*near, root)


def precond_kernel(a, b, c, d, rows, p0, p1, p2, p3, grad, out, square_out, root):
    scale = scale_of((a[...] + b[...]) + (c[...] + d[...]))
    factor = 0.25 / jnp.sqrt(jnp.sqrt(scale))
    inverse = 1.0 / scale
    shape = (ROWS, ROWS)
    eye = lax.broadcasted_iota(jnp.int32, shape, 0) == lax.broadcasted_iota(jnp.int32, shape, 1)
    inverse, factor = widened(inverse, ROWS), widened(factor, ROWS)
    own = rows[:, :ROWS].astype(F32)
    own = jnp.where(eye, 5.0 - (own + damping) * inverse, -own * inverse) * factor
    root[:, :ROWS] = own.astype(BF16)
    for start in range(ROWS, BLOCK, ROWS):
        part = rows[:, start : start + ROWS].astype(F32)
        root[:, start : start + ROWS] = ((-part * inverse) * factor).astype(BF16)
    total = jnp.zeros((8, LANE), F32)
    for start in range(0, BLOCK, 256):
        part = jnp.dot(root[:, :ROWS], p0[:, start : start + 256], preferred_element_type=F32)
        for at, tile in ((1, p1), (2, p2), (3, p3)):
            part = part + jnp.dot(
                root[:, at * ROWS : (at + 1) * ROWS],
                tile[:, start : start + 256],
                preferred_element_type=F32,
            )
        out[:, start : start + 256] = part
        total = total + folded(part * part)
    square_out[:8, :] = total
    square_out[8:, :] = grad[...]


def precond(totals, rows, tiles, grad):
    return pl.pallas_call(
        precond_kernel,
        out_shape=[sds((ROWS, BLOCK), F32), sds((16, LANE), F32)],
        in_specs=[VMEM] * 10,
        out_specs=[VMEM] * 2,
        scratch_shapes=[pltpu.VMEM((ROWS, BLOCK), BF16)],
        compiler_params=params(40),
        cost_estimate=cost(18 * 10**8, 8 * 10**6),
        name="precond",
    )(*totals, rows, *tiles, grad)


def graft_kernel(a, b, c, d, value, out):
    total = (a[...] + b[...]) + (c[...] + d[...])
    pre = jnp.sum(jnp.sum(total[:8, :], axis=1, keepdims=True), axis=0, keepdims=True)
    factor = scale_of(total[8:, :]) / jnp.sqrt(jnp.broadcast_to(pre, (1, LANE)) + 1e-06)
    out[...] = (value[...] * widened(factor, BLOCK)).astype(BF16)


def graft(totals, value):
    step = 96
    small = pl.BlockSpec((16, LANE), lambda i: (0, 0))
    wide = pl.BlockSpec((step, BLOCK), lambda i: (i, 0))
    return pl.pallas_call(
        graft_kernel,
        grid=(ROWS // step,),
        out_shape=sds((ROWS, BLOCK), BF16),
        in_specs=[small] * 4 + [wide],
        out_specs=wide,
        compiler_params=params(24),
        cost_estimate=cost(10**6, 4 * 10**6),
        name="graft",
    )(*totals, value)


def total_of(a, b):
    return a.astype(F32) + b.astype(F32)


CORE, NEAR, FAR, ACROSS = 1, 2, 6, 8
ROUND = ((FAR, ACROSS), (ACROSS, FAR))
UP = ((4, 12), (12, 4))
DEEP = ((1, 3), (3, 1))


def turned(value, masks, at):
    pairs = []
    for device in range(256):
        mask = masks[device // 16 % 2][at]
        mask = mask * 16 if masks is ROUND else mask
        pairs.append((device, device ^ mask))
    return lax.ppermute(value, ("row", "col"), pairs)


def after(value, *tokens):
    return lax.optimization_barrier((value, tokens))[0]


def spread(value):
    return [value] + [hop(value, "row", mask) for mask in (CORE, NEAR, CORE | NEAR)]


def right_steps(keep, send):
    tokens = yield
    came = turned(after(send, *tokens), ROUND, 0)
    total = total_of(keep, came)
    tokens = yield came
    came = turned(after(total[RIGHT:].astype(BF16), *tokens), ROUND, 1)
    mine = total_of(total[:RIGHT], came).astype(BF16)
    tokens = yield came
    came = hop(after(mine, *tokens), "row", NEAR)
    mine = total_of(mine, came).astype(BF16)
    tokens = yield came
    came = turned(after(mine, *tokens), ROUND, 1)
    low = jnp.concatenate([mine, came], axis=0)
    tokens = yield came
    low = after(low, *tokens)
    high = turned(low, ROUND, 0)
    low_other = hop(low, "row", CORE)
    tokens = yield high
    high_other = hop(after(high, *tokens), "row", CORE)
    yield high_other
    yield [low, high, low_other, high_other]


def scatter_steps(keep, send):
    tokens = yield
    came = turned(after(send, *tokens), UP, 0)
    total = total_of(keep, came)
    tokens = yield came
    came = turned(after(total[LEFT:].astype(BF16), *tokens), UP, 1)
    yield came
    yield total_of(total[:LEFT], came).astype(BF16)


def deep_steps(mine):
    for at in range(2):
        tokens = yield
        came = turned(after(mine, *tokens), DEEP, at)
        mine = total_of(mine, came).astype(BF16)
        yield came
    yield mine


def pair_step(mine, tokens):
    mine = after(mine, *tokens)
    near = hop(mine, "row", NEAR)
    core = hop(mine[:, ROWS:], "row", CORE)
    first = total_of(mine[:, :ROWS], near[:, :ROWS]).astype(BF16)
    second = total_of(core, near[:, ROWS:]).astype(BF16)
    return near, jnp.concatenate([first, second], axis=1)


def gather_steps(mine):
    tokens = yield
    came = turned(after(mine, *tokens), UP, 1)
    low = jnp.concatenate([mine, came], axis=0)
    tokens = yield came
    high = turned(after(low, *tokens), UP, 0)
    yield high
    yield [low, high]


def begun(chain):
    next(chain)
    return chain


def local(gradient):
    row, col = lax.axis_index("row"), lax.axis_index("col")
    core, x, z_low = row % 2, row // 2 % 4, row // 8
    ring, y, upper = x // 2 * 2 + z_low, col // 4, x % 2
    rights = [ring, ring ^ (1 + core), ring ^ (2 - core), ring ^ 3]
    lefts = [y, y ^ (3 - 2 * core), y ^ (1 + 2 * core), y ^ 2]
    place = jnp.stack([core] + rights + lefts + [upper]).astype(jnp.int32)
    other = hop(gradient, "row", CORE)
    near = hop(lax.dynamic_slice(gradient, (0, (1 - upper) * HALF), (ROWS, HALF)), "row", NEAR)
    rights = begun(right_steps(*right_gram(place, gradient, other)))
    keep, send, grad = own_gram(place, gradient, other)
    owns = begun(scatter_steps(keep, send))
    r1, o1 = rights.send([]), owns.send([])
    near = after(near, send)
    crosses = begun(scatter_steps(*cross_gram(place, gradient, other, near)))
    c1 = crosses.send([o1])
    o2 = owns.send([])
    r2 = rights.send([])
    c2 = crosses.send([o2])
    r3 = rights.send([])
    own, cross = next(owns), next(crosses)
    deep = begun(deep_steps(jnp.concatenate([own, cross], axis=1)))
    c3 = deep.send([r2])
    r4 = rights.send([c3])
    next(deep)
    c4 = deep.send([r3])
    both = next(deep)
    r5 = rights.send([c4])
    c5, cross = pair_step(both[:, 2 * ROWS :], [r4])
    gather = begun(gather_steps(jnp.concatenate([both[:, : 2 * ROWS], cross], axis=1)))
    c6 = gather.send([r5])
    r6 = rights.send([])
    c7 = gather.send([r6])
    parts, sides = next(rights), next(gather)
    late = lax.dynamic_slice(after(gradient, r3), (0, upper * HALF), (ROWS, HALF))
    near_late = hop(late, "row", NEAR)
    far = hop(near, "row", CORE)
    far_late = hop(near_late, "row", CORE)
    rows, square = left_rows(place, sides)
    totals = spread(square)
    root = right_root(place, parts)
    tiles = [
        product(root, gradient),
        product(root, other),
        product(root, place, near, near_late),
        product(root, place, far, far_late),
    ]
    value, square = precond(totals, rows, tiles, grad)
    return graft(spread(square), value)


def solution(mesh):
    return jax.shard_map(
        local, mesh=mesh, in_specs=(P("row", "col"),), out_specs=P("row", "col"), check_vma=False
    )
```

profile of v0, /device:TPU:1, one launch (start us, length us, event | category | flops | bytes accessed | tf_op | source)
XLA Modules:
  0.0 111.3 jit_solution(3031519025695599889)
XLA Ops:
  0.0 3.2 %collective-permute-start = (bf16[384,1536]{1,0:T(8,128)(2,1)}, bf16[384,1536]{1,0:T(8,128)(2,1)S(1)}, u32[]{:S(2)}, u32[]{:S(2)}) collective-permute-start(bf16[384,1536]{1,0:T(8,128)(2,1)} %tile.1), channel_id=1, source_target_pairs={{0,16},{16,0},{32,48},{48,32},{64,80},{80,64},{96,112},{112,96},{1... | collective-permute-start | bytes 3538952 | tf_op jit(solution)/shard_map/ppermute | solution.py:40
  3.2 1.9 %constant_dynamic-slice_fusion.1 = bf16[384,768]{1,0:T(8,128)(2,1)} fusion(bf16[384,1536]{1,0:T(8,128)(2,1)} %tile.1, s32[]{:T(128)S(6)} %select_n.41), kind=kLoop, calls=%fused_computation.22 | loop fusion | bytes 1179652 | tf_op jit(solution)/shard_map/dynamic_slice | solution.py:469
  5.2 0.7 collective-permute-done.other.tile
  5.9 2.3 %right_gram.1 = (bf16[384,896]{1,0:T(8,128)(2,1)S(1)}, bf16[384,896]{1,0:T(8,128)(2,1)S(1)}) custom-call(s32[10]{0:T(128)S(1)} %stack.43.place, bf16[384,1536]{1,0:T(8,128)(2,1)S(1)} %copy-done, bf16[384,1536]{1,0:T(8,128)(2,1)S(1)} %collective-permute-done.other.tile), custom_call_target="tpu_custom_call" | custom-call | flops 1000000 | bytes 10000 | tf_op jit(solution)/shard_map/right_gram/pallas_call | solution.py:100
  8.3 0.5 collective-permute-start.6
  8.8 2.0 %own_gram.1 = (bf16[192,768]{1,0:T(8,128)(2,1)S(1)}, bf16[192,768]{1,0:T(8,128)(2,1)S(1)}, f32[8,128]{1,0:T(8,128)S(1)}) custom-call(s32[10]{0:T(128)S(1)} %stack.43.place, bf16[384,1536]{1,0:T(8,128)(2,1)S(1)} %copy-done, bf16[384,1536]{1,0:T(8,128)(2,1)S(1)} %collective-permute-done.other.tile), custom_call_target="tpu_custom_call" | custom-call | flops 1000000 | bytes 10000 | tf_op jit(solution)/shard_map/own_gram/pallas_call | solution.py:125
  10.8 2.8 %collective-permute-start.1 = (bf16[192,768]{1,0:T(8,128)(2,1)S(1)}, bf16[192,768]{1,0:T(8,128)(2,1)S(1)}, u32[]{:S(2)}, u32[]{:S(2)}) collective-permute-start(bf16[192,768]{1,0:T(8,128)(2,1)S(1)} %get-tuple-element.28), channel_id=1, source_target_pairs={{0,4},{1,5},{2,6},{3,7},{4,0},{5,1},{6,2},{7,3},{8,12},{9,13},{10,... | collective-permute-start | bytes 884744 | tf_op jit(solution)/shard_map/ppermute | solution.py:384
  13.6 6.6 %collective-permute-done.3.near.first = bf16[384,768]{1,0:T(8,128)(2,1)S(1)} collective-permute-done((bf16[384,768]{1,0:T(8,128)(2,1)}, bf16[384,768]{1,0:T(8,128)(2,1)S(1)}, u32[]{:S(2)}, u32[]{:S(2)}) %collective-permute-start.3) | collective-permute-done | bytes 589856 | tf_op jit(solution)/shard_map/ppermute | solution.py:40
  20.3 1.6 %cross_gram.1 = (bf16[192,768]{1,0:T(8,128)(2,1)S(1)}, bf16[192,768]{1,0:T(8,128)(2,1)S(1)}) custom-call(s32[10]{0:T(128)S(1)} %stack.43.place, bf16[384,1536]{1,0:T(8,128)(2,1)S(1)} %copy-done, bf16[384,1536]{1,0:T(8,128)(2,1)S(1)} %collective-permute-done.other.tile, bf16[384,768]{1,0:T(8,128)(2,1)S(1)} %collective-permute-done.3.near.first), custom_call_target="tpu_custom_call" | custom-call | flops 1000000 | bytes 10000 | tf_op jit(solution)/shard_map/cross_gram/pallas_call | solution.py:155
  22.1 1.5 %collective-permute-start.4 = (bf16[192,768]{1,0:T(8,128)(2,1)S(1)}, bf16[192,768]{1,0:T(8,128)(2,1)S(1)}, u32[]{:S(2)}, u32[]{:S(2)}) collective-permute-start(bf16[192,768]{1,0:T(8,128)(2,1)S(1)} %get-tuple-element.32), channel_id=1, source_target_pairs={{0,4},{1,5},{2,6},{3,7},{4,0},{5,1},{6,2},{7,3},{8,12},{9,13},{10,... | collective-permute-start | bytes 884744 | tf_op jit(solution)/shard_map/ppermute | solution.py:384
  23.5 0.1 convert_add_fusion
  23.7 2.6 %collective-permute-start.7 = (bf16[192,896]{1,0:T(8,128)(2,1)S(1)}, bf16[192,896]{1,0:T(8,128)(2,1)S(1)}, u32[]{:S(2)}, u32[]{:S(2)}) collective-permute-start(bf16[192,896]{1,0:T(8,128)(2,1)S(1)} %slice.76), channel_id=1, source_target_pairs={{0,128},{1,129},{2,130},{3,131},{4,132},{5,133},{6,134},{7,135},{8... | collective-permute-start | bytes 1032200 | tf_op jit(solution)/shard_map/ppermute | solution.py:384
  26.3 4.2 %collective-permute-done.4 = bf16[192,768]{1,0:T(8,128)(2,1)S(1)} collective-permute-done((bf16[192,768]{1,0:T(8,128)(2,1)S(1)}, bf16[192,768]{1,0:T(8,128)(2,1)S(1)}, u32[]{:S(2)}, u32[]{:S(2)}) %collective-permute-start.4) | collective-permute-done | bytes 294944 | tf_op jit(solution)/shard_map/ppermute | solution.py:384
  30.7 0.4 collective-permute-done.7
  31.2 0.4 collective-permute-start.9
  31.6 3.1 %collective-permute-done.5 = bf16[96,768]{1,0:T(8,128)(2,1)S(1)} collective-permute-done((bf16[96,768]{1,0:T(8,128)(2,1)S(1)}, bf16[96,768]{1,0:T(8,128)(2,1)S(1)}, u32[]{:S(2)}, u32[]{:S(2)}) %collective-permute-start.5) | collective-permute-done | bytes 147488 | tf_op jit(solution)/shard_map/ppermute | solution.py:384
  34.7 5.6 %collective-permute-start.8 = (bf16[96,1536]{1,0:T(8,128)(2,1)S(1)}, bf16[96,1536]{1,0:T(8,128)(2,1)S(1)}, u32[]{:S(2)}, u32[]{:S(2)}) collective-permute-start(bf16[96,1536]{1,0:T(8,128)(2,1)S(1)} %pad_maximum_fusion.2), channel_id=1, source_target_pairs={{0,1},{1,0},{2,3},{3,2},{4,5},{5,4},{6,7},{7,6},{8,9},{9,8},{10,11... | collective-permute-start | bytes 884744 | tf_op jit(solution)/shard_map/ppermute | solution.py:384
  40.4 6.7 %collective-permute-done.8 = bf16[96,1536]{1,0:T(8,128)(2,1)S(1)} collective-permute-done((bf16[96,1536]{1,0:T(8,128)(2,1)S(1)}, bf16[96,1536]{1,0:T(8,128)(2,1)S(1)}, u32[]{:S(2)}, u32[]{:S(2)}) %collective-permute-start.8) | collective-permute-done | bytes 294944 | tf_op jit(solution)/shard_map/ppermute | solution.py:384
  47.1 2.5 %collective-permute-start.11 = (bf16[192,896]{1,0:T(8,128)(2,1)S(1)}, bf16[192,896]{1,0:T(8,128)(2,1)S(1)}, u32[]{:S(2)}, u32[]{:S(2)}) collective-permute-start(bf16[192,896]{1,0:T(8,128)(2,1)S(1)} %add_convert_fusion), channel_id=1, source_target_pairs={{0,128},{1,129},{2,130},{3,131},{4,132},{5,133},{6,134},{7,135},{8... | collective-permute-start | bytes 1032200 | tf_op jit(solution)/shard_map/ppermute | solution.py:384
  49.7 1.8 %collective-permute-start.10 = (bf16[96,1536]{1,0:T(8,128)(2,1)S(1)}, bf16[96,1536]{1,0:T(8,128)(2,1)S(1)}, u32[]{:S(2)}, u32[]{:S(2)}) collective-permute-start(bf16[96,1536]{1,0:T(8,128)(2,1)S(1)} %add_convert_fusion.2), channel_id=1, source_target_pairs={{0,3},{1,2},{2,1},{3,0},{4,7},{5,6},{6,5},{7,4},{8,11},{9,10},{10,... | collective-permute-start | bytes 884744 | tf_op jit(solution)/shard_map/ppermute | solution.py:384
  51.5 2.9 %collective-permute-done.11 = bf16[192,896]{1,0:T(8,128)(2,1)S(1)} collective-permute-done((bf16[192,896]{1,0:T(8,128)(2,1)S(1)}, bf16[192,896]{1,0:T(8,128)(2,1)S(1)}, u32[]{:S(2)}, u32[]{:S(2)}) %collective-permute-start.11) | collective-permute-done | bytes 344096 | tf_op jit(solution)/shard_map/ppermute | solution.py:384
  54.5 6.0 %collective-permute-done.10 = bf16[96,1536]{1,0:T(8,128)(2,1)S(1)} collective-permute-done((bf16[96,1536]{1,0:T(8,128)(2,1)S(1)}, bf16[96,1536]{1,0:T(8,128)(2,1)S(1)}, u32[]{:S(2)}, u32[]{:S(2)}) %collective-permute-start.10) | collective-permute-done | bytes 294944 | tf_op jit(solution)/shard_map/ppermute | solution.py:384
  60.6 3.2 %collective-permute-start.14 = (bf16[384,896]{1,0:T(8,128)(2,1)S(1)}, bf16[384,896]{1,0:T(8,128)(2,1)}, u32[]{:S(2)}, u32[]{:S(2)}) collective-permute-start(bf16[384,896]{1,0:T(8,128)(2,1)S(1)} %pad_maximum_fusion.refs_0_), channel_id=1, source_target_pairs={{0,96},{1,97},{2,98},{3,99},{4,100},{5,101},{6,102},{7,103},{8,104... | collective-permute-start | bytes 2064392 | tf_op jit(solution)/shard_map/ppermute | solution.py:384
  63.9 0.3 collective-permute-start.12
  64.2 4.7 %collective-permute-start.13 = (bf16[96,384]{1,0:T(8,128)(2,1)S(1)}, bf16[96,384]{1,0:T(8,128)(2,1)S(1)}, u32[]{:S(2)}, u32[]{:S(2)}) collective-permute-start(bf16[96,384]{1,0:T(8,128)(2,1)S(1)} %slice.49), channel_id=1, source_target_pairs={{0,16},{16,0},{32,48},{48,32},{64,80},{80,64},{96,112},{112,96},{1... | collective-permute-start | bytes 221192 | tf_op jit(solution)/shard_map/ppermute | solution.py:40
  68.9 1.7 %collective-permute-start.22 = (bf16[384,768]{1,0:T(8,128)(2,1)S(1)}, bf16[384,768]{1,0:T(8,128)(2,1)S(1)}, u32[]{:S(2)}, u32[]{:S(2)}) collective-permute-start(bf16[384,768]{1,0:T(8,128)(2,1)S(1)} %constant_dynamic-slice_fusion), channel_id=1, source_target_pairs={{0,32},{16,48},{32,0},{48,16},{64,96},{80,112},{96,64},{112,80},{1... | collective-permute-start | bytes 1769480 | tf_op jit(solution)/shard_map/ppermute | solution.py:40
  70.6 0.3 collective-permute-start.21
  71.0 1.5 %collective-permute-done.14.refs_1_ = bf16[384,896]{1,0:T(8,128)(2,1)} collective-permute-done((bf16[384,896]{1,0:T(8,128)(2,1)S(1)}, bf16[384,896]{1,0:T(8,128)(2,1)}, u32[]{:S(2)}, u32[]{:S(2)}) %collective-permute-start.14) | collective-permute-done | bytes 688160 | tf_op jit(solution)/shard_map/ppermute | solution.py:384
  72.5 5.5 %collective-permute-start.16 = (bf16[384,896]{1,0:T(8,128)(2,1)}, bf16[384,896]{1,0:T(8,128)(2,1)S(1)}, u32[]{:S(2)}, u32[]{:S(2)}) collective-permute-start(bf16[384,896]{1,0:T(8,128)(2,1)} %collective-permute-done.14.refs_1_), channel_id=1, source_target_pairs={{0,16},{16,0},{32,48},{48,32},{64,80},{80,64},{96,112},{112,96},{1... | collective-permute-start | bytes 2064392 | tf_op jit(solution)/shard_map/ppermute | solution.py:40
  78.1 0.2 collective-permute-start.15
  78.3 5.8 %collective-permute-done.15 = bf16[96,1536]{1,0:T(8,128)(2,1)S(1)} collective-permute-done((bf16[96,1536]{1,0:T(8,128)(2,1)S(1)}, bf16[96,1536]{1,0:T(8,128)(2,1)S(1)}, u32[]{:S(2)}, u32[]{:S(2)}) %collective-permute-start.15) | collective-permute-done | bytes 294944 | tf_op jit(solution)/shard_map/ppermute | solution.py:384
  84.1 1.9 %collective-permute-start.17 = (bf16[192,1536]{1,0:T(8,128)(2,1)S(1)}, bf16[192,1536]{1,0:T(8,128)(2,1)S(1)}, u32[]{:S(2)}, u32[]{:S(2)}) collective-permute-start(bf16[192,1536]{1,0:T(8,128)(2,1)S(1)} %pad_maximum_fusion.1.low), channel_id=1, source_target_pairs={{0,4},{1,5},{2,6},{3,7},{4,0},{5,1},{6,2},{7,3},{8,12},{9,13},{10,... | collective-permute-start | bytes 1769480 | tf_op jit(solution)/shard_map/ppermute | solution.py:384
  86.0 0.3 collective-permute-start.23
  86.3 0.2 collective-permute-start.24
  86.5 4.0 %right_root.1.root = bf16[1536,1536]{1,0:T(8,128)(2,1)S(1)} custom-call(s32[10]{0:T(128)S(1)} %stack.43.place, bf16[384,896]{1,0:T(8,128)(2,1)S(1)} %pad_maximum_fusion.refs_0_, bf16[384,896]{1,0:T(8,128)(2,1)} %collective-permute-done.14.refs_1_, bf16[384,896]{1,0:T(8,128)(2,1)S(1)} %collective-permute-done.21.refs_2_, ...), custom_call_target="tpu_custom_call" | custom-call | flops 10000000 | bytes 8000000 | tf_op jit(solution)/shard_map/right_root/pallas_call | solution.py:261
  90.6 2.0 %product.4.p0 = bf16[384,1536]{1,0:T(8,128)(2,1)S(1)} custom-call(bf16[384,1536]{1,0:T(8,128)(2,1)S(1)} %copy-done, bf16[1536,1536]{1,0:T(8,128)(2,1)S(1)} %right_root.1.root), custom_call_target="tpu_custom_call" | custom-call | flops 1800000000 | bytes 7000000 | tf_op jit(solution)/shard_map/product/pallas_call | solution.py:293
  92.6 2.5 %product.6.p2 = bf16[384,1536]{1,0:T(8,128)(2,1)S(1)} custom-call(s32[10]{0:T(128)S(1)} %stack.43.place, bf16[384,768]{1,0:T(8,128)(2,1)S(1)} %copy-done.2, bf16[384,768]{1,0:T(8,128)(2,1)S(1)} %collective-permute-done.22.second, bf16[1536,1536]{1,0:T(8,128)(2,1)S(1)} %right_root.1.root), custom_call_target="tpu_custom_call" | custom-call | flops 1800000000 | bytes 7000000 | tf_op jit(solution)/shard_map/product/pallas_call | solution.py:293
  95.1 2.0 %product.5.p1 = bf16[384,1536]{1,0:T(8,128)(2,1)S(1)} custom-call(bf16[384,1536]{1,0:T(8,128)(2,1)S(1)} %collective-permute-done.other.tile, bf16[1536,1536]{1,0:T(8,128)(2,1)S(1)} %right_root.1.root), custom_call_target="tpu_custom_call" | custom-call | flops 1800000000 | bytes 7000000 | tf_op jit(solution)/shard_map/product/pallas_call | solution.py:293
  97.1 0.8 left_rows.1
  98.0 0.4 collective-permute-start.18
  98.4 1.8 %collective-permute-start.20 = (f32[8,128]{1,0:T(8,128)S(1)}, f32[8,128]{1,0:T(8,128)S(1)}, u32[]{:S(2)}, u32[]{:S(2)}) collective-permute-start(f32[8,128]{1,0:T(8,128)S(1)} %get-tuple-element.43.a), channel_id=1, source_target_pairs={{0,48},{16,32},{32,16},{48,0},{64,112},{80,96},{96,80},{112,64},{1... | collective-permute-start | bytes 12296 | tf_op jit(solution)/shard_map/ppermute | solution.py:40
  100.2 2.5 %product.7.p3 = bf16[384,1536]{1,0:T(8,128)(2,1)S(1)} custom-call(s32[10]{0:T(128)S(1)} %stack.43.place, bf16[384,768]{1,0:T(8,128)(2,1)S(1)} %collective-permute-done.23.first, bf16[384,768]{1,0:T(8,128)(2,1)S(1)} %collective-permute-done.24.second, bf16[1536,1536]{1,0:T(8,128)(2,1)S(1)} %right_root.1.root), custom_call_target="tpu_custom_call" | custom-call | flops 1800000000 | bytes 7000000 | tf_op jit(solution)/shard_map/product/pallas_call | solution.py:293
  102.8 2.7 %precond.1 = (f32[384,1536]{1,0:T(8,128)S(1)}, f32[16,128]{1,0:T(8,128)S(1)}) custom-call(f32[8,128]{1,0:T(8,128)S(1)} %get-tuple-element.43.a, f32[8,128]{1,0:T(8,128)S(1)} %collective-permute-done.18.b, f32[8,128]{1,0:T(8,128)S(1)} %collective-permute-done.19.c, f32[8,128]{1,0:T(8,128)S(1)} %collective-permute-done.20.d, ...), custom_call_target="tpu_custom_call" | custom-call | flops 1800000000 | bytes 8000000 | tf_op jit(solution)/shard_map/precond/pallas_call | solution.py:333
  105.6 0.6 collective-permute-start.26
  106.2 1.5 %collective-permute-start.27 = (f32[16,128]{1,0:T(8,128)S(1)}, f32[16,128]{1,0:T(8,128)S(1)}, u32[]{:S(2)}, u32[]{:S(2)}) collective-permute-start(f32[16,128]{1,0:T(8,128)S(1)} %get-tuple-element.47.a), channel_id=1, source_target_pairs={{0,48},{16,32},{32,16},{48,0},{64,112},{80,96},{96,80},{112,64},{1... | collective-permute-start | bytes 24584 | tf_op jit(solution)/shard_map/ppermute | solution.py:40
  107.7 0.5 collective-permute-done.26.c
  108.2 1.2 %collective-permute-done.27.d = f32[16,128]{1,0:T(8,128)S(1)} collective-permute-done((f32[16,128]{1,0:T(8,128)S(1)}, f32[16,128]{1,0:T(8,128)S(1)}, u32[]{:S(2)}, u32[]{:S(2)}) %collective-permute-start.27) | collective-permute-done | bytes 8224 | tf_op jit(solution)/shard_map/ppermute | solution.py:40
  109.4 1.9 %graft.1 = bf16[384,1536]{1,0:T(8,128)(2,1)} custom-call(f32[16,128]{1,0:T(8,128)S(1)} %get-tuple-element.47.a, f32[16,128]{1,0:T(8,128)S(1)} %collective-permute-done.25.b, f32[16,128]{1,0:T(8,128)S(1)} %collective-permute-done.26.c, f32[16,128]{1,0:T(8,128)S(1)} %collective-permute-done.27.d, f32[384,1536]{1,0:T(8,128)S(1)} %get-tuple-element.48.value), custom_call_target="tpu_custom_call" | custom-call | flops 1000000 | bytes 4000000 | tf_op jit(solution)/shard_map/graft/pallas_call | solution.py:356
  (47 shorter events, 1.3 us)
Async XLA Ops:
  0.0 5.9 %copy-start = (bf16[384,1536]{1,0:T(8,128)(2,1)S(1)}, bf16[384,1536]{1,0:T(8,128)(2,1)}, u32[]{:S(2)}) copy-start(bf16[384,1536]{1,0:T(8,128)(2,1)} %tile.1) | copy-start | bytes 3538948
  0.0 5.9 %collective-permute-start = (bf16[384,1536]{1,0:T(8,128)(2,1)}, bf16[384,1536]{1,0:T(8,128)(2,1)S(1)}, u32[]{:S(2)}, u32[]{:S(2)}) collective-permute-start(bf16[384,1536]{1,0:T(8,128)(2,1)} %tile.1), channel_id=1, source_target_pairs={{0,16},{16,0},{32,48},{48,32},{64,80},{80,64},{96,112},{112,96},{1... | collective-permute-start | bytes 3538952 | tf_op jit(solution)/shard_map/ppermute | solution.py:40
  5.2 15.1 %collective-permute-start.3 = (bf16[384,768]{1,0:T(8,128)(2,1)}, bf16[384,768]{1,0:T(8,128)(2,1)S(1)}, u32[]{:S(2)}, u32[]{:S(2)}) collective-permute-start(bf16[384,768]{1,0:T(8,128)(2,1)} %constant_dynamic-slice_fusion.1), channel_id=1, source_target_pairs={{0,32},{16,48},{32,0},{48,16},{64,96},{80,112},{96,64},{112,80},{1... | collective-permute-start | bytes 1769480 | tf_op jit(solution)/shard_map/ppermute | solution.py:40
  8.3 15.2 %collective-permute-start.6 = (bf16[384,896]{1,0:T(8,128)(2,1)S(1)}, bf16[384,896]{1,0:T(8,128)(2,1)S(1)}, u32[]{:S(2)}, u32[]{:S(2)}) collective-permute-start(bf16[384,896]{1,0:T(8,128)(2,1)S(1)} %get-tuple-element.35), channel_id=1, source_target_pairs={{0,96},{1,97},{2,98},{3,99},{4,100},{5,101},{6,102},{7,103},{8,104... | collective-permute-start | bytes 2064392 | tf_op jit(solution)/shard_map/ppermute | solution.py:384
  10.8 11.0 %collective-permute-start.1 = (bf16[192,768]{1,0:T(8,128)(2,1)S(1)}, bf16[192,768]{1,0:T(8,128)(2,1)S(1)}, u32[]{:S(2)}, u32[]{:S(2)}) collective-permute-start(bf16[192,768]{1,0:T(8,128)(2,1)S(1)} %get-tuple-element.28), channel_id=1, source_target_pairs={{0,4},{1,5},{2,6},{3,7},{4,0},{5,1},{6,2},{7,3},{8,12},{9,13},{10,... | collective-permute-start | bytes 884744 | tf_op jit(solution)/shard_map/ppermute | solution.py:384
  20.3 1.6 %copy-start.1 = (bf16[384,768]{1,0:T(8,128)(2,1)}, bf16[384,768]{1,0:T(8,128)(2,1)S(1)}, u32[]{:S(2)}) copy-start(bf16[384,768]{1,0:T(8,128)(2,1)S(1)} %collective-permute-done.3.near.first) | copy-start | bytes 1769476
  22.0 4.3 %collective-permute-start.2 = (bf16[96,768]{1,0:T(8,128)(2,1)S(1)}, bf16[96,768]{1,0:T(8,128)(2,1)S(1)}, u32[]{:S(2)}, u32[]{:S(2)}) collective-permute-start(bf16[96,768]{1,0:T(8,128)(2,1)S(1)} %slice.78), channel_id=1, source_target_pairs={{0,12},{1,13},{2,14},{3,15},{4,8},{5,9},{6,10},{7,11},{8,4},{9,5},... | collective-permute-start | bytes 442376 | tf_op jit(solution)/shard_map/ppermute | solution.py:384
  22.1 8.5 %collective-permute-start.4 = (bf16[192,768]{1,0:T(8,128)(2,1)S(1)}, bf16[192,768]{1,0:T(8,128)(2,1)S(1)}, u32[]{:S(2)}, u32[]{:S(2)}) collective-permute-start(bf16[192,768]{1,0:T(8,128)(2,1)S(1)} %get-tuple-element.32), channel_id=1, source_target_pairs={{0,4},{1,5},{2,6},{3,7},{4,0},{5,1},{6,2},{7,3},{8,12},{9,13},{10,... | collective-permute-start | bytes 884744 | tf_op jit(solution)/shard_map/ppermute | solution.py:384
  23.7 7.4 %collective-permute-start.7 = (bf16[192,896]{1,0:T(8,128)(2,1)S(1)}, bf16[192,896]{1,0:T(8,128)(2,1)S(1)}, u32[]{:S(2)}, u32[]{:S(2)}) collective-permute-start(bf16[192,896]{1,0:T(8,128)(2,1)S(1)} %slice.76), channel_id=1, source_target_pairs={{0,128},{1,129},{2,130},{3,131},{4,132},{5,133},{6,134},{7,135},{8... | collective-permute-start | bytes 1032200 | tf_op jit(solution)/shard_map/ppermute | solution.py:384
  30.6 4.1 %collective-permute-start.5 = (bf16[96,768]{1,0:T(8,128)(2,1)S(1)}, bf16[96,768]{1,0:T(8,128)(2,1)S(1)}, u32[]{:S(2)}, u32[]{:S(2)}) collective-permute-start(bf16[96,768]{1,0:T(8,128)(2,1)S(1)} %slice.77), channel_id=1, source_target_pairs={{0,12},{1,13},{2,14},{3,15},{4,8},{5,9},{6,10},{7,11},{8,4},{9,5},... | collective-permute-start | bytes 442376 | tf_op jit(solution)/shard_map/ppermute | solution.py:384
  31.2 9.1 %collective-permute-start.9 = (bf16[192,896]{1,0:T(8,128)(2,1)S(1)}, bf16[192,896]{1,0:T(8,128)(2,1)S(1)}, u32[]{:S(2)}, u32[]{:S(2)}) collective-permute-start(bf16[192,896]{1,0:T(8,128)(2,1)S(1)} %fusion), channel_id=1, source_target_pairs={{0,32},{16,48},{32,0},{48,16},{64,96},{80,112},{96,64},{112,80},{1... | collective-permute-start | bytes 1032200 | tf_op jit(solution)/shard_map/ppermute | solution.py:40
  34.7 12.4 %collective-permute-start.8 = (bf16[96,1536]{1,0:T(8,128)(2,1)S(1)}, bf16[96,1536]{1,0:T(8,128)(2,1)S(1)}, u32[]{:S(2)}, u32[]{:S(2)}) collective-permute-start(bf16[96,1536]{1,0:T(8,128)(2,1)S(1)} %pad_maximum_fusion.2), channel_id=1, source_target_pairs={{0,1},{1,0},{2,3},{3,2},{4,5},{5,4},{6,7},{7,6},{8,9},{9,8},{10,11... | collective-permute-start | bytes 884744 | tf_op jit(solution)/shard_map/ppermute | solution.py:384
  47.1 7.3 %collective-permute-start.11 = (bf16[192,896]{1,0:T(8,128)(2,1)S(1)}, bf16[192,896]{1,0:T(8,128)(2,1)S(1)}, u32[]{:S(2)}, u32[]{:S(2)}) collective-permute-start(bf16[192,896]{1,0:T(8,128)(2,1)S(1)} %add_convert_fusion), channel_id=1, source_target_pairs={{0,128},{1,129},{2,130},{3,131},{4,132},{5,133},{6,134},{7,135},{8... | collective-permute-start | bytes 1032200 | tf_op jit(solution)/shard_map/ppermute | solution.py:384
  49.7 10.9 %collective-permute-start.10 = (bf16[96,1536]{1,0:T(8,128)(2,1)S(1)}, bf16[96,1536]{1,0:T(8,128)(2,1)S(1)}, u32[]{:S(2)}, u32[]{:S(2)}) collective-permute-start(bf16[96,1536]{1,0:T(8,128)(2,1)S(1)} %add_convert_fusion.2), channel_id=1, source_target_pairs={{0,3},{1,2},{2,1},{3,0},{4,7},{5,6},{6,5},{7,4},{8,11},{9,10},{10,... | collective-permute-start | bytes 884744 | tf_op jit(solution)/shard_map/ppermute | solution.py:384
  60.6 12.0 %collective-permute-start.14 = (bf16[384,896]{1,0:T(8,128)(2,1)S(1)}, bf16[384,896]{1,0:T(8,128)(2,1)}, u32[]{:S(2)}, u32[]{:S(2)}) collective-permute-start(bf16[384,896]{1,0:T(8,128)(2,1)S(1)} %pad_maximum_fusion.refs_0_), channel_id=1, source_target_pairs={{0,96},{1,97},{2,98},{3,99},{4,100},{5,101},{6,102},{7,103},{8,104... | collective-permute-start | bytes 2064392 | tf_op jit(solution)/shard_map/ppermute | solution.py:384
  63.9 7.0 %collective-permute-start.12 = (bf16[96,768]{1,0:T(8,128)(2,1)S(1)}, bf16[96,768]{1,0:T(8,128)(2,1)S(1)}, u32[]{:S(2)}, u32[]{:S(2)}) collective-permute-start(bf16[96,768]{1,0:T(8,128)(2,1)S(1)} %get-tuple-element.39), channel_id=1, source_target_pairs={{0,32},{16,48},{32,0},{48,16},{64,96},{80,112},{96,64},{112,80},{1... | collective-permute-start | bytes 442376 | tf_op jit(solution)/shard_map/ppermute | solution.py:40
  64.2 6.7 %collective-permute-start.13 = (bf16[96,384]{1,0:T(8,128)(2,1)S(1)}, bf16[96,384]{1,0:T(8,128)(2,1)S(1)}, u32[]{:S(2)}, u32[]{:S(2)}) collective-permute-start(bf16[96,384]{1,0:T(8,128)(2,1)S(1)} %slice.49), channel_id=1, source_target_pairs={{0,16},{16,0},{32,48},{48,32},{64,80},{80,64},{96,112},{112,96},{1... | collective-permute-start | bytes 221192 | tf_op jit(solution)/shard_map/ppermute | solution.py:40
  68.9 17.1 %copy-start.2 = (bf16[384,768]{1,0:T(8,128)(2,1)S(1)}, bf16[384,768]{1,0:T(8,128)(2,1)}, u32[]{:S(2)}) copy-start(bf16[384,768]{1,0:T(8,128)(2,1)} %copy-done.1) | copy-start | bytes 1769476
  68.9 17.4 %collective-permute-start.22 = (bf16[384,768]{1,0:T(8,128)(2,1)S(1)}, bf16[384,768]{1,0:T(8,128)(2,1)S(1)}, u32[]{:S(2)}, u32[]{:S(2)}) collective-permute-start(bf16[384,768]{1,0:T(8,128)(2,1)S(1)} %constant_dynamic-slice_fusion), channel_id=1, source_target_pairs={{0,32},{16,48},{32,0},{48,16},{64,96},{80,112},{96,64},{112,80},{1... | collective-permute-start | bytes 1769480 | tf_op jit(solution)/shard_map/ppermute | solution.py:40
  70.6 15.9 %collective-permute-start.21 = (bf16[384,896]{1,0:T(8,128)(2,1)S(1)}, bf16[384,896]{1,0:T(8,128)(2,1)S(1)}, u32[]{:S(2)}, u32[]{:S(2)}) collective-permute-start(bf16[384,896]{1,0:T(8,128)(2,1)S(1)} %pad_maximum_fusion.refs_0_), channel_id=1, source_target_pairs={{0,16},{16,0},{32,48},{48,32},{64,80},{80,64},{96,112},{112,96},{1... | collective-permute-start | bytes 2064392 | tf_op jit(solution)/shard_map/ppermute | solution.py:40
  72.5 11.5 %collective-permute-start.16 = (bf16[384,896]{1,0:T(8,128)(2,1)}, bf16[384,896]{1,0:T(8,128)(2,1)S(1)}, u32[]{:S(2)}, u32[]{:S(2)}) collective-permute-start(bf16[384,896]{1,0:T(8,128)(2,1)} %collective-permute-done.14.refs_1_), channel_id=1, source_target_pairs={{0,16},{16,0},{32,48},{48,32},{64,80},{80,64},{96,112},{112,96},{1... | collective-permute-start | bytes 2064392 | tf_op jit(solution)/shard_map/ppermute | solution.py:40
  78.1 6.0 %collective-permute-start.15 = (bf16[96,1536]{1,0:T(8,128)(2,1)S(1)}, bf16[96,1536]{1,0:T(8,128)(2,1)S(1)}, u32[]{:S(2)}, u32[]{:S(2)}) collective-permute-start(bf16[96,1536]{1,0:T(8,128)(2,1)S(1)} %pad_maximum_fusion.3), channel_id=1, source_target_pairs={{0,12},{1,13},{2,14},{3,15},{4,8},{5,9},{6,10},{7,11},{8,4},{9,5},... | collective-permute-start | bytes 884744 | tf_op jit(solution)/shard_map/ppermute | solution.py:384
  84.1 13.0 %collective-permute-start.17 = (bf16[192,1536]{1,0:T(8,128)(2,1)S(1)}, bf16[192,1536]{1,0:T(8,128)(2,1)S(1)}, u32[]{:S(2)}, u32[]{:S(2)}) collective-permute-start(bf16[192,1536]{1,0:T(8,128)(2,1)S(1)} %pad_maximum_fusion.1.low), channel_id=1, source_target_pairs={{0,4},{1,5},{2,6},{3,7},{4,0},{5,1},{6,2},{7,3},{8,12},{9,13},{10,... | collective-permute-start | bytes 1769480 | tf_op jit(solution)/shard_map/ppermute | solution.py:384
  86.0 14.2 %collective-permute-start.23 = (bf16[384,768]{1,0:T(8,128)(2,1)S(1)}, bf16[384,768]{1,0:T(8,128)(2,1)S(1)}, u32[]{:S(2)}, u32[]{:S(2)}) collective-permute-start(bf16[384,768]{1,0:T(8,128)(2,1)S(1)} %copy-done.2), channel_id=1, source_target_pairs={{0,16},{16,0},{32,48},{48,32},{64,80},{80,64},{96,112},{112,96},{1... | collective-permute-start | bytes 1769480 | tf_op jit(solution)/shard_map/ppermute | solution.py:40
  86.3 13.9 %collective-permute-start.24 = (bf16[384,768]{1,0:T(8,128)(2,1)S(1)}, bf16[384,768]{1,0:T(8,128)(2,1)S(1)}, u32[]{:S(2)}, u32[]{:S(2)}) collective-permute-start(bf16[384,768]{1,0:T(8,128)(2,1)S(1)} %collective-permute-done.22.second), channel_id=1, source_target_pairs={{0,16},{16,0},{32,48},{48,32},{64,80},{80,64},{96,112},{112,96},{1... | collective-permute-start | bytes 1769480 | tf_op jit(solution)/shard_map/ppermute | solution.py:40
  98.0 4.8 %collective-permute-start.18 = (f32[8,128]{1,0:T(8,128)S(1)}, f32[8,128]{1,0:T(8,128)S(1)}, u32[]{:S(2)}, u32[]{:S(2)}) collective-permute-start(f32[8,128]{1,0:T(8,128)S(1)} %get-tuple-element.43.a), channel_id=1, source_target_pairs={{0,16},{16,0},{32,48},{48,32},{64,80},{80,64},{96,112},{112,96},{1... | collective-permute-start | bytes 12296 | tf_op jit(solution)/shard_map/ppermute | solution.py:40
  98.4 4.4 %collective-permute-start.19 = (f32[8,128]{1,0:T(8,128)S(1)}, f32[8,128]{1,0:T(8,128)S(1)}, u32[]{:S(2)}, u32[]{:S(2)}) collective-permute-start(f32[8,128]{1,0:T(8,128)S(1)} %get-tuple-element.43.a), channel_id=1, source_target_pairs={{0,32},{16,48},{32,0},{48,16},{64,96},{80,112},{96,64},{112,80},{1... | collective-permute-start | bytes 12296 | tf_op jit(solution)/shard_map/ppermute | solution.py:40
  98.4 4.4 %collective-permute-start.20 = (f32[8,128]{1,0:T(8,128)S(1)}, f32[8,128]{1,0:T(8,128)S(1)}, u32[]{:S(2)}, u32[]{:S(2)}) collective-permute-start(f32[8,128]{1,0:T(8,128)S(1)} %get-tuple-element.43.a), channel_id=1, source_target_pairs={{0,48},{16,32},{32,16},{48,0},{64,112},{80,96},{96,80},{112,64},{1... | collective-permute-start | bytes 12296 | tf_op jit(solution)/shard_map/ppermute | solution.py:40
  105.5 2.2 %collective-permute-start.25 = (f32[16,128]{1,0:T(8,128)S(1)}, f32[16,128]{1,0:T(8,128)S(1)}, u32[]{:S(2)}, u32[]{:S(2)}) collective-permute-start(f32[16,128]{1,0:T(8,128)S(1)} %get-tuple-element.47.a), channel_id=1, source_target_pairs={{0,16},{16,0},{32,48},{48,32},{64,80},{80,64},{96,112},{112,96},{1... | collective-permute-start | bytes 24584 | tf_op jit(solution)/shard_map/ppermute | solution.py:40
  105.6 2.6 %collective-permute-start.26 = (f32[16,128]{1,0:T(8,128)S(1)}, f32[16,128]{1,0:T(8,128)S(1)}, u32[]{:S(2)}, u32[]{:S(2)}) collective-permute-start(f32[16,128]{1,0:T(8,128)S(1)} %get-tuple-element.47.a), channel_id=1, source_target_pairs={{0,32},{16,48},{32,0},{48,16},{64,96},{80,112},{96,64},{112,80},{1... | collective-permute-start | bytes 24584 | tf_op jit(solution)/shard_map/ppermute | solution.py:40
  106.2 3.2 %collective-permute-start.27 = (f32[16,128]{1,0:T(8,128)S(1)}, f32[16,128]{1,0:T(8,128)S(1)}, u32[]{:S(2)}, u32[]{:S(2)}) collective-permute-start(f32[16,128]{1,0:T(8,128)S(1)} %get-tuple-element.47.a), channel_id=1, source_target_pairs={{0,48},{16,32},{32,16},{48,0},{64,112},{80,96},{96,80},{112,64},{1... | collective-permute-start | bytes 24584 | tf_op jit(solution)/shard_map/ppermute | solution.py:40
where the time goes:
time: 112 us; the launch traced here: 111 us
  starting transfers between devices  43.8 us (39%)
  waiting for transfers between devices  39.7 us (35%)
  Pallas kernels  24.4 us (22%)
  local copies, waits for them, and re-layouts  2.16 us (2%)
    ppermute x12, waiting for transfers between devices, turned(): return lax.ppermute(value, ('row', 'col'), pairs)  30.8 us
    ppermute x12, starting transfers between devices, turned(): return lax.ppermute(value, ('row', 'col'), pairs)  22.8 us
    ppermute x16, starting transfers between devices, hop(): return lax.ppermute(value, axis, [(i, i ^ mask) for i in range(16)])  21 us
    pallas_call x4, Pallas kernels, product(): pl.pallas_call(near_product_kernel if more else product_kernel, out_shape...  9.03 us
    ppermute x16, waiting for transfers between devices, hop(): return lax.ppermute(value, axis, [(i, i ^ mask) for i in range(16)])  8.97 us
    pallas_call x1, Pallas kernels, right_root(): pl.pallas_call(root_kernel, out_shape=sds((BLOCK, BLOCK), BF16), in_specs...  4.03 us
    pallas_call x1, Pallas kernels, precond(): pl.pallas_call(precond_kernel, out_shape=[sds((ROWS, BLOCK), F32), sds((1...  2.72 us
    pallas_call x1, Pallas kernels, right_gram(): pl.pallas_call(right_kernel, out_shape=[sds((2 * RIGHT, BAND * LANE), BF1...  2.35 us
  transfers between devices with their start and end apart: 28, of which 12 were waited for; matrix products, arithmetic and copies ran while one was open for 3% of the time, Pallas kernels for 18%

commit v1 on v0

--- a/solution.py
+++ b/solution.py
@@ -13,6 +13,7 @@
 HALF = BLOCK // 2
 RIGHT = 192
 LEFT = 96
+GRAFT = 96
 
 damping = 0.001
 F32 = jnp.float32
@@ -265,43 +266,47 @@
         out_specs=VMEM,
         scratch_shapes=[pltpu.VMEM((BLOCK, BAND * LANE), BF16), pltpu.SemaphoreType.DMA((8,))],
         compiler_params=params(24),
-        cost_estimate=cost(10**7, 8 * 10**6),
+        cost_estimate=cost(18 * 10**9, 8 * 10**6),
         name="right_root",
     )(place, *parts)
 
 
-def product_kernel(tile, root, out):
+def multiply(tile, root, out):
     for start in range(0, BLOCK, 512):
         out[:, start : start + 512] = jnp.dot(
             tile[...], root[:, start : start + 512], preferred_element_type=F32
         ).astype(BF16)
 
 
-def near_product_kernel(place, first, second, root, out):
+def chip_product_kernel(mine, other, root, out):
+    multiply(mine, root, out.at[pl.ds(0, ROWS), :])
+    multiply(other, root, out.at[pl.ds(ROWS, ROWS), :])
+
+
+def near_product_kernel(place, near, near_late, far, far_late, root, out, tile):
     upper = place[9]
-    top = pl.ds(pl.multiple_of(upper * HALF, 16), HALF)
-    rest = pl.ds(pl.multiple_of((1 - upper) * HALF, 16), HALF)
-    for start in range(0, BLOCK, 512):
-        span = slice(start, start + 512)
-        part = jnp.dot(first[...], root[top, span], preferred_element_type=F32)
-        part = part + jnp.dot(second[...], root[rest, span], preferred_element_type=F32)
-        out[:, span] = part.astype(BF16)
-
-
-def product(root, tile, *more):
-    near = [tile, *more]
-    return pl.pallas_call(
-        near_product_kernel if more else product_kernel,
-        out_shape=sds((ROWS, BLOCK), BF16),
-        in_specs=([SMEM] if more else []) + [VMEM] * (len(near) - 1 if more else len(near)) + [VMEM],
+    early = pl.ds(pl.multiple_of(upper * HALF, LANE), HALF)
+    late = pl.ds(pl.multiple_of((1 - upper) * HALF, LANE), HALF)
+    for at, (first, second) in enumerate(((near, near_late), (far, far_late))):
+        tile[at, :, early] = first[...]
+        tile[at, :, late] = second[...]
+        multiply(tile.at[at], root, out.at[pl.ds(at * ROWS, ROWS), :])
+
+
+def product(kernel, scratch, *refs):
+    return pl.pallas_call(
+        kernel,
+        out_shape=sds((2 * ROWS, BLOCK), BF16),
+        in_specs=[SMEM if ref.ndim == 1 else VMEM for ref in refs],
         out_specs=VMEM,
+        scratch_shapes=scratch,
         compiler_params=params(24),
-        cost_estimate=cost(18 * 10**8, 7 * 10**6),
+        cost_estimate=cost(18 * 10**9, 9 * 10**6),
         name="product",
-    )(*near, root)
-
-
-def precond_kernel(a, b, c, d, rows, p0, p1, p2, p3, grad, out, square_out, root):
+    )(*refs)
+
+
+def precond_kernel(a, b, c, d, rows, chip, near, grad, out, square_out, root):
     scale = scale_of((a[...] + b[...]) + (c[...] + d[...]))
     factor = 0.25 / jnp.sqrt(jnp.sqrt(scale))
     inverse = 1.0 / scale
@@ -316,13 +321,9 @@
         root[:, start : start + ROWS] = ((-part * inverse) * factor).astype(BF16)
     total = jnp.zeros((8, LANE), F32)
     for start in range(0, BLOCK, 256):
-        part = jnp.dot(root[:, :ROWS], p0[:, start : start + 256], preferred_element_type=F32)
-        for at, tile in ((1, p1), (2, p2), (3, p3)):
-            part = part + jnp.dot(
-                root[:, at * ROWS : (at + 1) * ROWS],
-                tile[:, start : start + 256],
-                preferred_element_type=F32,
-            )
+        span = slice(start, start + 256)
+        part = jnp.dot(root[:, :HALF], chip[:, span], preferred_element_type=F32)
+        part = part + jnp.dot(root[:, HALF:], near[:, span], preferred_element_type=F32)
         out[:, start : start + 256] = part
         total = total + folded(part * part)
     square_out[:8, :] = total
@@ -333,7 +334,7 @@
     return pl.pallas_call(
         precond_kernel,
         out_shape=[sds((ROWS, BLOCK), F32), sds((16, LANE), F32)],
-        in_specs=[VMEM] * 10,
+        in_specs=[VMEM] * 8,
         out_specs=[VMEM] * 2,
         scratch_shapes=[pltpu.VMEM((ROWS, BLOCK), BF16)],
         compiler_params=params(40),
@@ -342,23 +343,28 @@
     )(*totals, rows, *tiles, grad)
 
 
-def graft_kernel(a, b, c, d, value, out):
+def graft_kernel(a, b, c, d, value, out, held, sems):
     total = (a[...] + b[...]) + (c[...] + d[...])
     pre = jnp.sum(jnp.sum(total[:8, :], axis=1, keepdims=True), axis=0, keepdims=True)
     factor = scale_of(total[8:, :]) / jnp.sqrt(jnp.broadcast_to(pre, (1, LANE)) + 1e-06)
-    out[...] = (value[...] * widened(factor, BLOCK)).astype(BF16)
+    factor = widened(factor, BLOCK)
+    copies = []
+    for at in range(ROWS // GRAFT):
+        rows = pl.ds(at * GRAFT, GRAFT)
+        held[rows, :] = (value[rows, :] * factor).astype(BF16)
+        copies.append(pltpu.make_async_copy(held.at[rows, :], out.at[rows, :], sems.at[at]))
+        copies[-1].start()
+    for copy in copies:
+        copy.wait()
 
 
 def graft(totals, value):
-    step = 96
-    small = pl.BlockSpec((16, LANE), lambda i: (0, 0))
-    wide = pl.BlockSpec((step, BLOCK), lambda i: (i, 0))
     return pl.pallas_call(
         graft_kernel,
-        grid=(ROWS // step,),
         out_shape=sds((ROWS, BLOCK), BF16),
-        in_specs=[small] * 4 + [wide],
-        out_specs=wide,
+        in_specs=[VMEM] * 5,
+        out_specs=ANY,
+        scratch_shapes=[pltpu.VMEM((ROWS, BLOCK), BF16), pltpu.SemaphoreType.DMA((ROWS // GRAFT,))],
         compiler_params=params(24),
         cost_estimate=cost(10**6, 4 * 10**6),
         name="graft",
@@ -481,29 +487,29 @@
     own, cross = next(owns), next(crosses)
     deep = begun(deep_steps(jnp.concatenate([own, cross], axis=1)))
     c3 = deep.send([r2])
-    r4 = rights.send([c3])
+    r4 = rights.send([])
     next(deep)
     c4 = deep.send([r3])
     both = next(deep)
-    r5 = rights.send([c4])
-    c5, cross = pair_step(both[:, 2 * ROWS :], [r4])
+    r5 = rights.send([])
+    late = lax.dynamic_slice(after(gradient, r3), (0, upper * HALF), (ROWS, HALF))
+    near_late = hop(late, "row", NEAR)
+    c5, cross = pair_step(both[:, 2 * ROWS :], [r4, near_late])
     gather = begun(gather_steps(jnp.concatenate([both[:, : 2 * ROWS], cross], axis=1)))
     c6 = gather.send([r5])
     r6 = rights.send([])
+    parts = next(rights)
+    root = right_root(place, parts)
     c7 = gather.send([r6])
-    parts, sides = next(rights), next(gather)
-    late = lax.dynamic_slice(after(gradient, r3), (0, upper * HALF), (ROWS, HALF))
-    near_late = hop(late, "row", NEAR)
+    sides = next(gather)
     far = hop(near, "row", CORE)
     far_late = hop(near_late, "row", CORE)
     rows, square = left_rows(place, sides)
     totals = spread(square)
-    root = right_root(place, parts)
+    scratch = [pltpu.VMEM((2, ROWS, BLOCK), BF16)]
     tiles = [
-        product(root, gradient),
-        product(root, other),
-        product(root, place, near, near_late),
-        product(root, place, far, far_late),
+        product(chip_product_kernel, [], gradient, other, root),
+        product(near_product_kernel, scratch, place, near, near_late, far, far_late, root),
     ]
     value, square = precond(totals, rows, tiles, grad)
     return graft(spread(square), value)

time: 112 us -> 104 us (0.929)
  waiting for transfers between devices: 39.7 us -> 30.2 us
  starting transfers between devices: 43.8 us -> 46.6 us
  other arithmetic: 0.78 us -> 3.53 us
  Pallas kernels: 24.4 us -> 22 us
    ppermute x12, waiting for transfers between devices: 30.8 us -> 19.5 us  [turned(): return lax.ppermute(value, ('row', 'col'), pairs)]
    ppermute x16, starting transfers between devices: 21 us -> 25.5 us  [hop(): return lax.ppermute(value, axis, [(i, i ^ mask) for i in range(16)])]
    ppermute x16, waiting for transfers between devices: 8.97 us -> 10.7 us  [hop(): return lax.ppermute(value, axis, [(i, i ^ mask) for i in range(16)])]
    convert_element_type x2, other arithmetic: 0.14 us -> 1.91 us  [deep_steps(): mine = total_of(mine, came).astype(BF16)]
    ppermute x12, starting transfers between devices: 22.8 us -> 21.1 us  [turned(): return lax.ppermute(value, ('row', 'col'), pairs)]
    pallas_call x5 -> x3, Pallas kernels: 10.9 us -> 9.45 us  [the longest x2 8.25 us: product(): pl.pallas_call(kernel, out_shape=sds((2 * ROWS, BLOCK), BF16), in_specs=[...]
  transfers between devices with their start and end apart: 28 -> 28, of which waited for: 12 -> 13; matrix products, arithmetic and copies ran while one was open for 3% -> 5% of each run, Pallas kernels for 18% -> 18%
where the time goes in v1:
time: 104 us
  starting transfers between devices  46.6 us (45%)
  waiting for transfers between devices  30.2 us (29%)
  Pallas kernels  22 us (21%)
  other arithmetic  3.53 us (3%)
  local copies, waits for them, and re-layouts  1.34 us (1%)
    ppermute x16, starting transfers between devices, hop(): return lax.ppermute(value, axis, [(i, i ^ mask) for i in range(16)])  25.5 us
    ppermute x12, starting transfers between devices, turned(): return lax.ppermute(value, ('row', 'col'), pairs)  21.1 us
    ppermute x12, waiting for transfers between devices, turned(): return lax.ppermute(value, ('row', 'col'), pairs)  19.5 us
    ppermute x16, waiting for transfers between devices, hop(): return lax.ppermute(value, axis, [(i, i ^ mask) for i in range(16)])  10.7 us
    pallas_call x2, Pallas kernels, product(): pl.pallas_call(kernel, out_shape=sds((2 * ROWS, BLOCK), BF16), in_specs=[...  8.25 us
    pallas_call x1, Pallas kernels, right_root(): pl.pallas_call(root_kernel, out_shape=sds((BLOCK, BLOCK), BF16), in_specs...  3.7 us
    pallas_call x1, Pallas kernels, right_gram(): pl.pallas_call(right_kernel, out_shape=[sds((2 * RIGHT, BAND * LANE), BF1...  2.35 us
    pallas_call x1, Pallas kernels, precond(): pl.pallas_call(precond_kernel, out_shape=[sds((ROWS, BLOCK), F32), sds((1...  2.11 us
  transfers between devices with their start and end apart: 28, of which 13 were waited for; matrix products, arithmetic and copies ran while one was open for 5% of the time, Pallas kernels for 18%

profile of v1, /device:TPU:1, one launch (start us, length us, event | category | flops | bytes accessed | tf_op | source)
XLA Modules:
  0.0 104.2 jit_solution(4997119298071612278)
XLA Ops:
  0.0 3.2 %collective-permute-start = (bf16[384,1536]{1,0:T(8,128)(2,1)}, bf16[384,1536]{1,0:T(8,128)(2,1)S(1)}, u32[]{:S(2)}, u32[]{:S(2)}) collective-permute-start(bf16[384,1536]{1,0:T(8,128)(2,1)} %mine.7), channel_id=1, source_target_pairs={{0,16},{16,0},{32,48},{48,32},{64,80},{80,64},{96,112},{112,96},{1... | collective-permute-start | bytes 3538952 | tf_op jit(solution)/shard_map/ppermute | solution.py:41
  3.2 1.1 %constant_dynamic-slice_fusion.1 = bf16[384,768]{1,0:T(8,128)(2,1)S(1)} fusion(bf16[384,1536]{1,0:T(8,128)(2,1)} %mine.7, s32[]{:T(128)S(6)} %select_n.41), kind=kLoop, calls=%fused_computation.22 | loop fusion | bytes 1179652 | tf_op jit(solution)/shard_map/dynamic_slice | solution.py:475
  4.3 0.1 collective-permute-start.3
  4.6 1.3 %collective-permute-done.other = bf16[384,1536]{1,0:T(8,128)(2,1)S(1)} collective-permute-done((bf16[384,1536]{1,0:T(8,128)(2,1)}, bf16[384,1536]{1,0:T(8,128)(2,1)S(1)}, u32[]{:S(2)}, u32[]{:S(2)}) %collective-permute-start) | collective-permute-done | bytes 1179680 | tf_op jit(solution)/shard_map/ppermute | solution.py:41
  5.9 2.3 %right_gram.1 = (bf16[384,896]{1,0:T(8,128)(2,1)S(1)}, bf16[384,896]{1,0:T(8,128)(2,1)S(1)}) custom-call(s32[10]{0:T(128)S(1)} %stack.43.place, bf16[384,1536]{1,0:T(8,128)(2,1)S(1)} %copy-done, bf16[384,1536]{1,0:T(8,128)(2,1)S(1)} %collective-permute-done.other), custom_call_target="tpu_custom_call" | custom-call | flops 1000000 | bytes 10000 | tf_op jit(solution)/shard_map/right_gram/pallas_call | solution.py:101
  8.4 2.0 %own_gram.1 = (bf16[192,768]{1,0:T(8,128)(2,1)S(1)}, bf16[192,768]{1,0:T(8,128)(2,1)S(1)}, f32[8,128]{1,0:T(8,128)S(1)}) custom-call(s32[10]{0:T(128)S(1)} %stack.43.place, bf16[384,1536]{1,0:T(8,128)(2,1)S(1)} %copy-done, bf16[384,1536]{1,0:T(8,128)(2,1)S(1)} %collective-permute-done.other), custom_call_target="tpu_custom_call" | custom-call | flops 1000000 | bytes 10000 | tf_op jit(solution)/shard_map/own_gram/pallas_call | solution.py:126
  10.4 2.7 %collective-permute-start.1 = (bf16[192,768]{1,0:T(8,128)(2,1)S(1)}, bf16[192,768]{1,0:T(8,128)(2,1)S(1)}, u32[]{:S(2)}, u32[]{:S(2)}) collective-permute-start(bf16[192,768]{1,0:T(8,128)(2,1)S(1)} %get-tuple-element.26), channel_id=1, source_target_pairs={{0,4},{1,5},{2,6},{3,7},{4,0},{5,1},{6,2},{7,3},{8,12},{9,13},{10,... | collective-permute-start | bytes 884744 | tf_op jit(solution)/shard_map/ppermute | solution.py:390
  13.1 6.3 %collective-permute-done.3.near = bf16[384,768]{1,0:T(8,128)(2,1)S(1)} collective-permute-done((bf16[384,768]{1,0:T(8,128)(2,1)S(1)}, bf16[384,768]{1,0:T(8,128)(2,1)S(1)}, u32[]{:S(2)}, u32[]{:S(2)}) %collective-permute-start.3) | collective-permute-done | bytes 589856 | tf_op jit(solution)/shard_map/ppermute | solution.py:41
  19.3 1.6 %cross_gram.1 = (bf16[192,768]{1,0:T(8,128)(2,1)S(1)}, bf16[192,768]{1,0:T(8,128)(2,1)S(1)}) custom-call(s32[10]{0:T(128)S(1)} %stack.43.place, bf16[384,1536]{1,0:T(8,128)(2,1)S(1)} %copy-done, bf16[384,1536]{1,0:T(8,128)(2,1)S(1)} %collective-permute-done.other, bf16[384,768]{1,0:T(8,128)(2,1)S(1)} %collective-permute-done.3.near), custom_call_target="tpu_custom_call" | custom-call | flops 1000000 | bytes 10000 | tf_op jit(solution)/shard_map/cross_gram/pallas_call | solution.py:156
  21.1 1.4 %collective-permute-start.4 = (bf16[192,768]{1,0:T(8,128)(2,1)S(1)}, bf16[192,768]{1,0:T(8,128)(2,1)S(1)}, u32[]{:S(2)}, u32[]{:S(2)}) collective-permute-start(bf16[192,768]{1,0:T(8,128)(2,1)S(1)} %get-tuple-element.30), channel_id=1, source_target_pairs={{0,4},{1,5},{2,6},{3,7},{4,0},{5,1},{6,2},{7,3},{8,12},{9,13},{10,... | collective-permute-start | bytes 884744 | tf_op jit(solution)/shard_map/ppermute | solution.py:390
  22.6 0.1 convert_add_fusion
  22.7 2.6 %collective-permute-start.7 = (bf16[192,896]{1,0:T(8,128)(2,1)S(1)}, bf16[192,896]{1,0:T(8,128)(2,1)S(1)}, u32[]{:S(2)}, u32[]{:S(2)}) collective-permute-start(bf16[192,896]{1,0:T(8,128)(2,1)S(1)} %slice.76), channel_id=1, source_target_pairs={{0,128},{1,129},{2,130},{3,131},{4,132},{5,133},{6,134},{7,135},{8... | collective-permute-start | bytes 1032200 | tf_op jit(solution)/shard_map/ppermute | solution.py:390
  25.4 4.2 %collective-permute-done.4 = bf16[192,768]{1,0:T(8,128)(2,1)S(1)} collective-permute-done((bf16[192,768]{1,0:T(8,128)(2,1)S(1)}, bf16[192,768]{1,0:T(8,128)(2,1)S(1)}, u32[]{:S(2)}, u32[]{:S(2)}) %collective-permute-start.4) | collective-permute-done | bytes 294944 | tf_op jit(solution)/shard_map/ppermute | solution.py:390
  29.8 0.4 collective-permute-done.7
  30.2 0.4 collective-permute-start.9
  30.6 3.1 %collective-permute-done.5 = bf16[96,768]{1,0:T(8,128)(2,1)S(1)} collective-permute-done((bf16[96,768]{1,0:T(8,128)(2,1)S(1)}, bf16[96,768]{1,0:T(8,128)(2,1)S(1)}, u32[]{:S(2)}, u32[]{:S(2)}) %collective-permute-start.5) | collective-permute-done | bytes 147488 | tf_op jit(solution)/shard_map/ppermute | solution.py:390
  33.8 5.6 %collective-permute-start.8 = (bf16[96,1536]{1,0:T(8,128)(2,1)S(1)}, bf16[96,1536]{1,0:T(8,128)(2,1)S(1)}, u32[]{:S(2)}, u32[]{:S(2)}) collective-permute-start(bf16[96,1536]{1,0:T(8,128)(2,1)S(1)} %pad_maximum_fusion.2), channel_id=1, source_target_pairs={{0,1},{1,0},{2,3},{3,2},{4,5},{5,4},{6,7},{7,6},{8,9},{9,8},{10,11... | collective-permute-start | bytes 884744 | tf_op jit(solution)/shard_map/ppermute | solution.py:390
  39.4 2.6 %collective-permute-start.11 = (bf16[192,896]{1,0:T(8,128)(2,1)S(1)}, bf16[192,896]{1,0:T(8,128)(2,1)}, u32[]{:S(2)}, u32[]{:S(2)}) collective-permute-start(bf16[192,896]{1,0:T(8,128)(2,1)S(1)} %add_convert_fusion), channel_id=1, source_target_pairs={{0,128},{1,129},{2,130},{3,131},{4,132},{5,133},{6,134},{7,135},{8... | collective-permute-start | bytes 1032200 | tf_op jit(solution)/shard_map/ppermute | solution.py:390
  42.0 3.4 %collective-permute-done.8 = bf16[96,1536]{1,0:T(8,128)(2,1)S(1)} collective-permute-done((bf16[96,1536]{1,0:T(8,128)(2,1)S(1)}, bf16[96,1536]{1,0:T(8,128)(2,1)S(1)}, u32[]{:S(2)}, u32[]{:S(2)}) %collective-permute-start.8) | collective-permute-done | bytes 294944 | tf_op jit(solution)/shard_map/ppermute | solution.py:390
  45.4 0.8 add_convert_fusion.2
  46.2 2.5 %collective-permute-start.10 = (bf16[96,1536]{1,0:T(8,128)(2,1)}, bf16[96,1536]{1,0:T(8,128)(2,1)}, u32[]{:S(2)}, u32[]{:S(2)}) collective-permute-start(bf16[96,1536]{1,0:T(8,128)(2,1)} %add_convert_fusion.2), channel_id=1, source_target_pairs={{0,3},{1,2},{2,1},{3,0},{4,7},{5,6},{6,5},{7,4},{8,11},{9,10},{10,... | collective-permute-start | bytes 884744 | tf_op jit(solution)/shard_map/ppermute | solution.py:390
  48.7 1.3 %collective-permute-start.12 = (bf16[384,768]{1,0:T(8,128)(2,1)S(1)}, bf16[384,768]{1,0:T(8,128)(2,1)S(1)}, u32[]{:S(2)}, u32[]{:S(2)}) collective-permute-start(bf16[384,768]{1,0:T(8,128)(2,1)S(1)} %constant_dynamic-slice_fusion), channel_id=1, source_target_pairs={{0,32},{16,48},{32,0},{48,16},{64,96},{80,112},{96,64},{112,80},{1... | collective-permute-start | bytes 1769480 | tf_op jit(solution)/shard_map/ppermute | solution.py:41
  50.0 1.0 pad_maximum_fusion.refs_0_
  51.1 1.4 %collective-permute-start.15 = (bf16[384,896]{1,0:T(8,128)(2,1)S(1)}, bf16[384,896]{1,0:T(8,128)(2,1)S(1)}, u32[]{:S(2)}, u32[]{:S(2)}) collective-permute-start(bf16[384,896]{1,0:T(8,128)(2,1)S(1)} %pad_maximum_fusion.refs_0_), channel_id=1, source_target_pairs={{0,96},{1,97},{2,98},{3,99},{4,100},{5,101},{6,102},{7,103},{8,104... | collective-permute-start | bytes 2064392 | tf_op jit(solution)/shard_map/ppermute | solution.py:390
  52.4 4.2 %collective-permute-done.10 = bf16[96,1536]{1,0:T(8,128)(2,1)} collective-permute-done((bf16[96,1536]{1,0:T(8,128)(2,1)}, bf16[96,1536]{1,0:T(8,128)(2,1)}, u32[]{:S(2)}, u32[]{:S(2)}) %collective-permute-start.10) | collective-permute-done | bytes 294944 | tf_op jit(solution)/shard_map/ppermute | solution.py:390
  56.6 1.1 %add_convert_fusion.1 = bf16[96,1536]{1,0:T(8,128)(2,1)S(1)} fusion(bf16[96,1536]{1,0:T(8,128)(2,1)} %collective-permute-done.10, bf16[96,1536]{1,0:T(8,128)(2,1)} %add_convert_fusion.2), kind=kLoop, calls=%fused_computation.7 | loop fusion | flops 589824 | bytes 884736 | tf_op jit(solution)/shard_map/convert_element_type | solution.py:438
  57.8 0.6 collective-permute-done.12.near_late
  58.4 1.2 %collective-permute-start.13 = (bf16[96,768]{1,0:T(8,128)(2,1)S(1)}, bf16[96,768]{1,0:T(8,128)(2,1)S(1)}, u32[]{:S(2)}, u32[]{:S(2)}) collective-permute-start(bf16[96,768]{1,0:T(8,128)(2,1)S(1)} %get-tuple-element.37), channel_id=1, source_target_pairs={{0,32},{16,48},{32,0},{48,16},{64,96},{80,112},{96,64},{112,80},{1... | collective-permute-start | bytes 442376 | tf_op jit(solution)/shard_map/ppermute | solution.py:41
  59.6 8.2 %collective-permute-start.14 = (bf16[96,384]{1,0:T(8,128)(2,1)S(1)}, bf16[96,384]{1,0:T(8,128)(2,1)S(1)}, u32[]{:S(2)}, u32[]{:S(2)}) collective-permute-start(bf16[96,384]{1,0:T(8,128)(2,1)S(1)} %slice.49), channel_id=1, source_target_pairs={{0,16},{16,0},{32,48},{48,32},{64,80},{80,64},{96,112},{112,96},{1... | collective-permute-start | bytes 221192 | tf_op jit(solution)/shard_map/ppermute | solution.py:41
  67.7 0.1 collective-permute-start.22
  67.8 0.8 collective-permute-done.14
  68.7 2.7 %collective-permute-start.17 = (bf16[384,896]{1,0:T(8,128)(2,1)S(1)}, bf16[384,896]{1,0:T(8,128)(2,1)S(1)}, u32[]{:S(2)}, u32[]{:S(2)}) collective-permute-start(bf16[384,896]{1,0:T(8,128)(2,1)S(1)} %collective-permute-done.15.refs_1_), channel_id=1, source_target_pairs={{0,16},{16,0},{32,48},{48,32},{64,80},{80,64},{96,112},{112,96},{1... | collective-permute-start | bytes 2064392 | tf_op jit(solution)/shard_map/ppermute | solution.py:41
  71.6 2.2 %collective-permute-start.23 = (bf16[384,768]{1,0:T(8,128)(2,1)S(1)}, bf16[384,768]{1,0:T(8,128)(2,1)S(1)}, u32[]{:S(2)}, u32[]{:S(2)}) collective-permute-start(bf16[384,768]{1,0:T(8,128)(2,1)S(1)} %collective-permute-done.3.near), channel_id=1, source_target_pairs={{0,16},{16,0},{32,48},{48,32},{64,80},{80,64},{96,112},{112,96},{1... | collective-permute-start | bytes 1769480 | tf_op jit(solution)/shard_map/ppermute | solution.py:41
  73.8 3.7 %collective-permute-done.16 = bf16[96,1536]{1,0:T(8,128)(2,1)S(1)} collective-permute-done((bf16[96,1536]{1,0:T(8,128)(2,1)S(1)}, bf16[96,1536]{1,0:T(8,128)(2,1)S(1)}, u32[]{:S(2)}, u32[]{:S(2)}) %collective-permute-start.16) | collective-permute-done | bytes 294944 | tf_op jit(solution)/shard_map/ppermute | solution.py:390
  77.5 2.0 %collective-permute-start.18 = (bf16[192,1536]{1,0:T(8,128)(2,1)S(1)}, bf16[192,1536]{1,0:T(8,128)(2,1)S(1)}, u32[]{:S(2)}, u32[]{:S(2)}) collective-permute-start(bf16[192,1536]{1,0:T(8,128)(2,1)S(1)} %pad_maximum_fusion.1.low), channel_id=1, source_target_pairs={{0,4},{1,5},{2,6},{3,7},{4,0},{5,1},{6,2},{7,3},{8,12},{9,13},{10,... | collective-permute-start | bytes 1769480 | tf_op jit(solution)/shard_map/ppermute | solution.py:390
  79.5 3.7 %right_root.1.root = bf16[1536,1536]{1,0:T(8,128)(2,1)S(1)} custom-call(s32[10]{0:T(128)S(1)} %stack.43.place, bf16[384,896]{1,0:T(8,128)(2,1)S(1)} %pad_maximum_fusion.refs_0_, bf16[384,896]{1,0:T(8,128)(2,1)S(1)} %collective-permute-done.15.refs_1_, bf16[384,896]{1,0:T(8,128)(2,1)S(1)} %collective-permute-done.22.refs_2_, ...), custom_call_target="tpu_custom_call" | custom-call | flops 17999998976 | bytes 8000000 | tf_op jit(solution)/shard_map/right_root/pallas_call | solution.py:262
  83.2 3.8 %product.2.chip = bf16[768,1536]{1,0:T(8,128)(2,1)S(1)} custom-call(bf16[384,1536]{1,0:T(8,128)(2,1)S(1)} %copy-done, bf16[384,1536]{1,0:T(8,128)(2,1)S(1)} %collective-permute-done.other, bf16[1536,1536]{1,0:T(8,128)(2,1)S(1)} %right_root.1.root), custom_call_target="tpu_custom_call" | custom-call | flops 17999998976 | bytes 9000000 | tf_op jit(solution)/shard_map/product/pallas_call | solution.py:297
  87.0 0.5 collective-permute-done.18.high
  87.5 0.8 left_rows.1
  88.4 3.4 %collective-permute-start.21 = (f32[8,128]{1,0:T(8,128)S(1)}, f32[8,128]{1,0:T(8,128)S(1)}, u32[]{:S(2)}, u32[]{:S(2)}) collective-permute-start(f32[8,128]{1,0:T(8,128)S(1)} %get-tuple-element.40.a), channel_id=1, source_target_pairs={{0,48},{16,32},{32,16},{48,0},{64,112},{80,96},{96,80},{112,64},{1... | collective-permute-start | bytes 12296 | tf_op jit(solution)/shard_map/ppermute | solution.py:41
  91.8 0.4 collective-permute-start.19
  92.3 4.4 %product.3.near = bf16[768,1536]{1,0:T(8,128)(2,1)S(1)} custom-call(s32[10]{0:T(128)S(1)} %stack.43.place, bf16[384,768]{1,0:T(8,128)(2,1)S(1)} %collective-permute-done.3.near, bf16[384,768]{1,0:T(8,128)(2,1)S(1)} %collective-permute-done.12.near_late, bf16[384,768]{1,0:T(8,128)(2,1)S(1)} %collective-permute-done.23.far, ...), custom_call_target="tpu_custom_call" | custom-call | flops 17999998976 | bytes 9000000 | tf_op jit(solution)/shard_map/product/pallas_call | solution.py:297
  96.7 2.1 %precond.1 = (f32[384,1536]{1,0:T(8,128)S(1)}, f32[16,128]{1,0:T(8,128)S(1)}) custom-call(f32[8,128]{1,0:T(8,128)S(1)} %get-tuple-element.40.a, f32[8,128]{1,0:T(8,128)S(1)} %collective-permute-done.19.b, f32[8,128]{1,0:T(8,128)S(1)} %collective-permute-done.20.c, f32[8,128]{1,0:T(8,128)S(1)} %collective-permute-done.21.d, ...), custom_call_target="tpu_custom_call" | custom-call | flops 1800000000 | bytes 8000000 | tf_op jit(solution)/shard_map/precond/pallas_call | solution.py:334
  98.8 1.4 %collective-permute-start.27 = (f32[16,128]{1,0:T(8,128)S(1)}, f32[16,128]{1,0:T(8,128)S(1)}, u32[]{:S(2)}, u32[]{:S(2)}) collective-permute-start(f32[16,128]{1,0:T(8,128)S(1)} %get-tuple-element.43.a), channel_id=1, source_target_pairs={{0,48},{16,32},{32,16},{48,0},{64,112},{80,96},{96,80},{112,64},{1... | collective-permute-start | bytes 24584 | tf_op jit(solution)/shard_map/ppermute | solution.py:41
  100.4 0.7 collective-permute-start.25
  101.1 0.9 collective-permute-done.27.d
  102.0 0.8 collective-permute-done.26.c
  102.8 1.2 %graft.1 = bf16[384,1536]{1,0:T(8,128)(2,1)} custom-call(f32[16,128]{1,0:T(8,128)S(1)} %get-tuple-element.43.a, f32[16,128]{1,0:T(8,128)S(1)} %collective-permute-done.25.b, f32[16,128]{1,0:T(8,128)S(1)} %collective-permute-done.26.c, f32[16,128]{1,0:T(8,128)S(1)} %collective-permute-done.27.d, f32[384,1536]{1,0:T(8,128)S(1)} %get-tuple-element.44.value), custom_call_target="tpu_custom_call" | custom-call | flops 1000000 | bytes 4000000 | tf_op jit(solution)/shard_map/graft/pallas_call | solution.py:362
  (41 shorter events, 1.2 us)
Async XLA Ops:
  0.0 5.9 %copy-start = (bf16[384,1536]{1,0:T(8,128)(2,1)S(1)}, bf16[384,1536]{1,0:T(8,128)(2,1)}, u32[]{:S(2)}) copy-start(bf16[384,1536]{1,0:T(8,128)(2,1)} %mine.7) | copy-start | bytes 3538948
  0.0 5.9 %collective-permute-start = (bf16[384,1536]{1,0:T(8,128)(2,1)}, bf16[384,1536]{1,0:T(8,128)(2,1)S(1)}, u32[]{:S(2)}, u32[]{:S(2)}) collective-permute-start(bf16[384,1536]{1,0:T(8,128)(2,1)} %mine.7), channel_id=1, source_target_pairs={{0,16},{16,0},{32,48},{48,32},{64,80},{80,64},{96,112},{112,96},{1... | collective-permute-start | bytes 3538952 | tf_op jit(solution)/shard_map/ppermute | solution.py:41
  4.3 15.0 %collective-permute-start.3 = (bf16[384,768]{1,0:T(8,128)(2,1)S(1)}, bf16[384,768]{1,0:T(8,128)(2,1)S(1)}, u32[]{:S(2)}, u32[]{:S(2)}) collective-permute-start(bf16[384,768]{1,0:T(8,128)(2,1)S(1)} %constant_dynamic-slice_fusion.1), channel_id=1, source_target_pairs={{0,32},{16,48},{32,0},{48,16},{64,96},{80,112},{96,64},{112,80},{1... | collective-permute-start | bytes 1769480 | tf_op jit(solution)/shard_map/ppermute | solution.py:41
  8.3 14.3 %collective-permute-start.6 = (bf16[384,896]{1,0:T(8,128)(2,1)S(1)}, bf16[384,896]{1,0:T(8,128)(2,1)S(1)}, u32[]{:S(2)}, u32[]{:S(2)}) collective-permute-start(bf16[384,896]{1,0:T(8,128)(2,1)S(1)} %get-tuple-element.33), channel_id=1, source_target_pairs={{0,96},{1,97},{2,98},{3,99},{4,100},{5,101},{6,102},{7,103},{8,104... | collective-permute-start | bytes 2064392 | tf_op jit(solution)/shard_map/ppermute | solution.py:390
  10.4 10.5 %collective-permute-start.1 = (bf16[192,768]{1,0:T(8,128)(2,1)S(1)}, bf16[192,768]{1,0:T(8,128)(2,1)S(1)}, u32[]{:S(2)}, u32[]{:S(2)}) collective-permute-start(bf16[192,768]{1,0:T(8,128)(2,1)S(1)} %get-tuple-element.26), channel_id=1, source_target_pairs={{0,4},{1,5},{2,6},{3,7},{4,0},{5,1},{6,2},{7,3},{8,12},{9,13},{10,... | collective-permute-start | bytes 884744 | tf_op jit(solution)/shard_map/ppermute | solution.py:390
  21.0 4.3 %collective-permute-start.2 = (bf16[96,768]{1,0:T(8,128)(2,1)S(1)}, bf16[96,768]{1,0:T(8,128)(2,1)S(1)}, u32[]{:S(2)}, u32[]{:S(2)}) collective-permute-start(bf16[96,768]{1,0:T(8,128)(2,1)S(1)} %slice.78), channel_id=1, source_target_pairs={{0,12},{1,13},{2,14},{3,15},{4,8},{5,9},{6,10},{7,11},{8,4},{9,5},... | collective-permute-start | bytes 442376 | tf_op jit(solution)/shard_map/ppermute | solution.py:390
  21.1 8.5 %collective-permute-start.4 = (bf16[192,768]{1,0:T(8,128)(2,1)S(1)}, bf16[192,768]{1,0:T(8,128)(2,1)S(1)}, u32[]{:S(2)}, u32[]{:S(2)}) collective-permute-start(bf16[192,768]{1,0:T(8,128)(2,1)S(1)} %get-tuple-element.30), channel_id=1, source_target_pairs={{0,4},{1,5},{2,6},{3,7},{4,0},{5,1},{6,2},{7,3},{8,12},{9,13},{10,... | collective-permute-start | bytes 884744 | tf_op jit(solution)/shard_map/ppermute | solution.py:390
  22.7 7.4 %collective-permute-start.7 = (bf16[192,896]{1,0:T(8,128)(2,1)S(1)}, bf16[192,896]{1,0:T(8,128)(2,1)S(1)}, u32[]{:S(2)}, u32[]{:S(2)}) collective-permute-start(bf16[192,896]{1,0:T(8,128)(2,1)S(1)} %slice.76), channel_id=1, source_target_pairs={{0,128},{1,129},{2,130},{3,131},{4,132},{5,133},{6,134},{7,135},{8... | collective-permute-start | bytes 1032200 | tf_op jit(solution)/shard_map/ppermute | solution.py:390
  29.7 4.1 %collective-permute-start.5 = (bf16[96,768]{1,0:T(8,128)(2,1)S(1)}, bf16[96,768]{1,0:T(8,128)(2,1)S(1)}, u32[]{:S(2)}, u32[]{:S(2)}) collective-permute-start(bf16[96,768]{1,0:T(8,128)(2,1)S(1)} %slice.77), channel_id=1, source_target_pairs={{0,12},{1,13},{2,14},{3,15},{4,8},{5,9},{6,10},{7,11},{8,4},{9,5},... | collective-permute-start | bytes 442376 | tf_op jit(solution)/shard_map/ppermute | solution.py:390
  30.2 9.1 %collective-permute-start.9 = (bf16[192,896]{1,0:T(8,128)(2,1)S(1)}, bf16[192,896]{1,0:T(8,128)(2,1)S(1)}, u32[]{:S(2)}, u32[]{:S(2)}) collective-permute-start(bf16[192,896]{1,0:T(8,128)(2,1)S(1)} %fusion), channel_id=1, source_target_pairs={{0,32},{16,48},{32,0},{48,16},{64,96},{80,112},{96,64},{112,80},{1... | collective-permute-start | bytes 1032200 | tf_op jit(solution)/shard_map/ppermute | solution.py:41
  33.8 11.6 %collective-permute-start.8 = (bf16[96,1536]{1,0:T(8,128)(2,1)S(1)}, bf16[96,1536]{1,0:T(8,128)(2,1)S(1)}, u32[]{:S(2)}, u32[]{:S(2)}) collective-permute-start(bf16[96,1536]{1,0:T(8,128)(2,1)S(1)} %pad_maximum_fusion.2), channel_id=1, source_target_pairs={{0,1},{1,0},{2,3},{3,2},{4,5},{5,4},{6,7},{7,6},{8,9},{9,8},{10,11... | collective-permute-start | bytes 884744 | tf_op jit(solution)/shard_map/ppermute | solution.py:390
  39.4 10.6 %collective-permute-start.11 = (bf16[192,896]{1,0:T(8,128)(2,1)S(1)}, bf16[192,896]{1,0:T(8,128)(2,1)}, u32[]{:S(2)}, u32[]{:S(2)}) collective-permute-start(bf16[192,896]{1,0:T(8,128)(2,1)S(1)} %add_convert_fusion), channel_id=1, source_target_pairs={{0,128},{1,129},{2,130},{3,131},{4,132},{5,133},{6,134},{7,135},{8... | collective-permute-start | bytes 1032200 | tf_op jit(solution)/shard_map/ppermute | solution.py:390
  46.2 10.4 %collective-permute-start.10 = (bf16[96,1536]{1,0:T(8,128)(2,1)}, bf16[96,1536]{1,0:T(8,128)(2,1)}, u32[]{:S(2)}, u32[]{:S(2)}) collective-permute-start(bf16[96,1536]{1,0:T(8,128)(2,1)} %add_convert_fusion.2), channel_id=1, source_target_pairs={{0,3},{1,2},{2,1},{3,0},{4,7},{5,6},{6,5},{7,4},{8,11},{9,10},{10,... | collective-permute-start | bytes 884744 | tf_op jit(solution)/shard_map/ppermute | solution.py:390
  48.7 9.6 %collective-permute-start.12 = (bf16[384,768]{1,0:T(8,128)(2,1)S(1)}, bf16[384,768]{1,0:T(8,128)(2,1)S(1)}, u32[]{:S(2)}, u32[]{:S(2)}) collective-permute-start(bf16[384,768]{1,0:T(8,128)(2,1)S(1)} %constant_dynamic-slice_fusion), channel_id=1, source_target_pairs={{0,32},{16,48},{32,0},{48,16},{64,96},{80,112},{96,64},{112,80},{1... | collective-permute-start | bytes 1769480 | tf_op jit(solution)/shard_map/ppermute | solution.py:41
  51.1 17.6 %collective-permute-start.15 = (bf16[384,896]{1,0:T(8,128)(2,1)S(1)}, bf16[384,896]{1,0:T(8,128)(2,1)S(1)}, u32[]{:S(2)}, u32[]{:S(2)}) collective-permute-start(bf16[384,896]{1,0:T(8,128)(2,1)S(1)} %pad_maximum_fusion.refs_0_), channel_id=1, source_target_pairs={{0,96},{1,97},{2,98},{3,99},{4,100},{5,101},{6,102},{7,103},{8,104... | collective-permute-start | bytes 2064392 | tf_op jit(solution)/shard_map/ppermute | solution.py:390
  58.4 10.3 %collective-permute-start.13 = (bf16[96,768]{1,0:T(8,128)(2,1)S(1)}, bf16[96,768]{1,0:T(8,128)(2,1)S(1)}, u32[]{:S(2)}, u32[]{:S(2)}) collective-permute-start(bf16[96,768]{1,0:T(8,128)(2,1)S(1)} %get-tuple-element.37), channel_id=1, source_target_pairs={{0,32},{16,48},{32,0},{48,16},{64,96},{80,112},{96,64},{112,80},{1... | collective-permute-start | bytes 442376 | tf_op jit(solution)/shard_map/ppermute | solution.py:41
  59.6 9.1 %collective-permute-start.14 = (bf16[96,384]{1,0:T(8,128)(2,1)S(1)}, bf16[96,384]{1,0:T(8,128)(2,1)S(1)}, u32[]{:S(2)}, u32[]{:S(2)}) collective-permute-start(bf16[96,384]{1,0:T(8,128)(2,1)S(1)} %slice.49), channel_id=1, source_target_pairs={{0,16},{16,0},{32,48},{48,32},{64,80},{80,64},{96,112},{112,96},{1... | collective-permute-start | bytes 221192 | tf_op jit(solution)/shard_map/ppermute | solution.py:41
  67.7 11.7 %collective-permute-start.22 = (bf16[384,896]{1,0:T(8,128)(2,1)S(1)}, bf16[384,896]{1,0:T(8,128)(2,1)S(1)}, u32[]{:S(2)}, u32[]{:S(2)}) collective-permute-start(bf16[384,896]{1,0:T(8,128)(2,1)S(1)} %pad_maximum_fusion.refs_0_), channel_id=1, source_target_pairs={{0,16},{16,0},{32,48},{48,32},{64,80},{80,64},{96,112},{112,96},{1... | collective-permute-start | bytes 2064392 | tf_op jit(solution)/shard_map/ppermute | solution.py:41
  68.7 8.8 %collective-permute-start.17 = (bf16[384,896]{1,0:T(8,128)(2,1)S(1)}, bf16[384,896]{1,0:T(8,128)(2,1)S(1)}, u32[]{:S(2)}, u32[]{:S(2)}) collective-permute-start(bf16[384,896]{1,0:T(8,128)(2,1)S(1)} %collective-permute-done.15.refs_1_), channel_id=1, source_target_pairs={{0,16},{16,0},{32,48},{48,32},{64,80},{80,64},{96,112},{112,96},{1... | collective-permute-start | bytes 2064392 | tf_op jit(solution)/shard_map/ppermute | solution.py:41
  71.5 6.0 %collective-permute-start.16 = (bf16[96,1536]{1,0:T(8,128)(2,1)S(1)}, bf16[96,1536]{1,0:T(8,128)(2,1)S(1)}, u32[]{:S(2)}, u32[]{:S(2)}) collective-permute-start(bf16[96,1536]{1,0:T(8,128)(2,1)S(1)} %pad_maximum_fusion.3), channel_id=1, source_target_pairs={{0,12},{1,13},{2,14},{3,15},{4,8},{5,9},{6,10},{7,11},{8,4},{9,5},... | collective-permute-start | bytes 884744 | tf_op jit(solution)/shard_map/ppermute | solution.py:390
  71.6 20.7 %collective-permute-start.23 = (bf16[384,768]{1,0:T(8,128)(2,1)S(1)}, bf16[384,768]{1,0:T(8,128)(2,1)S(1)}, u32[]{:S(2)}, u32[]{:S(2)}) collective-permute-start(bf16[384,768]{1,0:T(8,128)(2,1)S(1)} %collective-permute-done.3.near), channel_id=1, source_target_pairs={{0,16},{16,0},{32,48},{48,32},{64,80},{80,64},{96,112},{112,96},{1... | collective-permute-start | bytes 1769480 | tf_op jit(solution)/shard_map/ppermute | solution.py:41
  73.8 18.5 %collective-permute-start.24 = (bf16[384,768]{1,0:T(8,128)(2,1)S(1)}, bf16[384,768]{1,0:T(8,128)(2,1)S(1)}, u32[]{:S(2)}, u32[]{:S(2)}) collective-permute-start(bf16[384,768]{1,0:T(8,128)(2,1)S(1)} %collective-permute-done.12.near_late), channel_id=1, source_target_pairs={{0,16},{16,0},{32,48},{48,32},{64,80},{80,64},{96,112},{112,96},{1... | collective-permute-start | bytes 1769480 | tf_op jit(solution)/shard_map/ppermute | solution.py:41
  77.5 10.0 %collective-permute-start.18 = (bf16[192,1536]{1,0:T(8,128)(2,1)S(1)}, bf16[192,1536]{1,0:T(8,128)(2,1)S(1)}, u32[]{:S(2)}, u32[]{:S(2)}) collective-permute-start(bf16[192,1536]{1,0:T(8,128)(2,1)S(1)} %pad_maximum_fusion.1.low), channel_id=1, source_target_pairs={{0,4},{1,5},{2,6},{3,7},{4,0},{5,1},{6,2},{7,3},{8,12},{9,13},{10,... | collective-permute-start | bytes 1769480 | tf_op jit(solution)/shard_map/ppermute | solution.py:390
  88.4 8.3 %collective-permute-start.21 = (f32[8,128]{1,0:T(8,128)S(1)}, f32[8,128]{1,0:T(8,128)S(1)}, u32[]{:S(2)}, u32[]{:S(2)}) collective-permute-start(f32[8,128]{1,0:T(8,128)S(1)} %get-tuple-element.40.a), channel_id=1, source_target_pairs={{0,48},{16,32},{32,16},{48,0},{64,112},{80,96},{96,80},{112,64},{1... | collective-permute-start | bytes 12296 | tf_op jit(solution)/shard_map/ppermute | solution.py:41
  91.8 5.0 %collective-permute-start.20 = (f32[8,128]{1,0:T(8,128)S(1)}, f32[8,128]{1,0:T(8,128)S(1)}, u32[]{:S(2)}, u32[]{:S(2)}) collective-permute-start(f32[8,128]{1,0:T(8,128)S(1)} %get-tuple-element.40.a), channel_id=1, source_target_pairs={{0,32},{16,48},{32,0},{48,16},{64,96},{80,112},{96,64},{112,80},{1... | collective-permute-start | bytes 12296 | tf_op jit(solution)/shard_map/ppermute | solution.py:41
  91.8 4.9 %collective-permute-start.19 = (f32[8,128]{1,0:T(8,128)S(1)}, f32[8,128]{1,0:T(8,128)S(1)}, u32[]{:S(2)}, u32[]{:S(2)}) collective-permute-start(f32[8,128]{1,0:T(8,128)S(1)} %get-tuple-element.40.a), channel_id=1, source_target_pairs={{0,16},{16,0},{32,48},{48,32},{64,80},{80,64},{96,112},{112,96},{1... | collective-permute-start | bytes 12296 | tf_op jit(solution)/shard_map/ppermute | solution.py:41
  98.8 3.2 %collective-permute-start.27 = (f32[16,128]{1,0:T(8,128)S(1)}, f32[16,128]{1,0:T(8,128)S(1)}, u32[]{:S(2)}, u32[]{:S(2)}) collective-permute-start(f32[16,128]{1,0:T(8,128)S(1)} %get-tuple-element.43.a), channel_id=1, source_target_pairs={{0,48},{16,32},{32,16},{48,0},{64,112},{80,96},{96,80},{112,64},{1... | collective-permute-start | bytes 24584 | tf_op jit(solution)/shard_map/ppermute | solution.py:41
  100.3 2.5 %collective-permute-start.26 = (f32[16,128]{1,0:T(8,128)S(1)}, f32[16,128]{1,0:T(8,128)S(1)}, u32[]{:S(2)}, u32[]{:S(2)}) collective-permute-start(f32[16,128]{1,0:T(8,128)S(1)} %get-tuple-element.43.a), channel_id=1, source_target_pairs={{0,32},{16,48},{32,0},{48,16},{64,96},{80,112},{96,64},{112,80},{1... | collective-permute-start | bytes 24584 | tf_op jit(solution)/shard_map/ppermute | solution.py:41
  100.4 2.4 %collective-permute-start.25 = (f32[16,128]{1,0:T(8,128)S(1)}, f32[16,128]{1,0:T(8,128)S(1)}, u32[]{:S(2)}, u32[]{:S(2)}) collective-permute-start(f32[16,128]{1,0:T(8,128)S(1)} %get-tuple-element.43.a), channel_id=1, source_target_pairs={{0,16},{16,0},{32,48},{48,32},{64,80},{80,64},{96,112},{112,96},{1... | collective-permute-start | bytes 24584 | tf_op jit(solution)/shard_map/ppermute | solution.py:41

commit v2 on v1

--- a/solution.py
+++ b/solution.py
@@ -108,7 +108,7 @@
             pltpu.VMEM((HALF, BAND * LANE), BF16),
             pltpu.SemaphoreType.DMA((4,)),
         ],
-        compiler_params=params(32),
+        compiler_params=params(16),
         cost_estimate=cost(10**6, 10**4),
         name="right_gram",
     )(place, mine, other)
@@ -129,7 +129,7 @@
         in_specs=[SMEM, VMEM, VMEM],
         out_specs=[VMEM] * 3,
         scratch_shapes=[pltpu.VMEM((ROWS, 2 * ROWS), BF16)],
-        compiler_params=params(24),
+        compiler_params=params(16),
         cost_estimate=cost(10**6, 10**4),
         name="own_gram",
     )(place, mine, other)
@@ -159,7 +159,7 @@
         in_specs=[SMEM] + [VMEM] * 3,
         out_specs=[VMEM] * 2,
         scratch_shapes=[pltpu.VMEM((ROWS, 2 * ROWS), BF16)],
-        compiler_params=params(24),
+        compiler_params=params(16),
         cost_estimate=cost(10**6, 10**4),
         name="cross_gram",
     )(place, mine, other, near)
@@ -196,7 +196,7 @@
         in_specs=[SMEM] + [VMEM] * 2,
         out_specs=[VMEM] * 2,
         scratch_shapes=[pltpu.VMEM((ROWS, 2 * ROWS), BF16)],
-        compiler_params=params(24),
+        compiler_params=params(16),
         cost_estimate=cost(10**6, 2 * 10**6),
         name="left_rows",
     )(place, *parts)
@@ -215,34 +215,37 @@
 def root_kernel(place, *refs):
     parts, (root, packed, sems) = refs[:4], refs[4:]
     core = place[0]
-    copies = []
+    copies, shards = [], []
     for side in range(2):
         for slot in range(4):
             turned = slot if side == 0 or slot in (0, 3) else 3 - slot
-            start = pl.multiple_of((core ^ side) * HALF + place[1 + turned] * RIGHT, 16)
+            shard = place[1 + turned]
+            source = parts[2 * side + slot // 2].at[pl.ds(slot % 2 * RIGHT, RIGHT), :]
+            start = pl.multiple_of((core ^ side) * HALF + shard * RIGHT, 16)
             copies.append(
                 pltpu.make_async_copy(
-                    parts[2 * side + slot // 2].at[pl.ds(slot % 2 * RIGHT, RIGHT), :],
-                    packed.at[pl.ds(start, RIGHT), :],
-                    sems.at[4 * side + slot],
+                    source, packed.at[pl.ds(start, RIGHT), :], sems.at[4 * side + slot]
                 )
             )
+            shards.append((source, shard % 2 * (LANE // 2)))
     for copy in copies:
         copy.start()
-    for copy in copies:
-        copy.wait()
-    shape = (LANE, LANE)
-    eye = lax.broadcasted_iota(jnp.int32, shape, 0) == lax.broadcasted_iota(jnp.int32, shape, 1)
+    row = lax.broadcasted_iota(jnp.int32, (RIGHT, LANE), 0)
+    lane = lax.broadcasted_iota(jnp.int32, (RIGHT, LANE), 1)
     total = jnp.zeros((8, LANE), F32)
-    for row in range(BLOCKS):
-        strip = packed[row * LANE : (row + 1) * LANE, :].astype(F32)
-        head = strip[:, :LANE] + jnp.where(eye, damping, 0.0)
-        tail = strip[:, 6 * LANE :]
-        middle = strip[:, LANE : 6 * LANE]
-        total = total + folded(head * head) + folded(tail * tail) + 2.0 * folded(middle * middle)
+    for source, shift in shards:
+        diagonal = lax.rem(row + shift, LANE) == lane
+        head = source[:, :LANE].astype(F32) + jnp.where(diagonal, damping, 0.0)
+        tail = source[:, 6 * LANE :].astype(F32)
+        middle = source[:, LANE : 6 * LANE].astype(F32)
+        total = total + folded(head * head + tail * tail) + 2.0 * folded(middle * middle)
     scale = scale_of(total)
     factor = 0.25 / jnp.sqrt(jnp.sqrt(scale))
     inverse = 1.0 / scale
+    shape = (LANE, LANE)
+    eye = lax.broadcasted_iota(jnp.int32, shape, 0) == lax.broadcasted_iota(jnp.int32, shape, 1)
+    for copy in copies:
+        copy.wait()
     for row in range(BLOCKS):
         for apart in range(BAND):
             part = packed[row * LANE : (row + 1) * LANE, apart * LANE : (apart + 1) * LANE]
@@ -252,20 +255,21 @@
                 part = part * factor
             else:
                 part = (-part * inverse) * factor
+            part = part.astype(BF16)
             col = (row + apart) % BLOCKS
-            root[row * LANE : (row + 1) * LANE, col * LANE : (col + 1) * LANE] = part.astype(BF16)
+            root[row * LANE : (row + 1) * LANE, col * LANE : (col + 1) * LANE] = part
             if 0 < apart < 6:
-                root[col * LANE : (col + 1) * LANE, row * LANE : (row + 1) * LANE] = part.T.astype(BF16)
+                root[col * LANE : (col + 1) * LANE, row * LANE : (row + 1) * LANE] = part.T
 
 
 def right_root(place, parts):
     return pl.pallas_call(
         root_kernel,
         out_shape=sds((BLOCK, BLOCK), BF16),
-        in_specs=[SMEM] + [ANY] * 4,
+        in_specs=[SMEM] + [VMEM] * 4,
         out_specs=VMEM,
         scratch_shapes=[pltpu.VMEM((BLOCK, BAND * LANE), BF16), pltpu.SemaphoreType.DMA((8,))],
-        compiler_params=params(24),
+        compiler_params=params(16),
         cost_estimate=cost(18 * 10**9, 8 * 10**6),
         name="right_root",
     )(place, *parts)
@@ -300,7 +304,7 @@
         in_specs=[SMEM if ref.ndim == 1 else VMEM for ref in refs],
         out_specs=VMEM,
         scratch_shapes=scratch,
-        compiler_params=params(24),
+        compiler_params=params(16),
         cost_estimate=cost(18 * 10**9, 9 * 10**6),
         name="product",
     )(*refs)
@@ -337,7 +341,7 @@
         in_specs=[VMEM] * 8,
         out_specs=[VMEM] * 2,
         scratch_shapes=[pltpu.VMEM((ROWS, BLOCK), BF16)],
-        compiler_params=params(40),
+        compiler_params=params(16),
         cost_estimate=cost(18 * 10**8, 8 * 10**6),
         name="precond",
     )(*totals, rows, *tiles, grad)
@@ -365,7 +369,7 @@
         in_specs=[VMEM] * 5,
         out_specs=ANY,
         scratch_shapes=[pltpu.VMEM((ROWS, BLOCK), BF16), pltpu.SemaphoreType.DMA((ROWS // GRAFT,))],
-        compiler_params=params(24),
+        compiler_params=params(16),
         cost_estimate=cost(10**6, 4 * 10**6),
         name="graft",
     )(*totals, value)
@@ -377,6 +381,7 @@
 
 CORE, NEAR, FAR, ACROSS = 1, 2, 6, 8
 ROUND = ((FAR, ACROSS), (ACROSS, FAR))
+BACK = ROUND
 UP = ((4, 12), (12, 4))
 DEEP = ((1, 3), (3, 1))
 
@@ -385,7 +390,7 @@
     pairs = []
     for device in range(256):
         mask = masks[device // 16 % 2][at]
-        mask = mask * 16 if masks is ROUND else mask
+        mask = mask * 16 if masks in (ROUND, BACK) else mask
         pairs.append((device, device ^ mask))
     return lax.ppermute(value, ("row", "col"), pairs)
 
@@ -409,11 +414,11 @@
     came = hop(after(mine, *tokens), "row", NEAR)
     mine = total_of(mine, came).astype(BF16)
     tokens = yield came
-    came = turned(after(mine, *tokens), ROUND, 1)
+    came = turned(after(mine, *tokens), BACK, 1)
     low = jnp.concatenate([mine, came], axis=0)
     tokens = yield came
     low = after(low, *tokens)
-    high = turned(low, ROUND, 0)
+    high = turned(low, BACK, 0)
     low_other = hop(low, "row", CORE)
     tokens = yield high
     high_other = hop(after(high, *tokens), "row", CORE)
@@ -446,15 +451,16 @@
     core = hop(mine[:, ROWS:], "row", CORE)
     first = total_of(mine[:, :ROWS], near[:, :ROWS]).astype(BF16)
     second = total_of(core, near[:, ROWS:]).astype(BF16)
-    return near, jnp.concatenate([first, second], axis=1)
+    return [near, core], jnp.concatenate([first, second], axis=1)
 
 
 def gather_steps(mine):
     tokens = yield
-    came = turned(after(mine, *tokens), UP, 1)
-    low = jnp.concatenate([mine, came], axis=0)
+    mine = after(mine, *tokens)
+    came = turned(mine, UP, 1)
     tokens = yield came
-    high = turned(after(low, *tokens), UP, 0)
+    low = jnp.concatenate([after(mine, *tokens), came], axis=0)
+    high = turned(low, UP, 0)
     yield high
     yield [low, high]
 
@@ -482,7 +488,7 @@
     c1 = crosses.send([o1])
     o2 = owns.send([])
     r2 = rights.send([])
-    c2 = crosses.send([o2])
+    c2 = crosses.send([o2, r1])
     r3 = rights.send([])
     own, cross = next(owns), next(crosses)
     deep = begun(deep_steps(jnp.concatenate([own, cross], axis=1)))
@@ -497,20 +503,20 @@
     c5, cross = pair_step(both[:, 2 * ROWS :], [r4, near_late])
     gather = begun(gather_steps(jnp.concatenate([both[:, : 2 * ROWS], cross], axis=1)))
     c6 = gather.send([r5])
-    r6 = rights.send([])
+    r6 = rights.send(c5)
     parts = next(rights)
     root = right_root(place, parts)
-    c7 = gather.send([r6])
+    c7 = gather.send([root])
+    far = hop(after(near, root), "row", CORE)
+    far_late = hop(after(near_late, root), "row", CORE)
     sides = next(gather)
-    far = hop(near, "row", CORE)
-    far_late = hop(near_late, "row", CORE)
-    rows, square = left_rows(place, sides)
-    totals = spread(square)
     scratch = [pltpu.VMEM((2, ROWS, BLOCK), BF16)]
     tiles = [
         product(chip_product_kernel, [], gradient, other, root),
         product(near_product_kernel, scratch, place, near, near_late, far, far_late, root),
     ]
+    rows, square = left_rows(place, after(sides, *tiles))
+    totals = spread(square)
     value, square = precond(totals, rows, tiles, grad)
     return graft(spread(square), value)
 

time: 104 us -> 102 us (0.981)
  starting transfers between devices: 46.6 us -> 44.3 us
    ppermute x12, waiting for transfers between devices: 19.5 us -> 15.9 us  [turned(): return lax.ppermute(value, ('row', 'col'), pairs)]
    ppermute x16, waiting for transfers between devices: 10.7 us -> 14.2 us  [hop(): return lax.ppermute(value, axis, [(i, i ^ mask) for i in range(16)])]
    ppermute x16, starting transfers between devices: 25.5 us -> 23.2 us  [hop(): return lax.ppermute(value, axis, [(i, i ^ mask) for i in range(16)])]
  transfers between devices with their start and end apart: 28 -> 28, of which waited for: 13 -> 15; matrix products, arithmetic and copies ran while one was open for 5% -> 5% of each run, Pallas kernels for 18% -> 18%
where the time goes in v2:
time: 102 us
  starting transfers between devices  44.3 us (43%)
  waiting for transfers between devices  30 us (29%)
  Pallas kernels  22 us (22%)
  other arithmetic  3.48 us (3%)
  local copies, waits for them, and re-layouts  1.38 us (1%)
    ppermute x16, starting transfers between devices, hop(): return lax.ppermute(value, axis, [(i, i ^ mask) for i in range(16)])  23.2 us
    ppermute x12, starting transfers between devices, turned(): return lax.ppermute(value, ('row', 'col'), pairs)  21.1 us
    ppermute x12, waiting for transfers between devices, turned(): return lax.ppermute(value, ('row', 'col'), pairs)  15.9 us
    ppermute x16, waiting for transfers between devices, hop(): return lax.ppermute(value, axis, [(i, i ^ mask) for i in range(16)])  14.2 us
    pallas_call x2, Pallas kernels, product(): pl.pallas_call(kernel, out_shape=sds((2 * ROWS, BLOCK), BF16), in_specs=[...  8.24 us
    pallas_call x1, Pallas kernels, right_root(): pl.pallas_call(root_kernel, out_shape=sds((BLOCK, BLOCK), BF16), in_specs...  3.68 us
    pallas_call x1, Pallas kernels, right_gram(): pl.pallas_call(right_kernel, out_shape=[sds((2 * RIGHT, BAND * LANE), BF1...  2.35 us
    pallas_call x1, Pallas kernels, precond(): pl.pallas_call(precond_kernel, out_shape=[sds((ROWS, BLOCK), F32), sds((1...  2.14 us
  transfers between devices with their start and end apart: 28, of which 15 were waited for; matrix products, arithmetic and copies ran while one was open for 5% of the time, Pallas kernels for 18%

profile of v2, /device:TPU:1, one launch (start us, length us, event | category | flops | bytes accessed | tf_op | source)
XLA Modules:
  0.0 101.7 jit_solution(2664967678571346111)
XLA Ops:
  0.0 3.2 %collective-permute-start = (bf16[384,1536]{1,0:T(8,128)(2,1)}, bf16[384,1536]{1,0:T(8,128)(2,1)S(1)}, u32[]{:S(2)}, u32[]{:S(2)}) collective-permute-start(bf16[384,1536]{1,0:T(8,128)(2,1)} %mine.7), channel_id=1, source_target_pairs={{0,16},{16,0},{32,48},{48,32},{64,80},{80,64},{96,112},{112,96},{1... | collective-permute-start | bytes 3538952 | tf_op jit(solution)/shard_map/ppermute | solution.py:41
  3.2 1.1 %constant_dynamic-slice_fusion.1 = bf16[384,768]{1,0:T(8,128)(2,1)S(1)} fusion(bf16[384,1536]{1,0:T(8,128)(2,1)} %mine.7, s32[]{:T(128)S(6)} %select_n.41), kind=kLoop, calls=%fused_computation.23 | loop fusion | bytes 1179652 | tf_op jit(solution)/shard_map/dynamic_slice | solution.py:481
  4.6 1.3 %collective-permute-done.other = bf16[384,1536]{1,0:T(8,128)(2,1)S(1)} collective-permute-done((bf16[384,1536]{1,0:T(8,128)(2,1)}, bf16[384,1536]{1,0:T(8,128)(2,1)S(1)}, u32[]{:S(2)}, u32[]{:S(2)}) %collective-permute-start) | collective-permute-done | bytes 1179680 | tf_op jit(solution)/shard_map/ppermute | solution.py:41
  5.9 2.3 %right_gram.1 = (bf16[384,896]{1,0:T(8,128)(2,1)S(1)}, bf16[384,896]{1,0:T(8,128)(2,1)S(1)}) custom-call(s32[10]{0:T(128)S(1)} %stack.43.place, bf16[384,1536]{1,0:T(8,128)(2,1)S(1)} %copy-done, bf16[384,1536]{1,0:T(8,128)(2,1)S(1)} %collective-permute-done.other), custom_call_target="tpu_custom_call" | custom-call | flops 1000000 | bytes 10000 | tf_op jit(solution)/shard_map/right_gram/pallas_call | solution.py:101
  8.4 2.0 %own_gram.1 = (bf16[192,768]{1,0:T(8,128)(2,1)S(1)}, bf16[192,768]{1,0:T(8,128)(2,1)S(1)}, f32[8,128]{1,0:T(8,128)S(1)}) custom-call(s32[10]{0:T(128)S(1)} %stack.43.place, bf16[384,1536]{1,0:T(8,128)(2,1)S(1)} %copy-done, bf16[384,1536]{1,0:T(8,128)(2,1)S(1)} %collective-permute-done.other), custom_call_target="tpu_custom_call" | custom-call | flops 1000000 | bytes 10000 | tf_op jit(solution)/shard_map/own_gram/pallas_call | solution.py:126
  10.4 2.7 %collective-permute-start.1 = (bf16[192,768]{1,0:T(8,128)(2,1)S(1)}, bf16[192,768]{1,0:T(8,128)(2,1)S(1)}, u32[]{:S(2)}, u32[]{:S(2)}) collective-permute-start(bf16[192,768]{1,0:T(8,128)(2,1)S(1)} %get-tuple-element.31), channel_id=1, source_target_pairs={{0,4},{1,5},{2,6},{3,7},{4,0},{5,1},{6,2},{7,3},{8,12},{9,13},{10,... | collective-permute-start | bytes 884744 | tf_op jit(solution)/shard_map/ppermute | solution.py:395
  13.1 6.3 %collective-permute-done.3.near = bf16[384,768]{1,0:T(8,128)(2,1)S(1)} collective-permute-done((bf16[384,768]{1,0:T(8,128)(2,1)S(1)}, bf16[384,768]{1,0:T(8,128)(2,1)S(1)}, u32[]{:S(2)}, u32[]{:S(2)}) %collective-permute-start.3) | collective-permute-done | bytes 589856 | tf_op jit(solution)/shard_map/ppermute | solution.py:41
  19.3 1.6 %cross_gram.1 = (bf16[192,768]{1,0:T(8,128)(2,1)S(1)}, bf16[192,768]{1,0:T(8,128)(2,1)S(1)}) custom-call(s32[10]{0:T(128)S(1)} %stack.43.place, bf16[384,1536]{1,0:T(8,128)(2,1)S(1)} %copy-done, bf16[384,1536]{1,0:T(8,128)(2,1)S(1)} %collective-permute-done.other, bf16[384,768]{1,0:T(8,128)(2,1)S(1)} %collective-permute-done.3.near), custom_call_target="tpu_custom_call" | custom-call | flops 1000000 | bytes 10000 | tf_op jit(solution)/shard_map/cross_gram/pallas_call | solution.py:156
  21.1 1.4 %collective-permute-start.4 = (bf16[192,768]{1,0:T(8,128)(2,1)S(1)}, bf16[192,768]{1,0:T(8,128)(2,1)S(1)}, u32[]{:S(2)}, u32[]{:S(2)}) collective-permute-start(bf16[192,768]{1,0:T(8,128)(2,1)S(1)} %get-tuple-element.35), channel_id=1, source_target_pairs={{0,4},{1,5},{2,6},{3,7},{4,0},{5,1},{6,2},{7,3},{8,12},{9,13},{10,... | collective-permute-start | bytes 884744 | tf_op jit(solution)/shard_map/ppermute | solution.py:395
  22.7 2.6 %collective-permute-start.7 = (bf16[192,896]{1,0:T(8,128)(2,1)S(1)}, bf16[192,896]{1,0:T(8,128)(2,1)S(1)}, u32[]{:S(2)}, u32[]{:S(2)}) collective-permute-start(bf16[192,896]{1,0:T(8,128)(2,1)S(1)} %slice.76), channel_id=1, source_target_pairs={{0,128},{1,129},{2,130},{3,131},{4,132},{5,133},{6,134},{7,135},{8... | collective-permute-start | bytes 1032200 | tf_op jit(solution)/shard_map/ppermute | solution.py:395
  25.4 4.2 %collective-permute-done.4 = bf16[192,768]{1,0:T(8,128)(2,1)S(1)} collective-permute-done((bf16[192,768]{1,0:T(8,128)(2,1)S(1)}, bf16[192,768]{1,0:T(8,128)(2,1)S(1)}, u32[]{:S(2)}, u32[]{:S(2)}) %collective-permute-start.4) | collective-permute-done | bytes 294944 | tf_op jit(solution)/shard_map/ppermute | solution.py:395
  29.8 0.4 collective-permute-done.7
  30.2 0.4 collective-permute-start.9
  30.6 3.1 %collective-permute-done.6 = bf16[96,768]{1,0:T(8,128)(2,1)S(1)} collective-permute-done((bf16[96,768]{1,0:T(8,128)(2,1)S(1)}, bf16[96,768]{1,0:T(8,128)(2,1)S(1)}, u32[]{:S(2)}, u32[]{:S(2)}) %collective-permute-start.6) | collective-permute-done | bytes 147488 | tf_op jit(solution)/shard_map/ppermute | solution.py:395
  33.8 5.6 %collective-permute-start.8 = (bf16[96,1536]{1,0:T(8,128)(2,1)S(1)}, bf16[96,1536]{1,0:T(8,128)(2,1)S(1)}, u32[]{:S(2)}, u32[]{:S(2)}) collective-permute-start(bf16[96,1536]{1,0:T(8,128)(2,1)S(1)} %pad_maximum_fusion.1), channel_id=1, source_target_pairs={{0,1},{1,0},{2,3},{3,2},{4,5},{5,4},{6,7},{7,6},{8,9},{9,8},{10,11... | collective-permute-start | bytes 884744 | tf_op jit(solution)/shard_map/ppermute | solution.py:395
  39.4 2.6 %collective-permute-start.11 = (bf16[192,896]{1,0:T(8,128)(2,1)S(1)}, bf16[192,896]{1,0:T(8,128)(2,1)}, u32[]{:S(2)}, u32[]{:S(2)}) collective-permute-start(bf16[192,896]{1,0:T(8,128)(2,1)S(1)} %add_convert_fusion), channel_id=1, source_target_pairs={{0,128},{1,129},{2,130},{3,131},{4,132},{5,133},{6,134},{7,135},{8... | collective-permute-start | bytes 1032200 | tf_op jit(solution)/shard_map/ppermute | solution.py:395
  42.0 3.4 %collective-permute-done.8 = bf16[96,1536]{1,0:T(8,128)(2,1)S(1)} collective-permute-done((bf16[96,1536]{1,0:T(8,128)(2,1)S(1)}, bf16[96,1536]{1,0:T(8,128)(2,1)S(1)}, u32[]{:S(2)}, u32[]{:S(2)}) %collective-permute-start.8) | collective-permute-done | bytes 294944 | tf_op jit(solution)/shard_map/ppermute | solution.py:395
  45.4 0.8 add_convert_fusion.2
  46.2 2.5 %collective-permute-start.10 = (bf16[96,1536]{1,0:T(8,128)(2,1)}, bf16[96,1536]{1,0:T(8,128)(2,1)}, u32[]{:S(2)}, u32[]{:S(2)}) collective-permute-start(bf16[96,1536]{1,0:T(8,128)(2,1)} %add_convert_fusion.2), channel_id=1, source_target_pairs={{0,3},{1,2},{2,1},{3,0},{4,7},{5,6},{6,5},{7,4},{8,11},{9,10},{10,... | collective-permute-start | bytes 884744 | tf_op jit(solution)/shard_map/ppermute | solution.py:395
  48.7 1.3 %collective-permute-start.12 = (bf16[384,768]{1,0:T(8,128)(2,1)S(1)}, bf16[384,768]{1,0:T(8,128)(2,1)S(1)}, u32[]{:S(2)}, u32[]{:S(2)}) collective-permute-start(bf16[384,768]{1,0:T(8,128)(2,1)S(1)} %constant_dynamic-slice_fusion), channel_id=1, source_target_pairs={{0,32},{16,48},{32,0},{48,16},{64,96},{80,112},{96,64},{112,80},{1... | collective-permute-start | bytes 1769480 | tf_op jit(solution)/shard_map/ppermute | solution.py:41
  50.0 1.0 %pad_maximum_fusion.refs_0_ = bf16[384,896]{1,0:T(8,128)(2,1)S(1)} fusion(bf16[192,896]{1,0:T(8,128)(2,1)} %collective-permute-done.11, bf16[192,896]{1,0:T(8,128)(2,1)S(1)} %add_convert_fusion), kind=kLoop, calls=%fused_computation.4 | loop fusion | flops 1376256 | bytes 1376256 | tf_op jit(solution)/shard_map/concatenate | solution.py:418
  51.1 1.4 %collective-permute-start.15 = (bf16[384,896]{1,0:T(8,128)(2,1)S(1)}, bf16[384,896]{1,0:T(8,128)(2,1)S(1)}, u32[]{:S(2)}, u32[]{:S(2)}) collective-permute-start(bf16[384,896]{1,0:T(8,128)(2,1)S(1)} %pad_maximum_fusion.refs_0_), channel_id=1, source_target_pairs={{0,96},{1,97},{2,98},{3,99},{4,100},{5,101},{6,102},{7,103},{8,104... | collective-permute-start | bytes 2064392 | tf_op jit(solution)/shard_map/ppermute | solution.py:395
  52.4 4.2 %collective-permute-done.10 = bf16[96,1536]{1,0:T(8,128)(2,1)} collective-permute-done((bf16[96,1536]{1,0:T(8,128)(2,1)}, bf16[96,1536]{1,0:T(8,128)(2,1)}, u32[]{:S(2)}, u32[]{:S(2)}) %collective-permute-start.10) | collective-permute-done | bytes 294944 | tf_op jit(solution)/shard_map/ppermute | solution.py:395
  56.6 1.1 %add_convert_fusion.1 = bf16[96,1536]{1,0:T(8,128)(2,1)S(1)} fusion(bf16[96,1536]{1,0:T(8,128)(2,1)} %collective-permute-done.10, bf16[96,1536]{1,0:T(8,128)(2,1)} %add_convert_fusion.2), kind=kLoop, calls=%fused_computation.6 | loop fusion | flops 589824 | bytes 884736 | tf_op jit(solution)/shard_map/convert_element_type | solution.py:443
  57.8 0.6 collective-permute-done.12.near_late
  58.4 1.2 %collective-permute-start.13 = (bf16[96,768]{1,0:T(8,128)(2,1)S(1)}, bf16[96,768]{1,0:T(8,128)(2,1)S(1)}, u32[]{:S(2)}, u32[]{:S(2)}) collective-permute-start(bf16[96,768]{1,0:T(8,128)(2,1)S(1)} %get-tuple-element.42), channel_id=1, source_target_pairs={{0,32},{16,48},{32,0},{48,16},{64,96},{80,112},{96,64},{112,80},{1... | collective-permute-start | bytes 442376 | tf_op jit(solution)/shard_map/ppermute | solution.py:41
  59.6 8.2 %collective-permute-start.14 = (bf16[96,384]{1,0:T(8,128)(2,1)S(1)}, bf16[96,384]{1,0:T(8,128)(2,1)S(1)}, u32[]{:S(2)}, u32[]{:S(2)}) collective-permute-start(bf16[96,384]{1,0:T(8,128)(2,1)S(1)} %slice.49), channel_id=1, source_target_pairs={{0,16},{16,0},{32,48},{48,32},{64,80},{80,64},{96,112},{112,96},{1... | collective-permute-start | bytes 221192 | tf_op jit(solution)/shard_map/ppermute | solution.py:41
  67.8 0.8 collective-permute-done.14
  68.7 2.6 %collective-permute-start.17 = (bf16[384,896]{1,0:T(8,128)(2,1)S(1)}, bf16[384,896]{1,0:T(8,128)(2,1)S(1)}, u32[]{:S(2)}, u32[]{:S(2)}) collective-permute-start(bf16[384,896]{1,0:T(8,128)(2,1)S(1)} %collective-permute-done.15.refs_1_), channel_id=1, source_target_pairs={{0,16},{16,0},{32,48},{48,32},{64,80},{80,64},{96,112},{112,96},{1... | collective-permute-start | bytes 2064392 | tf_op jit(solution)/shard_map/ppermute | solution.py:41
  71.5 1.6 %collective-permute-done.17.refs_3_ = bf16[384,896]{1,0:T(8,128)(2,1)S(1)} collective-permute-done((bf16[384,896]{1,0:T(8,128)(2,1)S(1)}, bf16[384,896]{1,0:T(8,128)(2,1)S(1)}, u32[]{:S(2)}, u32[]{:S(2)}) %collective-permute-start.17) | collective-permute-done | bytes 688160 | tf_op jit(solution)/shard_map/ppermute | solution.py:41
  73.1 3.7 %right_root.1.root = bf16[1536,1536]{1,0:T(8,128)(2,1)S(1)} custom-call(s32[10]{0:T(128)S(1)} %stack.43.place, bf16[384,896]{1,0:T(8,128)(2,1)S(1)} %pad_maximum_fusion.refs_0_, bf16[384,896]{1,0:T(8,128)(2,1)S(1)} %collective-permute-done.15.refs_1_, bf16[384,896]{1,0:T(8,128)(2,1)S(1)} %collective-permute-done.16.refs_2_, ...), custom_call_target="tpu_custom_call" | custom-call | flops 17999998976 | bytes 8000000 | tf_op jit(solution)/shard_map/right_root/pallas_call | solution.py:266
  76.8 0.5 collective-permute-done.18
  77.3 2.0 %collective-permute-start.19 = (bf16[192,1536]{1,0:T(8,128)(2,1)S(1)}, bf16[192,1536]{1,0:T(8,128)(2,1)S(1)}, u32[]{:S(2)}, u32[]{:S(2)}) collective-permute-start(bf16[192,1536]{1,0:T(8,128)(2,1)S(1)} %constant_dynamic-update-slice_fusion.low), channel_id=1, source_target_pairs={{0,4},{1,5},{2,6},{3,7},{4,0},{5,1},{6,2},{7,3},{8,12},{9,13},{10,... | collective-permute-start | bytes 1769480 | tf_op jit(solution)/shard_map/ppermute | solution.py:395
  79.3 0.3 collective-permute-start.20
  79.9 3.8 %product.2.chip = bf16[768,1536]{1,0:T(8,128)(2,1)S(1)} custom-call(bf16[384,1536]{1,0:T(8,128)(2,1)S(1)} %copy-done, bf16[384,1536]{1,0:T(8,128)(2,1)S(1)} %collective-permute-done.other, bf16[1536,1536]{1,0:T(8,128)(2,1)S(1)} %right_root.1.root), custom_call_target="tpu_custom_call" | custom-call | flops 17999998976 | bytes 9000000 | tf_op jit(solution)/shard_map/product/pallas_call | solution.py:301
  83.7 4.4 %product.3.near = bf16[768,1536]{1,0:T(8,128)(2,1)S(1)} custom-call(s32[10]{0:T(128)S(1)} %stack.43.place, bf16[384,768]{1,0:T(8,128)(2,1)S(1)} %collective-permute-done.3.near, bf16[384,768]{1,0:T(8,128)(2,1)S(1)} %collective-permute-done.12.near_late, bf16[384,768]{1,0:T(8,128)(2,1)S(1)} %collective-permute-done.20.far, ...), custom_call_target="tpu_custom_call" | custom-call | flops 17999998976 | bytes 9000000 | tf_op jit(solution)/shard_map/product/pallas_call | solution.py:301
  88.1 0.8 left_rows.1
  89.0 2.6 %collective-permute-start.24 = (f32[8,128]{1,0:T(8,128)S(1)}, f32[8,128]{1,0:T(8,128)S(1)}, u32[]{:S(2)}, u32[]{:S(2)}) collective-permute-start(f32[8,128]{1,0:T(8,128)S(1)} %get-tuple-element.50.a), channel_id=1, source_target_pairs={{0,48},{16,32},{32,16},{48,0},{64,112},{80,96},{96,80},{112,64},{1... | collective-permute-start | bytes 12296 | tf_op jit(solution)/shard_map/ppermute | solution.py:41
  91.7 0.7 collective-permute-start.22
  92.3 0.6 collective-permute-done.24.d
  93.0 1.1 %collective-permute-done.23.c = f32[8,128]{1,0:T(8,128)S(1)} collective-permute-done((f32[8,128]{1,0:T(8,128)S(1)}, f32[8,128]{1,0:T(8,128)S(1)}, u32[]{:S(2)}, u32[]{:S(2)}) %collective-permute-start.23) | collective-permute-done | bytes 4128 | tf_op jit(solution)/shard_map/ppermute | solution.py:41
  94.1 2.1 %precond.1 = (f32[384,1536]{1,0:T(8,128)S(1)}, f32[16,128]{1,0:T(8,128)S(1)}) custom-call(f32[8,128]{1,0:T(8,128)S(1)} %get-tuple-element.50.a, f32[8,128]{1,0:T(8,128)S(1)} %collective-permute-done.22.b, f32[8,128]{1,0:T(8,128)S(1)} %collective-permute-done.23.c, f32[8,128]{1,0:T(8,128)S(1)} %collective-permute-done.24.d, ...), custom_call_target="tpu_custom_call" | custom-call | flops 1800000000 | bytes 8000000 | tf_op jit(solution)/shard_map/precond/pallas_call | solution.py:338
  96.3 1.5 %collective-permute-start.27 = (f32[16,128]{1,0:T(8,128)S(1)}, f32[16,128]{1,0:T(8,128)S(1)}, u32[]{:S(2)}, u32[]{:S(2)}) collective-permute-start(f32[16,128]{1,0:T(8,128)S(1)} %get-tuple-element.53.a), channel_id=1, source_target_pairs={{0,48},{16,32},{32,16},{48,0},{64,112},{80,96},{96,80},{112,64},{1... | collective-permute-start | bytes 24584 | tf_op jit(solution)/shard_map/ppermute | solution.py:41
  97.8 0.3 collective-permute-start.26
  98.1 0.4 collective-permute-start.25
  98.5 0.9 collective-permute-done.27.d
  99.4 0.9 collective-permute-done.26.c
  100.3 1.2 %graft.1 = bf16[384,1536]{1,0:T(8,128)(2,1)} custom-call(f32[16,128]{1,0:T(8,128)S(1)} %get-tuple-element.53.a, f32[16,128]{1,0:T(8,128)S(1)} %collective-permute-done.25.b, f32[16,128]{1,0:T(8,128)S(1)} %collective-permute-done.26.c, f32[16,128]{1,0:T(8,128)S(1)} %collective-permute-done.27.d, f32[384,1536]{1,0:T(8,128)S(1)} %get-tuple-element.54.value), custom_call_target="tpu_custom_call" | custom-call | flops 1000000 | bytes 4000000 | tf_op jit(solution)/shard_map/graft/pallas_call | solution.py:366
  (42 shorter events, 1.7 us)
Async XLA Ops:
  0.0 5.9 %copy-start = (bf16[384,1536]{1,0:T(8,128)(2,1)S(1)}, bf16[384,1536]{1,0:T(8,128)(2,1)}, u32[]{:S(2)}) copy-start(bf16[384,1536]{1,0:T(8,128)(2,1)} %mine.7) | copy-start | bytes 3538948
  0.0 5.9 %collective-permute-start = (bf16[384,1536]{1,0:T(8,128)(2,1)}, bf16[384,1536]{1,0:T(8,128)(2,1)S(1)}, u32[]{:S(2)}, u32[]{:S(2)}) collective-permute-start(bf16[384,1536]{1,0:T(8,128)(2,1)} %mine.7), channel_id=1, source_target_pairs={{0,16},{16,0},{32,48},{48,32},{64,80},{80,64},{96,112},{112,96},{1... | collective-permute-start | bytes 3538952 | tf_op jit(solution)/shard_map/ppermute | solution.py:41
  4.3 15.0 %collective-permute-start.3 = (bf16[384,768]{1,0:T(8,128)(2,1)S(1)}, bf16[384,768]{1,0:T(8,128)(2,1)S(1)}, u32[]{:S(2)}, u32[]{:S(2)}) collective-permute-start(bf16[384,768]{1,0:T(8,128)(2,1)S(1)} %constant_dynamic-slice_fusion.1), channel_id=1, source_target_pairs={{0,32},{16,48},{32,0},{48,16},{64,96},{80,112},{96,64},{112,80},{1... | collective-permute-start | bytes 1769480 | tf_op jit(solution)/shard_map/ppermute | solution.py:41
  8.3 14.3 %collective-permute-start.5 = (bf16[384,896]{1,0:T(8,128)(2,1)S(1)}, bf16[384,896]{1,0:T(8,128)(2,1)S(1)}, u32[]{:S(2)}, u32[]{:S(2)}) collective-permute-start(bf16[384,896]{1,0:T(8,128)(2,1)S(1)} %get-tuple-element.36), channel_id=1, source_target_pairs={{0,96},{1,97},{2,98},{3,99},{4,100},{5,101},{6,102},{7,103},{8,104... | collective-permute-start | bytes 2064392 | tf_op jit(solution)/shard_map/ppermute | solution.py:395
  10.4 10.5 %collective-permute-start.1 = (bf16[192,768]{1,0:T(8,128)(2,1)S(1)}, bf16[192,768]{1,0:T(8,128)(2,1)S(1)}, u32[]{:S(2)}, u32[]{:S(2)}) collective-permute-start(bf16[192,768]{1,0:T(8,128)(2,1)S(1)} %get-tuple-element.31), channel_id=1, source_target_pairs={{0,4},{1,5},{2,6},{3,7},{4,0},{5,1},{6,2},{7,3},{8,12},{9,13},{10,... | collective-permute-start | bytes 884744 | tf_op jit(solution)/shard_map/ppermute | solution.py:395
  21.0 4.3 %collective-permute-start.2 = (bf16[96,768]{1,0:T(8,128)(2,1)S(1)}, bf16[96,768]{1,0:T(8,128)(2,1)S(1)}, u32[]{:S(2)}, u32[]{:S(2)}) collective-permute-start(bf16[96,768]{1,0:T(8,128)(2,1)S(1)} %slice.78), channel_id=1, source_target_pairs={{0,12},{1,13},{2,14},{3,15},{4,8},{5,9},{6,10},{7,11},{8,4},{9,5},... | collective-permute-start | bytes 442376 | tf_op jit(solution)/shard_map/ppermute | solution.py:395
  21.1 8.5 %collective-permute-start.4 = (bf16[192,768]{1,0:T(8,128)(2,1)S(1)}, bf16[192,768]{1,0:T(8,128)(2,1)S(1)}, u32[]{:S(2)}, u32[]{:S(2)}) collective-permute-start(bf16[192,768]{1,0:T(8,128)(2,1)S(1)} %get-tuple-element.35), channel_id=1, source_target_pairs={{0,4},{1,5},{2,6},{3,7},{4,0},{5,1},{6,2},{7,3},{8,12},{9,13},{10,... | collective-permute-start | bytes 884744 | tf_op jit(solution)/shard_map/ppermute | solution.py:395
  22.7 7.4 %collective-permute-start.7 = (bf16[192,896]{1,0:T(8,128)(2,1)S(1)}, bf16[192,896]{1,0:T(8,128)(2,1)S(1)}, u32[]{:S(2)}, u32[]{:S(2)}) collective-permute-start(bf16[192,896]{1,0:T(8,128)(2,1)S(1)} %slice.76), channel_id=1, source_target_pairs={{0,128},{1,129},{2,130},{3,131},{4,132},{5,133},{6,134},{7,135},{8... | collective-permute-start | bytes 1032200 | tf_op jit(solution)/shard_map/ppermute | solution.py:395
  29.7 4.1 %collective-permute-start.6 = (bf16[96,768]{1,0:T(8,128)(2,1)S(1)}, bf16[96,768]{1,0:T(8,128)(2,1)S(1)}, u32[]{:S(2)}, u32[]{:S(2)}) collective-permute-start(bf16[96,768]{1,0:T(8,128)(2,1)S(1)} %slice.77), channel_id=1, source_target_pairs={{0,12},{1,13},{2,14},{3,15},{4,8},{5,9},{6,10},{7,11},{8,4},{9,5},... | collective-permute-start | bytes 442376 | tf_op jit(solution)/shard_map/ppermute | solution.py:395
  30.2 9.1 %collective-permute-start.9 = (bf16[192,896]{1,0:T(8,128)(2,1)S(1)}, bf16[192,896]{1,0:T(8,128)(2,1)S(1)}, u32[]{:S(2)}, u32[]{:S(2)}) collective-permute-start(bf16[192,896]{1,0:T(8,128)(2,1)S(1)} %fusion), channel_id=1, source_target_pairs={{0,32},{16,48},{32,0},{48,16},{64,96},{80,112},{96,64},{112,80},{1... | collective-permute-start | bytes 1032200 | tf_op jit(solution)/shard_map/ppermute | solution.py:41
  33.8 11.6 %collective-permute-start.8 = (bf16[96,1536]{1,0:T(8,128)(2,1)S(1)}, bf16[96,1536]{1,0:T(8,128)(2,1)S(1)}, u32[]{:S(2)}, u32[]{:S(2)}) collective-permute-start(bf16[96,1536]{1,0:T(8,128)(2,1)S(1)} %pad_maximum_fusion.1), channel_id=1, source_target_pairs={{0,1},{1,0},{2,3},{3,2},{4,5},{5,4},{6,7},{7,6},{8,9},{9,8},{10,11... | collective-permute-start | bytes 884744 | tf_op jit(solution)/shard_map/ppermute | solution.py:395
  39.4 10.6 %collective-permute-start.11 = (bf16[192,896]{1,0:T(8,128)(2,1)S(1)}, bf16[192,896]{1,0:T(8,128)(2,1)}, u32[]{:S(2)}, u32[]{:S(2)}) collective-permute-start(bf16[192,896]{1,0:T(8,128)(2,1)S(1)} %add_convert_fusion), channel_id=1, source_target_pairs={{0,128},{1,129},{2,130},{3,131},{4,132},{5,133},{6,134},{7,135},{8... | collective-permute-start | bytes 1032200 | tf_op jit(solution)/shard_map/ppermute | solution.py:395
  46.2 10.4 %collective-permute-start.10 = (bf16[96,1536]{1,0:T(8,128)(2,1)}, bf16[96,1536]{1,0:T(8,128)(2,1)}, u32[]{:S(2)}, u32[]{:S(2)}) collective-permute-start(bf16[96,1536]{1,0:T(8,128)(2,1)} %add_convert_fusion.2), channel_id=1, source_target_pairs={{0,3},{1,2},{2,1},{3,0},{4,7},{5,6},{6,5},{7,4},{8,11},{9,10},{10,... | collective-permute-start | bytes 884744 | tf_op jit(solution)/shard_map/ppermute | solution.py:395
  48.7 9.6 %collective-permute-start.12 = (bf16[384,768]{1,0:T(8,128)(2,1)S(1)}, bf16[384,768]{1,0:T(8,128)(2,1)S(1)}, u32[]{:S(2)}, u32[]{:S(2)}) collective-permute-start(bf16[384,768]{1,0:T(8,128)(2,1)S(1)} %constant_dynamic-slice_fusion), channel_id=1, source_target_pairs={{0,32},{16,48},{32,0},{48,16},{64,96},{80,112},{96,64},{112,80},{1... | collective-permute-start | bytes 1769480 | tf_op jit(solution)/shard_map/ppermute | solution.py:41
  51.1 17.6 %collective-permute-start.15 = (bf16[384,896]{1,0:T(8,128)(2,1)S(1)}, bf16[384,896]{1,0:T(8,128)(2,1)S(1)}, u32[]{:S(2)}, u32[]{:S(2)}) collective-permute-start(bf16[384,896]{1,0:T(8,128)(2,1)S(1)} %pad_maximum_fusion.refs_0_), channel_id=1, source_target_pairs={{0,96},{1,97},{2,98},{3,99},{4,100},{5,101},{6,102},{7,103},{8,104... | collective-permute-start | bytes 2064392 | tf_op jit(solution)/shard_map/ppermute | solution.py:395
  58.4 10.3 %collective-permute-start.13 = (bf16[96,768]{1,0:T(8,128)(2,1)S(1)}, bf16[96,768]{1,0:T(8,128)(2,1)S(1)}, u32[]{:S(2)}, u32[]{:S(2)}) collective-permute-start(bf16[96,768]{1,0:T(8,128)(2,1)S(1)} %get-tuple-element.42), channel_id=1, source_target_pairs={{0,32},{16,48},{32,0},{48,16},{64,96},{80,112},{96,64},{112,80},{1... | collective-permute-start | bytes 442376 | tf_op jit(solution)/shard_map/ppermute | solution.py:41
  59.6 9.1 %collective-permute-start.14 = (bf16[96,384]{1,0:T(8,128)(2,1)S(1)}, bf16[96,384]{1,0:T(8,128)(2,1)S(1)}, u32[]{:S(2)}, u32[]{:S(2)}) collective-permute-start(bf16[96,384]{1,0:T(8,128)(2,1)S(1)} %slice.49), channel_id=1, source_target_pairs={{0,16},{16,0},{32,48},{48,32},{64,80},{80,64},{96,112},{112,96},{1... | collective-permute-start | bytes 221192 | tf_op jit(solution)/shard_map/ppermute | solution.py:41
  67.7 3.7 %collective-permute-start.16 = (bf16[384,896]{1,0:T(8,128)(2,1)S(1)}, bf16[384,896]{1,0:T(8,128)(2,1)S(1)}, u32[]{:S(2)}, u32[]{:S(2)}) collective-permute-start(bf16[384,896]{1,0:T(8,128)(2,1)S(1)} %pad_maximum_fusion.refs_0_), channel_id=1, source_target_pairs={{0,16},{16,0},{32,48},{48,32},{64,80},{80,64},{96,112},{112,96},{1... | collective-permute-start | bytes 2064392 | tf_op jit(solution)/shard_map/ppermute | solution.py:41
  68.7 4.4 %collective-permute-start.17 = (bf16[384,896]{1,0:T(8,128)(2,1)S(1)}, bf16[384,896]{1,0:T(8,128)(2,1)S(1)}, u32[]{:S(2)}, u32[]{:S(2)}) collective-permute-start(bf16[384,896]{1,0:T(8,128)(2,1)S(1)} %collective-permute-done.15.refs_1_), channel_id=1, source_target_pairs={{0,16},{16,0},{32,48},{48,32},{64,80},{80,64},{96,112},{112,96},{1... | collective-permute-start | bytes 2064392 | tf_op jit(solution)/shard_map/ppermute | solution.py:41
  71.4 6.0 %collective-permute-start.18 = (bf16[96,1536]{1,0:T(8,128)(2,1)S(1)}, bf16[96,1536]{1,0:T(8,128)(2,1)S(1)}, u32[]{:S(2)}, u32[]{:S(2)}) collective-permute-start(bf16[96,1536]{1,0:T(8,128)(2,1)S(1)} %pad_maximum_fusion.2), channel_id=1, source_target_pairs={{0,12},{1,13},{2,14},{3,15},{4,8},{5,9},{6,10},{7,11},{8,4},{9,5},... | collective-permute-start | bytes 884744 | tf_op jit(solution)/shard_map/ppermute | solution.py:395
  77.3 10.8 %collective-permute-start.19 = (bf16[192,1536]{1,0:T(8,128)(2,1)S(1)}, bf16[192,1536]{1,0:T(8,128)(2,1)S(1)}, u32[]{:S(2)}, u32[]{:S(2)}) collective-permute-start(bf16[192,1536]{1,0:T(8,128)(2,1)S(1)} %constant_dynamic-update-slice_fusion.low), channel_id=1, source_target_pairs={{0,4},{1,5},{2,6},{3,7},{4,0},{5,1},{6,2},{7,3},{8,12},{9,13},{10,... | collective-permute-start | bytes 1769480 | tf_op jit(solution)/shard_map/ppermute | solution.py:395
  79.3 4.3 %collective-permute-start.20 = (bf16[384,768]{1,0:T(8,128)(2,1)S(1)}, bf16[384,768]{1,0:T(8,128)(2,1)S(1)}, u32[]{:S(2)}, u32[]{:S(2)}) collective-permute-start(bf16[384,768]{1,0:T(8,128)(2,1)S(1)} %collective-permute-done.3.near), channel_id=1, source_target_pairs={{0,16},{16,0},{32,48},{48,32},{64,80},{80,64},{96,112},{112,96},{1... | collective-permute-start | bytes 1769480 | tf_op jit(solution)/shard_map/ppermute | solution.py:41
  79.6 4.1 %collective-permute-start.21 = (bf16[384,768]{1,0:T(8,128)(2,1)S(1)}, bf16[384,768]{1,0:T(8,128)(2,1)S(1)}, u32[]{:S(2)}, u32[]{:S(2)}) collective-permute-start(bf16[384,768]{1,0:T(8,128)(2,1)S(1)} %collective-permute-done.12.near_late), channel_id=1, source_target_pairs={{0,16},{16,0},{32,48},{48,32},{64,80},{80,64},{96,112},{112,96},{1... | collective-permute-start | bytes 1769480 | tf_op jit(solution)/shard_map/ppermute | solution.py:41
  89.0 4.0 %collective-permute-start.24 = (f32[8,128]{1,0:T(8,128)S(1)}, f32[8,128]{1,0:T(8,128)S(1)}, u32[]{:S(2)}, u32[]{:S(2)}) collective-permute-start(f32[8,128]{1,0:T(8,128)S(1)} %get-tuple-element.50.a), channel_id=1, source_target_pairs={{0,48},{16,32},{32,16},{48,0},{64,112},{80,96},{96,80},{112,64},{1... | collective-permute-start | bytes 12296 | tf_op jit(solution)/shard_map/ppermute | solution.py:41
  91.6 2.5 %collective-permute-start.23 = (f32[8,128]{1,0:T(8,128)S(1)}, f32[8,128]{1,0:T(8,128)S(1)}, u32[]{:S(2)}, u32[]{:S(2)}) collective-permute-start(f32[8,128]{1,0:T(8,128)S(1)} %get-tuple-element.50.a), channel_id=1, source_target_pairs={{0,32},{16,48},{32,0},{48,16},{64,96},{80,112},{96,64},{112,80},{1... | collective-permute-start | bytes 12296 | tf_op jit(solution)/shard_map/ppermute | solution.py:41
  91.7 2.4 %collective-permute-start.22 = (f32[8,128]{1,0:T(8,128)S(1)}, f32[8,128]{1,0:T(8,128)S(1)}, u32[]{:S(2)}, u32[]{:S(2)}) collective-permute-start(f32[8,128]{1,0:T(8,128)S(1)} %get-tuple-element.50.a), channel_id=1, source_target_pairs={{0,16},{16,0},{32,48},{48,32},{64,80},{80,64},{96,112},{112,96},{1... | collective-permute-start | bytes 12296 | tf_op jit(solution)/shard_map/ppermute | solution.py:41
  96.3 3.2 %collective-permute-start.27 = (f32[16,128]{1,0:T(8,128)S(1)}, f32[16,128]{1,0:T(8,128)S(1)}, u32[]{:S(2)}, u32[]{:S(2)}) collective-permute-start(f32[16,128]{1,0:T(8,128)S(1)} %get-tuple-element.53.a), channel_id=1, source_target_pairs={{0,48},{16,32},{32,16},{48,0},{64,112},{80,96},{96,80},{112,64},{1... | collective-permute-start | bytes 24584 | tf_op jit(solution)/shard_map/ppermute | solution.py:41
  97.8 2.5 %collective-permute-start.26 = (f32[16,128]{1,0:T(8,128)S(1)}, f32[16,128]{1,0:T(8,128)S(1)}, u32[]{:S(2)}, u32[]{:S(2)}) collective-permute-start(f32[16,128]{1,0:T(8,128)S(1)} %get-tuple-element.53.a), channel_id=1, source_target_pairs={{0,32},{16,48},{32,0},{48,16},{64,96},{80,112},{96,64},{112,80},{1... | collective-permute-start | bytes 24584 | tf_op jit(solution)/shard_map/ppermute | solution.py:41
  98.1 2.2 %collective-permute-start.25 = (f32[16,128]{1,0:T(8,128)S(1)}, f32[16,128]{1,0:T(8,128)S(1)}, u32[]{:S(2)}, u32[]{:S(2)}) collective-permute-start(f32[16,128]{1,0:T(8,128)S(1)} %get-tuple-element.53.a), channel_id=1, source_target_pairs={{0,16},{16,0},{32,48},{48,32},{64,80},{80,64},{96,112},{112,96},{1... | collective-permute-start | bytes 24584 | tf_op jit(solution)/shard_map/ppermute | solution.py:41

commit v3 on v2

--- a/solution.py
+++ b/solution.py
@@ -165,12 +165,12 @@
     )(place, mine, other, near)
 
 
-def left_rows_kernel(place, low, high, rows_out, square_out, cross):
+def left_rows_kernel(place, own_low, own_high, cross_low, cross_high, rows_out, square_out, cross):
     for slot in range(4):
         rows = pl.ds(pl.multiple_of(place[5 + slot] * LEFT, 16), LEFT)
         span = slice(slot % 2 * LEFT, slot % 2 * LEFT + LEFT)
-        rows_out[rows, : 2 * ROWS] = (low, high)[slot // 2][span, : 2 * ROWS]
-        cross[rows, :] = (low, high)[slot // 2][span, 2 * ROWS :]
+        rows_out[rows, : 2 * ROWS] = (own_low, own_high)[slot // 2][span, :]
+        cross[rows, :] = (cross_low, cross_high)[slot // 2][span, :]
 
     @pl.when(place[9] == 0)
     def _():
@@ -193,7 +193,7 @@
     return pl.pallas_call(
         left_rows_kernel,
         out_shape=[sds((ROWS, BLOCK), BF16), sds((8, LANE), F32)],
-        in_specs=[SMEM] + [VMEM] * 2,
+        in_specs=[SMEM] + [VMEM] * 4,
         out_specs=[VMEM] * 2,
         scratch_shapes=[pltpu.VMEM((ROWS, 2 * ROWS), BF16)],
         compiler_params=params(16),
@@ -501,21 +501,24 @@
     late = lax.dynamic_slice(after(gradient, r3), (0, upper * HALF), (ROWS, HALF))
     near_late = hop(late, "row", NEAR)
     c5, cross = pair_step(both[:, 2 * ROWS :], [r4, near_late])
-    gather = begun(gather_steps(jnp.concatenate([both[:, : 2 * ROWS], cross], axis=1)))
-    c6 = gather.send([r5])
-    r6 = rights.send(c5)
+    gather = begun(gather_steps(both[:, : 2 * ROWS]))
+    o5 = gather.send([])
+    cross_gather = begun(gather_steps(cross))
+    c6 = cross_gather.send([r5])
+    o6 = gather.send([])
+    r6 = rights.send([*c5, o5])
     parts = next(rights)
     root = right_root(place, parts)
-    c7 = gather.send([root])
+    c7 = cross_gather.send([root])
     far = hop(after(near, root), "row", CORE)
     far_late = hop(after(near_late, root), "row", CORE)
-    sides = next(gather)
+    sides = next(gather) + next(cross_gather)
     scratch = [pltpu.VMEM((2, ROWS, BLOCK), BF16)]
     tiles = [
         product(chip_product_kernel, [], gradient, other, root),
         product(near_product_kernel, scratch, place, near, near_late, far, far_late, root),
     ]
-    rows, square = left_rows(place, after(sides, *tiles))
+    rows, square = left_rows(place, after(sides, tiles[0]))
     totals = spread(square)
     value, square = precond(totals, rows, tiles, grad)
     return graft(spread(square), value)

time: 102 us -> 102 us (level)
  starting transfers between devices: 44.3 us -> 45.4 us
    ppermute x16, waiting for transfers between devices: 14.2 us -> 10.1 us  [hop(): return lax.ppermute(value, axis, [(i, i ^ mask) for i in range(16)])]
    ppermute x12 -> x14, waiting for transfers between devices: 15.9 us -> 19 us  [turned(): return lax.ppermute(value, ('row', 'col'), pairs)]
    ppermute x12 -> x14, starting transfers between devices: 21.1 us -> 22.9 us  [turned(): return lax.ppermute(value, ('row', 'col'), pairs)]
  transfers between devices with their start and end apart: 28 -> 30, of which waited for: 15 -> 12; matrix products, arithmetic and copies ran while one was open for 5% -> 5% of each run, Pallas kernels for 18% -> 18%
where the time goes in v3:
time: 102 us
  starting transfers between devices  45.4 us (45%)
  waiting for transfers between devices  29.1 us (29%)
  Pallas kernels  21.9 us (21%)
  other arithmetic  3.49 us (3%)
  local copies, waits for them, and re-layouts  1.36 us (1%)
    ppermute x14, starting transfers between devices, turned(): return lax.ppermute(value, ('row', 'col'), pairs)  22.9 us
    ppermute x16, starting transfers between devices, hop(): return lax.ppermute(value, axis, [(i, i ^ mask) for i in range(16)])  22.6 us
    ppermute x14, waiting for transfers between devices, turned(): return lax.ppermute(value, ('row', 'col'), pairs)  19 us
    ppermute x16, waiting for transfers between devices, hop(): return lax.ppermute(value, axis, [(i, i ^ mask) for i in range(16)])  10.1 us
    pallas_call x2, Pallas kernels, product(): pl.pallas_call(kernel, out_shape=sds((2 * ROWS, BLOCK), BF16), in_specs=[...  8.21 us
    pallas_call x1, Pallas kernels, right_root(): pl.pallas_call(root_kernel, out_shape=sds((BLOCK, BLOCK), BF16), in_specs...  3.68 us
    pallas_call x1, Pallas kernels, right_gram(): pl.pallas_call(right_kernel, out_shape=[sds((2 * RIGHT, BAND * LANE), BF1...  2.35 us
    pallas_call x1, Pallas kernels, precond(): pl.pallas_call(precond_kernel, out_shape=[sds((ROWS, BLOCK), F32), sds((1...  2.11 us
  transfers between devices with their start and end apart: 30, of which 12 were waited for; matrix products, arithmetic and copies ran while one was open for 5% of the time, Pallas kernels for 18%

profile of v3, /device:TPU:1, one launch (start us, length us, event | category | flops | bytes accessed | tf_op | source)
XLA Modules:
  0.0 101.9 jit_solution(13739568267526734857)
XLA Ops:
  0.0 3.2 %collective-permute-start = (bf16[384,1536]{1,0:T(8,128)(2,1)}, bf16[384,1536]{1,0:T(8,128)(2,1)S(1)}, u32[]{:S(2)}, u32[]{:S(2)}) collective-permute-start(bf16[384,1536]{1,0:T(8,128)(2,1)} %mine.7), channel_id=1, source_target_pairs={{0,16},{16,0},{32,48},{48,32},{64,80},{80,64},{96,112},{112,96},{1... | collective-permute-start | bytes 3538952 | tf_op jit(solution)/shard_map/ppermute | solution.py:41
  3.2 1.1 %constant_dynamic-slice_fusion.1 = bf16[384,768]{1,0:T(8,128)(2,1)S(1)} fusion(bf16[384,1536]{1,0:T(8,128)(2,1)} %mine.7, s32[]{:T(128)S(6)} %select_n.41), kind=kLoop, calls=%fused_computation.24 | loop fusion | bytes 1179652 | tf_op jit(solution)/shard_map/dynamic_slice | solution.py:481
  4.6 1.3 %collective-permute-done.other = bf16[384,1536]{1,0:T(8,128)(2,1)S(1)} collective-permute-done((bf16[384,1536]{1,0:T(8,128)(2,1)}, bf16[384,1536]{1,0:T(8,128)(2,1)S(1)}, u32[]{:S(2)}, u32[]{:S(2)}) %collective-permute-start) | collective-permute-done | bytes 1179680 | tf_op jit(solution)/shard_map/ppermute | solution.py:41
  5.9 2.3 %right_gram.1 = (bf16[384,896]{1,0:T(8,128)(2,1)S(1)}, bf16[384,896]{1,0:T(8,128)(2,1)S(1)}) custom-call(s32[10]{0:T(128)S(1)} %stack.43.place, bf16[384,1536]{1,0:T(8,128)(2,1)S(1)} %copy-done, bf16[384,1536]{1,0:T(8,128)(2,1)S(1)} %collective-permute-done.other), custom_call_target="tpu_custom_call" | custom-call | flops 1000000 | bytes 10000 | tf_op jit(solution)/shard_map/right_gram/pallas_call | solution.py:101
  8.4 2.0 %own_gram.1 = (bf16[192,768]{1,0:T(8,128)(2,1)S(1)}, bf16[192,768]{1,0:T(8,128)(2,1)S(1)}, f32[8,128]{1,0:T(8,128)S(1)}) custom-call(s32[10]{0:T(128)S(1)} %stack.43.place, bf16[384,1536]{1,0:T(8,128)(2,1)S(1)} %copy-done, bf16[384,1536]{1,0:T(8,128)(2,1)S(1)} %collective-permute-done.other), custom_call_target="tpu_custom_call" | custom-call | flops 1000000 | bytes 10000 | tf_op jit(solution)/shard_map/own_gram/pallas_call | solution.py:126
  10.4 2.7 %collective-permute-start.1 = (bf16[192,768]{1,0:T(8,128)(2,1)S(1)}, bf16[192,768]{1,0:T(8,128)(2,1)S(1)}, u32[]{:S(2)}, u32[]{:S(2)}) collective-permute-start(bf16[192,768]{1,0:T(8,128)(2,1)S(1)} %get-tuple-element.33), channel_id=1, source_target_pairs={{0,4},{1,5},{2,6},{3,7},{4,0},{5,1},{6,2},{7,3},{8,12},{9,13},{10,... | collective-permute-start | bytes 884744 | tf_op jit(solution)/shard_map/ppermute | solution.py:395
  13.1 6.3 %collective-permute-done.3.near = bf16[384,768]{1,0:T(8,128)(2,1)S(1)} collective-permute-done((bf16[384,768]{1,0:T(8,128)(2,1)S(1)}, bf16[384,768]{1,0:T(8,128)(2,1)S(1)}, u32[]{:S(2)}, u32[]{:S(2)}) %collective-permute-start.3) | collective-permute-done | bytes 589856 | tf_op jit(solution)/shard_map/ppermute | solution.py:41
  19.3 1.6 %cross_gram.1 = (bf16[192,768]{1,0:T(8,128)(2,1)S(1)}, bf16[192,768]{1,0:T(8,128)(2,1)S(1)}) custom-call(s32[10]{0:T(128)S(1)} %stack.43.place, bf16[384,1536]{1,0:T(8,128)(2,1)S(1)} %copy-done, bf16[384,1536]{1,0:T(8,128)(2,1)S(1)} %collective-permute-done.other, bf16[384,768]{1,0:T(8,128)(2,1)S(1)} %collective-permute-done.3.near), custom_call_target="tpu_custom_call" | custom-call | flops 1000000 | bytes 10000 | tf_op jit(solution)/shard_map/cross_gram/pallas_call | solution.py:156
  21.1 1.4 %collective-permute-start.4 = (bf16[192,768]{1,0:T(8,128)(2,1)S(1)}, bf16[192,768]{1,0:T(8,128)(2,1)S(1)}, u32[]{:S(2)}, u32[]{:S(2)}) collective-permute-start(bf16[192,768]{1,0:T(8,128)(2,1)S(1)} %get-tuple-element.37), channel_id=1, source_target_pairs={{0,4},{1,5},{2,6},{3,7},{4,0},{5,1},{6,2},{7,3},{8,12},{9,13},{10,... | collective-permute-start | bytes 884744 | tf_op jit(solution)/shard_map/ppermute | solution.py:395
  22.6 0.1 convert_add_fusion
  22.7 2.6 %collective-permute-start.7 = (bf16[192,896]{1,0:T(8,128)(2,1)S(1)}, bf16[192,896]{1,0:T(8,128)(2,1)S(1)}, u32[]{:S(2)}, u32[]{:S(2)}) collective-permute-start(bf16[192,896]{1,0:T(8,128)(2,1)S(1)} %slice.76), channel_id=1, source_target_pairs={{0,128},{1,129},{2,130},{3,131},{4,132},{5,133},{6,134},{7,135},{8... | collective-permute-start | bytes 1032200 | tf_op jit(solution)/shard_map/ppermute | solution.py:395
  25.4 4.2 %collective-permute-done.4 = bf16[192,768]{1,0:T(8,128)(2,1)S(1)} collective-permute-done((bf16[192,768]{1,0:T(8,128)(2,1)S(1)}, bf16[192,768]{1,0:T(8,128)(2,1)S(1)}, u32[]{:S(2)}, u32[]{:S(2)}) %collective-permute-start.4) | collective-permute-done | bytes 294944 | tf_op jit(solution)/shard_map/ppermute | solution.py:395
  29.8 0.4 collective-permute-done.7
  30.2 0.4 collective-permute-start.9
  30.6 3.1 %collective-permute-done.6 = bf16[96,768]{1,0:T(8,128)(2,1)S(1)} collective-permute-done((bf16[96,768]{1,0:T(8,128)(2,1)S(1)}, bf16[96,768]{1,0:T(8,128)(2,1)S(1)}, u32[]{:S(2)}, u32[]{:S(2)}) %collective-permute-start.6) | collective-permute-done | bytes 147488 | tf_op jit(solution)/shard_map/ppermute | solution.py:395
  33.8 5.6 %collective-permute-start.8 = (bf16[96,1536]{1,0:T(8,128)(2,1)S(1)}, bf16[96,1536]{1,0:T(8,128)(2,1)S(1)}, u32[]{:S(2)}, u32[]{:S(2)}) collective-permute-start(bf16[96,1536]{1,0:T(8,128)(2,1)S(1)} %pad_maximum_fusion.1), channel_id=1, source_target_pairs={{0,1},{1,0},{2,3},{3,2},{4,5},{5,4},{6,7},{7,6},{8,9},{9,8},{10,11... | collective-permute-start | bytes 884744 | tf_op jit(solution)/shard_map/ppermute | solution.py:395
  39.4 2.6 %collective-permute-start.13 = (bf16[192,896]{1,0:T(8,128)(2,1)S(1)}, bf16[192,896]{1,0:T(8,128)(2,1)}, u32[]{:S(2)}, u32[]{:S(2)}) collective-permute-start(bf16[192,896]{1,0:T(8,128)(2,1)S(1)} %add_convert_fusion), channel_id=1, source_target_pairs={{0,128},{1,129},{2,130},{3,131},{4,132},{5,133},{6,134},{7,135},{8... | collective-permute-start | bytes 1032200 | tf_op jit(solution)/shard_map/ppermute | solution.py:395
  42.0 3.4 %collective-permute-done.8 = bf16[96,1536]{1,0:T(8,128)(2,1)S(1)} collective-permute-done((bf16[96,1536]{1,0:T(8,128)(2,1)S(1)}, bf16[96,1536]{1,0:T(8,128)(2,1)S(1)}, u32[]{:S(2)}, u32[]{:S(2)}) %collective-permute-start.8) | collective-permute-done | bytes 294944 | tf_op jit(solution)/shard_map/ppermute | solution.py:395
  45.4 0.8 add_convert_fusion.2
  46.2 2.5 %collective-permute-start.10 = (bf16[96,1536]{1,0:T(8,128)(2,1)}, bf16[96,1536]{1,0:T(8,128)(2,1)}, u32[]{:S(2)}, u32[]{:S(2)}) collective-permute-start(bf16[96,1536]{1,0:T(8,128)(2,1)} %add_convert_fusion.2), channel_id=1, source_target_pairs={{0,3},{1,2},{2,1},{3,0},{4,7},{5,6},{6,5},{7,4},{8,11},{9,10},{10,... | collective-permute-start | bytes 884744 | tf_op jit(solution)/shard_map/ppermute | solution.py:395
  48.7 1.3 %collective-permute-start.14 = (bf16[384,768]{1,0:T(8,128)(2,1)S(1)}, bf16[384,768]{1,0:T(8,128)(2,1)S(1)}, u32[]{:S(2)}, u32[]{:S(2)}) collective-permute-start(bf16[384,768]{1,0:T(8,128)(2,1)S(1)} %constant_dynamic-slice_fusion), channel_id=1, source_target_pairs={{0,32},{16,48},{32,0},{48,16},{64,96},{80,112},{96,64},{112,80},{1... | collective-permute-start | bytes 1769480 | tf_op jit(solution)/shard_map/ppermute | solution.py:41
  50.0 1.0 %pad_maximum_fusion.refs_0_ = bf16[384,896]{1,0:T(8,128)(2,1)S(1)} fusion(bf16[192,896]{1,0:T(8,128)(2,1)} %collective-permute-done.13, bf16[192,896]{1,0:T(8,128)(2,1)S(1)} %add_convert_fusion), kind=kLoop, calls=%fused_computation.4 | loop fusion | flops 1376256 | bytes 1376256 | tf_op jit(solution)/shard_map/concatenate | solution.py:418
  51.1 1.4 %collective-permute-start.17 = (bf16[384,896]{1,0:T(8,128)(2,1)S(1)}, bf16[384,896]{1,0:T(8,128)(2,1)S(1)}, u32[]{:S(2)}, u32[]{:S(2)}) collective-permute-start(bf16[384,896]{1,0:T(8,128)(2,1)S(1)} %pad_maximum_fusion.refs_0_), channel_id=1, source_target_pairs={{0,96},{1,97},{2,98},{3,99},{4,100},{5,101},{6,102},{7,103},{8,104... | collective-permute-start | bytes 2064392 | tf_op jit(solution)/shard_map/ppermute | solution.py:395
  52.4 4.2 %collective-permute-done.10 = bf16[96,1536]{1,0:T(8,128)(2,1)} collective-permute-done((bf16[96,1536]{1,0:T(8,128)(2,1)}, bf16[96,1536]{1,0:T(8,128)(2,1)}, u32[]{:S(2)}, u32[]{:S(2)}) %collective-permute-start.10) | collective-permute-done | bytes 294944 | tf_op jit(solution)/shard_map/ppermute | solution.py:395
  56.6 1.1 %add_convert_fusion.1 = bf16[96,1536]{1,0:T(8,128)(2,1)S(1)} fusion(bf16[96,1536]{1,0:T(8,128)(2,1)} %collective-permute-done.10, bf16[96,1536]{1,0:T(8,128)(2,1)} %add_convert_fusion.2), kind=kLoop, calls=%fused_computation.6 | loop fusion | flops 589824 | bytes 884736 | tf_op jit(solution)/shard_map/convert_element_type | solution.py:443
  57.8 1.0 %collective-permute-start.11 = (bf16[96,768]{1,0:T(8,128)(2,1)S(1)}, bf16[96,768]{1,0:T(8,128)(2,1)S(1)}, u32[]{:S(2)}, u32[]{:S(2)}) collective-permute-start(bf16[96,768]{1,0:T(8,128)(2,1)S(1)} %get-tuple-element.60), channel_id=1, source_target_pairs={{0,12},{1,13},{2,14},{3,15},{4,8},{5,9},{6,10},{7,11},{8,4},{9,5},... | collective-permute-start | bytes 442376 | tf_op jit(solution)/shard_map/ppermute | solution.py:395
  58.8 1.2 %collective-permute-start.15 = (bf16[96,768]{1,0:T(8,128)(2,1)S(1)}, bf16[96,768]{1,0:T(8,128)(2,1)S(1)}, u32[]{:S(2)}, u32[]{:S(2)}) collective-permute-start(bf16[96,768]{1,0:T(8,128)(2,1)S(1)} %get-tuple-element.44), channel_id=1, source_target_pairs={{0,32},{16,48},{32,0},{48,16},{64,96},{80,112},{96,64},{112,80},{1... | collective-permute-start | bytes 442376 | tf_op jit(solution)/shard_map/ppermute | solution.py:41
  60.0 8.5 %collective-permute-start.16 = (bf16[96,384]{1,0:T(8,128)(2,1)S(1)}, bf16[96,384]{1,0:T(8,128)(2,1)S(1)}, u32[]{:S(2)}, u32[]{:S(2)}) collective-permute-start(bf16[96,384]{1,0:T(8,128)(2,1)S(1)} %slice.49), channel_id=1, source_target_pairs={{0,16},{16,0},{32,48},{48,32},{64,80},{80,64},{96,112},{112,96},{1... | collective-permute-start | bytes 221192 | tf_op jit(solution)/shard_map/ppermute | solution.py:41
  68.6 0.8 collective-permute-done.16
  69.4 2.5 %collective-permute-start.19 = (bf16[384,896]{1,0:T(8,128)(2,1)S(1)}, bf16[384,896]{1,0:T(8,128)(2,1)S(1)}, u32[]{:S(2)}, u32[]{:S(2)}) collective-permute-start(bf16[384,896]{1,0:T(8,128)(2,1)S(1)} %collective-permute-done.17.refs_1_), channel_id=1, source_target_pairs={{0,16},{16,0},{32,48},{48,32},{64,80},{80,64},{96,112},{112,96},{1... | collective-permute-start | bytes 2064392 | tf_op jit(solution)/shard_map/ppermute | solution.py:41
  71.9 1.7 %collective-permute-start.12 = (bf16[192,768]{1,0:T(8,128)(2,1)S(1)}, bf16[192,768]{1,0:T(8,128)(2,1)S(1)}, u32[]{:S(2)}, u32[]{:S(2)}) collective-permute-start(bf16[192,768]{1,0:T(8,128)(2,1)S(1)} %pad_maximum_fusion.2.own_low), channel_id=1, source_target_pairs={{0,4},{1,5},{2,6},{3,7},{4,0},{5,1},{6,2},{7,3},{8,12},{9,13},{10,... | collective-permute-start | bytes 884744 | tf_op jit(solution)/shard_map/ppermute | solution.py:395
  73.8 3.7 %right_root.1.root = bf16[1536,1536]{1,0:T(8,128)(2,1)S(1)} custom-call(s32[10]{0:T(128)S(1)} %stack.43.place, bf16[384,896]{1,0:T(8,128)(2,1)S(1)} %pad_maximum_fusion.refs_0_, bf16[384,896]{1,0:T(8,128)(2,1)S(1)} %collective-permute-done.17.refs_1_, bf16[384,896]{1,0:T(8,128)(2,1)S(1)} %collective-permute-done.18.refs_2_, ...), custom_call_target="tpu_custom_call" | custom-call | flops 17999998976 | bytes 8000000 | tf_op jit(solution)/shard_map/right_root/pallas_call | solution.py:266
  77.5 2.2 %collective-permute-done.20 = bf16[96,768]{1,0:T(8,128)(2,1)S(1)} collective-permute-done((bf16[96,768]{1,0:T(8,128)(2,1)S(1)}, bf16[96,768]{1,0:T(8,128)(2,1)S(1)}, u32[]{:S(2)}, u32[]{:S(2)}) %collective-permute-start.20) | collective-permute-done | bytes 147488 | tf_op jit(solution)/shard_map/ppermute | solution.py:395
  79.7 1.0 %collective-permute-start.21 = (bf16[192,768]{1,0:T(8,128)(2,1)S(1)}, bf16[192,768]{1,0:T(8,128)(2,1)S(1)}, u32[]{:S(2)}, u32[]{:S(2)}) collective-permute-start(bf16[192,768]{1,0:T(8,128)(2,1)S(1)} %constant_dynamic-update-slice_fusion.cross_low), channel_id=1, source_target_pairs={{0,4},{1,5},{2,6},{3,7},{4,0},{5,1},{6,2},{7,3},{8,12},{9,13},{10,... | collective-permute-start | bytes 884744 | tf_op jit(solution)/shard_map/ppermute | solution.py:395
  80.7 0.5 collective-permute-start.26
  81.2 3.8 %product.2.chip = bf16[768,1536]{1,0:T(8,128)(2,1)S(1)} custom-call(bf16[384,1536]{1,0:T(8,128)(2,1)S(1)} %copy-done, bf16[384,1536]{1,0:T(8,128)(2,1)S(1)} %collective-permute-done.other, bf16[1536,1536]{1,0:T(8,128)(2,1)S(1)} %right_root.1.root), custom_call_target="tpu_custom_call" | custom-call | flops 17999998976 | bytes 9000000 | tf_op jit(solution)/shard_map/product/pallas_call | solution.py:301
  85.1 1.5 %collective-permute-done.21.cross_high = bf16[192,768]{1,0:T(8,128)(2,1)S(1)} collective-permute-done((bf16[192,768]{1,0:T(8,128)(2,1)S(1)}, bf16[192,768]{1,0:T(8,128)(2,1)S(1)}, u32[]{:S(2)}, u32[]{:S(2)}) %collective-permute-start.21) | collective-permute-done | bytes 294944 | tf_op jit(solution)/shard_map/ppermute | solution.py:395
  86.6 0.8 left_rows.1
  87.4 2.1 %collective-permute-start.24 = (f32[8,128]{1,0:T(8,128)S(1)}, f32[8,128]{1,0:T(8,128)S(1)}, u32[]{:S(2)}, u32[]{:S(2)}) collective-permute-start(f32[8,128]{1,0:T(8,128)S(1)} %get-tuple-element.52.a), channel_id=1, source_target_pairs={{0,48},{16,32},{32,16},{48,0},{64,112},{80,96},{96,80},{112,64},{1... | collective-permute-start | bytes 12296 | tf_op jit(solution)/shard_map/ppermute | solution.py:41
  89.5 0.5 collective-permute-start.22
  90.0 4.4 %product.3.near = bf16[768,1536]{1,0:T(8,128)(2,1)S(1)} custom-call(s32[10]{0:T(128)S(1)} %stack.43.place, bf16[384,768]{1,0:T(8,128)(2,1)S(1)} %collective-permute-done.3.near, bf16[384,768]{1,0:T(8,128)(2,1)S(1)} %collective-permute-done.14.near_late, bf16[384,768]{1,0:T(8,128)(2,1)S(1)} %collective-permute-done.25.far, ...), custom_call_target="tpu_custom_call" | custom-call | flops 17999998976 | bytes 9000000 | tf_op jit(solution)/shard_map/product/pallas_call | solution.py:301
  94.5 2.1 %precond.1 = (f32[384,1536]{1,0:T(8,128)S(1)}, f32[16,128]{1,0:T(8,128)S(1)}) custom-call(f32[8,128]{1,0:T(8,128)S(1)} %get-tuple-element.52.a, f32[8,128]{1,0:T(8,128)S(1)} %collective-permute-done.22.b, f32[8,128]{1,0:T(8,128)S(1)} %collective-permute-done.23.c, f32[8,128]{1,0:T(8,128)S(1)} %collective-permute-done.24.d, ...), custom_call_target="tpu_custom_call" | custom-call | flops 1800000000 | bytes 8000000 | tf_op jit(solution)/shard_map/precond/pallas_call | solution.py:338
  96.6 1.4 %collective-permute-start.29 = (f32[16,128]{1,0:T(8,128)S(1)}, f32[16,128]{1,0:T(8,128)S(1)}, u32[]{:S(2)}, u32[]{:S(2)}) collective-permute-start(f32[16,128]{1,0:T(8,128)S(1)} %get-tuple-element.57.a), channel_id=1, source_target_pairs={{0,48},{16,32},{32,16},{48,0},{64,112},{80,96},{96,80},{112,64},{1... | collective-permute-start | bytes 24584 | tf_op jit(solution)/shard_map/ppermute | solution.py:41
  98.0 0.2 collective-permute-start.28
  98.2 0.6 collective-permute-start.27
  98.8 0.9 collective-permute-done.29.d
  99.7 0.8 collective-permute-done.28.c
  100.5 1.2 %graft.1 = bf16[384,1536]{1,0:T(8,128)(2,1)} custom-call(f32[16,128]{1,0:T(8,128)S(1)} %get-tuple-element.57.a, f32[16,128]{1,0:T(8,128)S(1)} %collective-permute-done.27.b, f32[16,128]{1,0:T(8,128)S(1)} %collective-permute-done.28.c, f32[16,128]{1,0:T(8,128)S(1)} %collective-permute-done.29.d, f32[384,1536]{1,0:T(8,128)S(1)} %get-tuple-element.58.value), custom_call_target="tpu_custom_call" | custom-call | flops 1000000 | bytes 4000000 | tf_op jit(solution)/shard_map/graft/pallas_call | solution.py:366
  (47 shorter events, 1.3 us)
Async XLA Ops:
  0.0 5.9 %copy-start = (bf16[384,1536]{1,0:T(8,128)(2,1)S(1)}, bf16[384,1536]{1,0:T(8,128)(2,1)}, u32[]{:S(2)}) copy-start(bf16[384,1536]{1,0:T(8,128)(2,1)} %mine.7) | copy-start | bytes 3538948
  0.0 5.9 %collective-permute-start = (bf16[384,1536]{1,0:T(8,128)(2,1)}, bf16[384,1536]{1,0:T(8,128)(2,1)S(1)}, u32[]{:S(2)}, u32[]{:S(2)}) collective-permute-start(bf16[384,1536]{1,0:T(8,128)(2,1)} %mine.7), channel_id=1, source_target_pairs={{0,16},{16,0},{32,48},{48,32},{64,80},{80,64},{96,112},{112,96},{1... | collective-permute-start | bytes 3538952 | tf_op jit(solution)/shard_map/ppermute | solution.py:41
  4.3 15.0 %collective-permute-start.3 = (bf16[384,768]{1,0:T(8,128)(2,1)S(1)}, bf16[384,768]{1,0:T(8,128)(2,1)S(1)}, u32[]{:S(2)}, u32[]{:S(2)}) collective-permute-start(bf16[384,768]{1,0:T(8,128)(2,1)S(1)} %constant_dynamic-slice_fusion.1), channel_id=1, source_target_pairs={{0,32},{16,48},{32,0},{48,16},{64,96},{80,112},{96,64},{112,80},{1... | collective-permute-start | bytes 1769480 | tf_op jit(solution)/shard_map/ppermute | solution.py:41
  8.3 14.3 %collective-permute-start.5 = (bf16[384,896]{1,0:T(8,128)(2,1)S(1)}, bf16[384,896]{1,0:T(8,128)(2,1)S(1)}, u32[]{:S(2)}, u32[]{:S(2)}) collective-permute-start(bf16[384,896]{1,0:T(8,128)(2,1)S(1)} %get-tuple-element.38), channel_id=1, source_target_pairs={{0,96},{1,97},{2,98},{3,99},{4,100},{5,101},{6,102},{7,103},{8,104... | collective-permute-start | bytes 2064392 | tf_op jit(solution)/shard_map/ppermute | solution.py:395
  10.4 10.5 %collective-permute-start.1 = (bf16[192,768]{1,0:T(8,128)(2,1)S(1)}, bf16[192,768]{1,0:T(8,128)(2,1)S(1)}, u32[]{:S(2)}, u32[]{:S(2)}) collective-permute-start(bf16[192,768]{1,0:T(8,128)(2,1)S(1)} %get-tuple-element.33), channel_id=1, source_target_pairs={{0,4},{1,5},{2,6},{3,7},{4,0},{5,1},{6,2},{7,3},{8,12},{9,13},{10,... | collective-permute-start | bytes 884744 | tf_op jit(solution)/shard_map/ppermute | solution.py:395
  21.0 4.3 %collective-permute-start.2 = (bf16[96,768]{1,0:T(8,128)(2,1)S(1)}, bf16[96,768]{1,0:T(8,128)(2,1)S(1)}, u32[]{:S(2)}, u32[]{:S(2)}) collective-permute-start(bf16[96,768]{1,0:T(8,128)(2,1)S(1)} %slice.78), channel_id=1, source_target_pairs={{0,12},{1,13},{2,14},{3,15},{4,8},{5,9},{6,10},{7,11},{8,4},{9,5},... | collective-permute-start | bytes 442376 | tf_op jit(solution)/shard_map/ppermute | solution.py:395
  21.1 8.5 %collective-permute-start.4 = (bf16[192,768]{1,0:T(8,128)(2,1)S(1)}, bf16[192,768]{1,0:T(8,128)(2,1)S(1)}, u32[]{:S(2)}, u32[]{:S(2)}) collective-permute-start(bf16[192,768]{1,0:T(8,128)(2,1)S(1)} %get-tuple-element.37), channel_id=1, source_target_pairs={{0,4},{1,5},{2,6},{3,7},{4,0},{5,1},{6,2},{7,3},{8,12},{9,13},{10,... | collective-permute-start | bytes 884744 | tf_op jit(solution)/shard_map/ppermute | solution.py:395
  22.7 7.4 %collective-permute-start.7 = (bf16[192,896]{1,0:T(8,128)(2,1)S(1)}, bf16[192,896]{1,0:T(8,128)(2,1)S(1)}, u32[]{:S(2)}, u32[]{:S(2)}) collective-permute-start(bf16[192,896]{1,0:T(8,128)(2,1)S(1)} %slice.76), channel_id=1, source_target_pairs={{0,128},{1,129},{2,130},{3,131},{4,132},{5,133},{6,134},{7,135},{8... | collective-permute-start | bytes 1032200 | tf_op jit(solution)/shard_map/ppermute | solution.py:395
  29.7 4.1 %collective-permute-start.6 = (bf16[96,768]{1,0:T(8,128)(2,1)S(1)}, bf16[96,768]{1,0:T(8,128)(2,1)S(1)}, u32[]{:S(2)}, u32[]{:S(2)}) collective-permute-start(bf16[96,768]{1,0:T(8,128)(2,1)S(1)} %slice.77), channel_id=1, source_target_pairs={{0,12},{1,13},{2,14},{3,15},{4,8},{5,9},{6,10},{7,11},{8,4},{9,5},... | collective-permute-start | bytes 442376 | tf_op jit(solution)/shard_map/ppermute | solution.py:395
  30.2 9.1 %collective-permute-start.9 = (bf16[192,896]{1,0:T(8,128)(2,1)S(1)}, bf16[192,896]{1,0:T(8,128)(2,1)S(1)}, u32[]{:S(2)}, u32[]{:S(2)}) collective-permute-start(bf16[192,896]{1,0:T(8,128)(2,1)S(1)} %fusion), channel_id=1, source_target_pairs={{0,32},{16,48},{32,0},{48,16},{64,96},{80,112},{96,64},{112,80},{1... | collective-permute-start | bytes 1032200 | tf_op jit(solution)/shard_map/ppermute | solution.py:41
  33.8 11.6 %collective-permute-start.8 = (bf16[96,1536]{1,0:T(8,128)(2,1)S(1)}, bf16[96,1536]{1,0:T(8,128)(2,1)S(1)}, u32[]{:S(2)}, u32[]{:S(2)}) collective-permute-start(bf16[96,1536]{1,0:T(8,128)(2,1)S(1)} %pad_maximum_fusion.1), channel_id=1, source_target_pairs={{0,1},{1,0},{2,3},{3,2},{4,5},{5,4},{6,7},{7,6},{8,9},{9,8},{10,11... | collective-permute-start | bytes 884744 | tf_op jit(solution)/shard_map/ppermute | solution.py:395
  39.4 10.6 %collective-permute-start.13 = (bf16[192,896]{1,0:T(8,128)(2,1)S(1)}, bf16[192,896]{1,0:T(8,128)(2,1)}, u32[]{:S(2)}, u32[]{:S(2)}) collective-permute-start(bf16[192,896]{1,0:T(8,128)(2,1)S(1)} %add_convert_fusion), channel_id=1, source_target_pairs={{0,128},{1,129},{2,130},{3,131},{4,132},{5,133},{6,134},{7,135},{8... | collective-permute-start | bytes 1032200 | tf_op jit(solution)/shard_map/ppermute | solution.py:395
  46.2 10.4 %collective-permute-start.10 = (bf16[96,1536]{1,0:T(8,128)(2,1)}, bf16[96,1536]{1,0:T(8,128)(2,1)}, u32[]{:S(2)}, u32[]{:S(2)}) collective-permute-start(bf16[96,1536]{1,0:T(8,128)(2,1)} %add_convert_fusion.2), channel_id=1, source_target_pairs={{0,3},{1,2},{2,1},{3,0},{4,7},{5,6},{6,5},{7,4},{8,11},{9,10},{10,... | collective-permute-start | bytes 884744 | tf_op jit(solution)/shard_map/ppermute | solution.py:395
  48.7 10.1 %collective-permute-start.14 = (bf16[384,768]{1,0:T(8,128)(2,1)S(1)}, bf16[384,768]{1,0:T(8,128)(2,1)S(1)}, u32[]{:S(2)}, u32[]{:S(2)}) collective-permute-start(bf16[384,768]{1,0:T(8,128)(2,1)S(1)} %constant_dynamic-slice_fusion), channel_id=1, source_target_pairs={{0,32},{16,48},{32,0},{48,16},{64,96},{80,112},{96,64},{112,80},{1... | collective-permute-start | bytes 1769480 | tf_op jit(solution)/shard_map/ppermute | solution.py:41
  51.1 18.3 %collective-permute-start.17 = (bf16[384,896]{1,0:T(8,128)(2,1)S(1)}, bf16[384,896]{1,0:T(8,128)(2,1)S(1)}, u32[]{:S(2)}, u32[]{:S(2)}) collective-permute-start(bf16[384,896]{1,0:T(8,128)(2,1)S(1)} %pad_maximum_fusion.refs_0_), channel_id=1, source_target_pairs={{0,96},{1,97},{2,98},{3,99},{4,100},{5,101},{6,102},{7,103},{8,104... | collective-permute-start | bytes 2064392 | tf_op jit(solution)/shard_map/ppermute | solution.py:395
  57.8 10.8 %collective-permute-start.11 = (bf16[96,768]{1,0:T(8,128)(2,1)S(1)}, bf16[96,768]{1,0:T(8,128)(2,1)S(1)}, u32[]{:S(2)}, u32[]{:S(2)}) collective-permute-start(bf16[96,768]{1,0:T(8,128)(2,1)S(1)} %get-tuple-element.60), channel_id=1, source_target_pairs={{0,12},{1,13},{2,14},{3,15},{4,8},{5,9},{6,10},{7,11},{8,4},{9,5},... | collective-permute-start | bytes 442376 | tf_op jit(solution)/shard_map/ppermute | solution.py:395
  58.8 10.6 %collective-permute-start.15 = (bf16[96,768]{1,0:T(8,128)(2,1)S(1)}, bf16[96,768]{1,0:T(8,128)(2,1)S(1)}, u32[]{:S(2)}, u32[]{:S(2)}) collective-permute-start(bf16[96,768]{1,0:T(8,128)(2,1)S(1)} %get-tuple-element.44), channel_id=1, source_target_pairs={{0,32},{16,48},{32,0},{48,16},{64,96},{80,112},{96,64},{112,80},{1... | collective-permute-start | bytes 442376 | tf_op jit(solution)/shard_map/ppermute | solution.py:41
  60.0 9.4 %collective-permute-start.16 = (bf16[96,384]{1,0:T(8,128)(2,1)S(1)}, bf16[96,384]{1,0:T(8,128)(2,1)S(1)}, u32[]{:S(2)}, u32[]{:S(2)}) collective-permute-start(bf16[96,384]{1,0:T(8,128)(2,1)S(1)} %slice.49), channel_id=1, source_target_pairs={{0,16},{16,0},{32,48},{48,32},{64,80},{80,64},{96,112},{112,96},{1... | collective-permute-start | bytes 221192 | tf_op jit(solution)/shard_map/ppermute | solution.py:41
  68.5 5.3 %collective-permute-start.18 = (bf16[384,896]{1,0:T(8,128)(2,1)S(1)}, bf16[384,896]{1,0:T(8,128)(2,1)S(1)}, u32[]{:S(2)}, u32[]{:S(2)}) collective-permute-start(bf16[384,896]{1,0:T(8,128)(2,1)S(1)} %pad_maximum_fusion.refs_0_), channel_id=1, source_target_pairs={{0,16},{16,0},{32,48},{48,32},{64,80},{80,64},{96,112},{112,96},{1... | collective-permute-start | bytes 2064392 | tf_op jit(solution)/shard_map/ppermute | solution.py:41
  69.4 4.4 %collective-permute-start.19 = (bf16[384,896]{1,0:T(8,128)(2,1)S(1)}, bf16[384,896]{1,0:T(8,128)(2,1)S(1)}, u32[]{:S(2)}, u32[]{:S(2)}) collective-permute-start(bf16[384,896]{1,0:T(8,128)(2,1)S(1)} %collective-permute-done.17.refs_1_), channel_id=1, source_target_pairs={{0,16},{16,0},{32,48},{48,32},{64,80},{80,64},{96,112},{112,96},{1... | collective-permute-start | bytes 2064392 | tf_op jit(solution)/shard_map/ppermute | solution.py:41
  71.9 13.2 %collective-permute-start.12 = (bf16[192,768]{1,0:T(8,128)(2,1)S(1)}, bf16[192,768]{1,0:T(8,128)(2,1)S(1)}, u32[]{:S(2)}, u32[]{:S(2)}) collective-permute-start(bf16[192,768]{1,0:T(8,128)(2,1)S(1)} %pad_maximum_fusion.2.own_low), channel_id=1, source_target_pairs={{0,4},{1,5},{2,6},{3,7},{4,0},{5,1},{6,2},{7,3},{8,12},{9,13},{10,... | collective-permute-start | bytes 884744 | tf_op jit(solution)/shard_map/ppermute | solution.py:395
  73.7 6.0 %collective-permute-start.20 = (bf16[96,768]{1,0:T(8,128)(2,1)S(1)}, bf16[96,768]{1,0:T(8,128)(2,1)S(1)}, u32[]{:S(2)}, u32[]{:S(2)}) collective-permute-start(bf16[96,768]{1,0:T(8,128)(2,1)S(1)} %pad_maximum_fusion.3), channel_id=1, source_target_pairs={{0,12},{1,13},{2,14},{3,15},{4,8},{5,9},{6,10},{7,11},{8,4},{9,5},... | collective-permute-start | bytes 442376 | tf_op jit(solution)/shard_map/ppermute | solution.py:395
  79.7 6.9 %collective-permute-start.21 = (bf16[192,768]{1,0:T(8,128)(2,1)S(1)}, bf16[192,768]{1,0:T(8,128)(2,1)S(1)}, u32[]{:S(2)}, u32[]{:S(2)}) collective-permute-start(bf16[192,768]{1,0:T(8,128)(2,1)S(1)} %constant_dynamic-update-slice_fusion.cross_low), channel_id=1, source_target_pairs={{0,4},{1,5},{2,6},{3,7},{4,0},{5,1},{6,2},{7,3},{8,12},{9,13},{10,... | collective-permute-start | bytes 884744 | tf_op jit(solution)/shard_map/ppermute | solution.py:395
  80.7 9.3 %collective-permute-start.25 = (bf16[384,768]{1,0:T(8,128)(2,1)S(1)}, bf16[384,768]{1,0:T(8,128)(2,1)S(1)}, u32[]{:S(2)}, u32[]{:S(2)}) collective-permute-start(bf16[384,768]{1,0:T(8,128)(2,1)S(1)} %collective-permute-done.3.near), channel_id=1, source_target_pairs={{0,16},{16,0},{32,48},{48,32},{64,80},{80,64},{96,112},{112,96},{1... | collective-permute-start | bytes 1769480 | tf_op jit(solution)/shard_map/ppermute | solution.py:41
  80.7 9.3 %collective-permute-start.26 = (bf16[384,768]{1,0:T(8,128)(2,1)S(1)}, bf16[384,768]{1,0:T(8,128)(2,1)S(1)}, u32[]{:S(2)}, u32[]{:S(2)}) collective-permute-start(bf16[384,768]{1,0:T(8,128)(2,1)S(1)} %collective-permute-done.14.near_late), channel_id=1, source_target_pairs={{0,16},{16,0},{32,48},{48,32},{64,80},{80,64},{96,112},{112,96},{1... | collective-permute-start | bytes 1769480 | tf_op jit(solution)/shard_map/ppermute | solution.py:41
  87.4 7.0 %collective-permute-start.24 = (f32[8,128]{1,0:T(8,128)S(1)}, f32[8,128]{1,0:T(8,128)S(1)}, u32[]{:S(2)}, u32[]{:S(2)}) collective-permute-start(f32[8,128]{1,0:T(8,128)S(1)} %get-tuple-element.52.a), channel_id=1, source_target_pairs={{0,48},{16,32},{32,16},{48,0},{64,112},{80,96},{96,80},{112,64},{1... | collective-permute-start | bytes 12296 | tf_op jit(solution)/shard_map/ppermute | solution.py:41
  89.5 4.9 %collective-permute-start.23 = (f32[8,128]{1,0:T(8,128)S(1)}, f32[8,128]{1,0:T(8,128)S(1)}, u32[]{:S(2)}, u32[]{:S(2)}) collective-permute-start(f32[8,128]{1,0:T(8,128)S(1)} %get-tuple-element.52.a), channel_id=1, source_target_pairs={{0,32},{16,48},{32,0},{48,16},{64,96},{80,112},{96,64},{112,80},{1... | collective-permute-start | bytes 12296 | tf_op jit(solution)/shard_map/ppermute | solution.py:41
  89.5 4.9 %collective-permute-start.22 = (f32[8,128]{1,0:T(8,128)S(1)}, f32[8,128]{1,0:T(8,128)S(1)}, u32[]{:S(2)}, u32[]{:S(2)}) collective-permute-start(f32[8,128]{1,0:T(8,128)S(1)} %get-tuple-element.52.a), channel_id=1, source_target_pairs={{0,16},{16,0},{32,48},{48,32},{64,80},{80,64},{96,112},{112,96},{1... | collective-permute-start | bytes 12296 | tf_op jit(solution)/shard_map/ppermute | solution.py:41
  96.6 3.2 %collective-permute-start.29 = (f32[16,128]{1,0:T(8,128)S(1)}, f32[16,128]{1,0:T(8,128)S(1)}, u32[]{:S(2)}, u32[]{:S(2)}) collective-permute-start(f32[16,128]{1,0:T(8,128)S(1)} %get-tuple-element.57.a), channel_id=1, source_target_pairs={{0,48},{16,32},{32,16},{48,0},{64,112},{80,96},{96,80},{112,64},{1... | collective-permute-start | bytes 24584 | tf_op jit(solution)/shard_map/ppermute | solution.py:41
  98.0 2.5 %collective-permute-start.28 = (f32[16,128]{1,0:T(8,128)S(1)}, f32[16,128]{1,0:T(8,128)S(1)}, u32[]{:S(2)}, u32[]{:S(2)}) collective-permute-start(f32[16,128]{1,0:T(8,128)S(1)} %get-tuple-element.57.a), channel_id=1, source_target_pairs={{0,32},{16,48},{32,0},{48,16},{64,96},{80,112},{96,64},{112,80},{1... | collective-permute-start | bytes 24584 | tf_op jit(solution)/shard_map/ppermute | solution.py:41
  98.2 2.3 %collective-permute-start.27 = (f32[16,128]{1,0:T(8,128)S(1)}, f32[16,128]{1,0:T(8,128)S(1)}, u32[]{:S(2)}, u32[]{:S(2)}) collective-permute-start(f32[16,128]{1,0:T(8,128)S(1)} %get-tuple-element.57.a), channel_id=1, source_target_pairs={{0,16},{16,0},{32,48},{48,32},{64,80},{80,64},{96,112},{112,96},{1... | collective-permute-start | bytes 24584 | tf_op jit(solution)/shard_map/ppermute | solution.py:41
